TPU v7x, 32 devices: a whole 2x2x4 slice. The times are simulated.
32 devices in a mesh: seq: 8 (over z, y), tp: 4 (over x, core).
Axes of the slice: x: 2, y: 2, z: 4, core: 2. Of those that a mesh axis runs over, the one named last changes fastest.
Arguments:
- stream_in: bfloat16 [8192, 2048], P('seq'), may hold values from -6 to 6
- doc_lengths: int32 [4], replicated, may hold values from 64 to 7808, as said below
- first_gain: bfloat16 [2048], P('seq'), may hold values from 0.5 to 1.5
- w_query: bfloat16 [2048, 256], P('seq', 'tp'), may hold values from -0.125 to 0.125
- w_key: bfloat16 [2048, 256], P('seq', 'tp'), may hold values from -0.125 to 0.125
- w_value: bfloat16 [2048, 2048], P('seq', 'tp'), may hold values from -0.125 to 0.125
- w_out: bfloat16 [2048, 2048], P('tp', 'seq'), may hold values from -2 to 2
- second_gain: bfloat16 [2048], P('seq'), may hold values from 0.5 to 1.5
- w_gate: bfloat16 [2048, 5504], P('seq', 'tp'), may hold values from -0.125 to 0.125
- w_up: bfloat16 [2048, 5504], P('seq', 'tp'), may hold values from -0.125 to 0.125
- w_down: bfloat16 [5504, 2048], P('tp', 'seq'), may hold values from -0.078125 to 0.078125
- cotangent: bfloat16 [8192, 2048], P('seq'), may hold values from -6 to 6
Outputs:
- activations: bfloat16 [8192, 2048], P('seq')
- input_grad: float32 [8192, 2048], P('seq')
- grad_first: float32 [2048], P('seq')
- grad_query: float32 [2048, 256], P('seq', 'tp')
- grad_key: float32 [2048, 256], P('seq', 'tp')
- grad_value: float32 [2048, 2048], P('seq', 'tp')
- grad_out: float32 [2048, 2048], P('tp', 'seq')
- grad_second: float32 [2048], P('seq')
- grad_gate: float32 [2048, 5504], P('seq', 'tp')
- grad_up: float32 [2048, 5504], P('seq', 'tp')
- grad_down: float32 [5504, 2048], P('tp', 'seq')
Inputs may be any that keep to these rules, and one draw needn't show every extreme that they name: `doc_lengths`: 4 row lengths in order, laid end to end over all 8192 tokens: one long row of 7808 tokens, placed anywhere among them, that starts within the first 1024 tokens and ends within the last 1024, and 3 short rows in any order, one of 64 tokens and two whose lengths, each of 64 to 256, sum to 320.
All inputs are finite; a program needn't handle non-finite values.
Results may differ from a plain program's by a relative error of at most 0.024.
Values may be sent and summed in bfloat16 or wider, within the bound.
A program may use at most 256 MiB of HBM per device.

v0:
```python
import math

import jax
import jax.numpy as jnp
from jax import lax
from jax.sharding import PartitionSpec as P

FEAT = 16


HIGH = lax.Precision.HIGHEST
EPSILON = 1e-06


def entering(value, axis, join, neutral):
    place = lax.axis_index(axis)
    gathered = jax.tree.map(
        lambda a, kind: lax.all_gather(a.astype(kind), axis),
        value,
        (jnp.bfloat16, jnp.bfloat16, jnp.bfloat16),
    )
    state = jax.tree.map(lambda a, e: jnp.zeros_like(a) + jnp.asarray(e, a.dtype), value, neutral)

    def one(step, state):
        return join(
            state,
            jax.tree.map(
                lambda a, own: lax.dynamic_index_in_dim(a, step, 0, False).astype(own.dtype),
                gathered,
                value,
            ),
        )

    return lax.fori_loop(0, place, one, state)


def entering_2(value, axis, combine, identity):
    devices, index = (lax.axis_size(axis), lax.axis_index(axis))
    everything = jax.tree.map(
        lambda part, kind: lax.all_gather(part.astype(kind), axis),
        value,
        jax.tree.map(lambda a: jnp.bfloat16 if a.dtype == jnp.float32 else a.dtype, value),
    )
    start = jax.tree.map(
        lambda part, zero: jnp.broadcast_to(jnp.asarray(zero, part.dtype), part.shape),
        value,
        identity,
    )

    def step(k, before):
        at = devices - 1 - k
        reached = at > index
        new = combine(
            before, jax.tree.map(lambda part, own: part[at].astype(own.dtype), everything, value)
        )
        return jax.tree.map(lambda a, b: jnp.where(reached, a, b), new, before)

    return lax.fori_loop(0, devices, step, start)


def rms_scale(values, gain):
    inverse = lax.rsqrt(jnp.mean(values * values, axis=-1, keepdims=True) + EPSILON)
    return values * inverse * gain


def features(vectors):
    halved = vectors * 0.5
    products = (halved[..., :, None] * halved[..., None, :]).reshape(
        halved.shape[:-1] + (halved.shape[-1] * halved.shape[-1],)
    )
    unit_col = jnp.ones(halved.shape[:-1] + (1,), jnp.float32)
    return jnp.concatenate([unit_col, halved, products * (1.0 / math.sqrt(2.0))], axis=-1)


def attend(queries, key_rows, value_rows, state_in, norm_in, allowed, carried):
    scores = jnp.einsum("ihf,jhf->hij", queries, key_rows, precision=HIGH) * 0.25
    weights = (1.0 + scores + 0.5 * scores * scores) * allowed[None]
    numerator = jnp.einsum("hij,jhd->ihd", weights, value_rows, precision=HIGH)
    denominator = jnp.transpose(jnp.sum(weights, axis=2))
    query_feat = features(queries) * carried[:, None, None]
    numerator = numerator + jnp.einsum("ihf,hfd->ihd", query_feat, state_in, precision=HIGH)
    denominator = denominator + jnp.einsum("ihf,hf->ih", query_feat, norm_in, precision=HIGH)
    return numerator / denominator[:, :, None]


def local_state(key_rows, value_rows, keep):
    key_feat = features(key_rows) * keep[:, None, None]
    return (
        jnp.einsum("jhf,jhd->hfd", key_feat, value_rows, precision=HIGH),
        jnp.sum(key_feat, axis=0),
    )


def chain(earlier, later):
    state_a, norm_a, closes_a = earlier
    state_b, norm_b, closes_b = later
    carry_on = 1.0 - closes_b
    return (
        state_b + carry_on * state_a,
        norm_b + carry_on * norm_a,
        jnp.maximum(closes_a, closes_b),
    )


def doc_starts(lengths, positions):
    ends = jnp.cumsum(lengths)
    starts = ends - lengths
    chosen = jnp.where(
        starts[None, :] <= positions[:, None], starts[None, :], jnp.zeros_like(starts)[None, :]
    )
    return jnp.max(chosen, axis=1)


def contract_rows(left, right):
    return lax.dot_general(
        left, right, (((0,), (0,)), ((), ())), preferred_element_type=jnp.float32
    )


def contract_cols(left, right):
    return lax.dot_general(
        left, right, (((1,), (1,)), ((), ())), preferred_element_type=jnp.float32
    )


def on_device(
    stream_in,
    doc_lengths,
    first_gain,
    w_query,
    w_key,
    w_value,
    w_out,
    second_gain,
    w_gate,
    w_up,
    w_down,
    cotangent,
):
    gathered = (
        lax.all_gather(first_gain, "seq", axis=0, tiled=True),
        lax.all_gather(w_query, "seq", axis=0, tiled=True),
        lax.all_gather(w_key, "seq", axis=0, tiled=True),
        lax.all_gather(w_value, "seq", axis=0, tiled=True),
        lax.all_gather(w_out, "seq", axis=1, tiled=True),
        lax.all_gather(second_gain, "seq", axis=0, tiled=True),
        lax.all_gather(w_gate, "seq", axis=0, tiled=True),
        lax.all_gather(w_up, "seq", axis=0, tiled=True),
        lax.all_gather(w_down, "seq", axis=1, tiled=True),
    )
    (
        first_full,
        query_full,
        key_full,
        value_full,
        out_full,
        second_full,
        gate_full,
        up_full,
        down_full,
    ) = gathered
    row_count = stream_in.shape[0]
    heads_local = query_full.shape[1] // FEAT
    head_width = value_full.shape[1] // heads_local
    dev_start = lax.axis_index("seq") * row_count
    positions = dev_start + jnp.arange(row_count, dtype=jnp.int32)
    starts = doc_starts(doc_lengths, positions)
    counter = jnp.arange(row_count, dtype=jnp.int32)
    allowed = (
        (counter[None, :] <= counter[:, None]) & (starts[None, :] == starts[:, None])
    ).astype(jnp.float32)
    carried = (starts < dev_start).astype(jnp.float32)
    keep = (starts == starts[row_count - 1]).astype(jnp.float32)
    closes = (starts[row_count - 1 :] >= dev_start).astype(jnp.float32)
    stream_f = stream_in.astype(jnp.float32)
    first_gf = first_full.astype(jnp.float32)
    second_gf = second_full.astype(jnp.float32)
    h_one = rms_scale(stream_f, first_gf).astype(jnp.bfloat16)
    query_b = jnp.dot(h_one, query_full, preferred_element_type=jnp.float32).astype(jnp.bfloat16)
    key_b = jnp.dot(h_one, key_full, preferred_element_type=jnp.float32).astype(jnp.bfloat16)
    value_b = jnp.dot(h_one, value_full, preferred_element_type=jnp.float32).astype(jnp.bfloat16)
    query_f = query_b.astype(jnp.float32).reshape(row_count, heads_local, FEAT)
    key_f = key_b.astype(jnp.float32).reshape(row_count, heads_local, FEAT)
    value_f = value_b.astype(jnp.float32).reshape(row_count, heads_local, head_width)
    state_loc, norm_loc = local_state(key_f, value_f, keep)
    identity = (jnp.zeros_like(state_loc), jnp.zeros_like(norm_loc), jnp.zeros((1,), jnp.float32))
    state_in, norm_in, _ = entering((state_loc, norm_loc, closes), "seq", chain, identity)

    def attend_local(queries, key_rows, value_rows, state_arg, norm_arg):
        return attend(queries, key_rows, value_rows, state_arg, norm_arg, allowed, carried)

    attn, attend_pull = jax.vjp(attend_local, query_f, key_f, value_f, state_in, norm_in)
    mixed_b = attn.reshape(row_count, heads_local * head_width).astype(jnp.bfloat16)
    attn_term = jnp.dot(mixed_b, out_full, preferred_element_type=jnp.float32)
    middle = stream_f + lax.psum(attn_term.astype(jnp.bfloat16), "tp").astype(jnp.float32)
    h_two = rms_scale(middle, second_gf).astype(jnp.bfloat16)
    gate = jnp.dot(h_two, gate_full, preferred_element_type=jnp.float32)
    up_proj = jnp.dot(h_two, up_full, preferred_element_type=jnp.float32)
    sigma = jax.nn.sigmoid(gate)
    silu_gate = gate * sigma
    hidden = (silu_gate * up_proj).astype(jnp.bfloat16)
    feed_term = jnp.dot(hidden, down_full, preferred_element_type=jnp.float32)
    grad_down = contract_rows(hidden, cotangent)
    dhidden = contract_cols(cotangent, down_full)
    dgate_b = (dhidden * up_proj * sigma * (1.0 + gate * (1.0 - sigma))).astype(jnp.bfloat16)
    dup_b = (dhidden * silu_gate).astype(jnp.bfloat16)
    grad_gate = contract_rows(h_two, dgate_b)
    grad_up = contract_rows(h_two, dup_b)
    dh_local_two = contract_cols(dgate_b, gate_full) + contract_cols(dup_b, up_full)
    activations = (
        middle + lax.psum(feed_term.astype(jnp.bfloat16), "tp").astype(jnp.float32)
    ).astype(jnp.bfloat16)
    dh_two = lax.psum(dh_local_two.astype(jnp.bfloat16), "tp").astype(jnp.float32)
    _, norm_two_pull = jax.vjp(rms_scale, middle, second_gf)
    dmid_norm, grad_second = norm_two_pull(dh_two)
    dmid = cotangent.astype(jnp.float32) + dmid_norm
    dmid_b = dmid.astype(jnp.bfloat16)
    grad_out = contract_rows(mixed_b, dmid_b)
    dattn = contract_cols(dmid_b, out_full).reshape(row_count, heads_local, head_width)
    dq_own, dk_own, dv_own, pull_state, pull_norm = attend_pull(dattn)
    back_state, back_norm, _ = entering_2((pull_state, pull_norm, closes), "seq", chain, identity)

    def state_local(key_rows, value_rows):
        return local_state(key_rows, value_rows, keep)

    _, state_pull = jax.vjp(state_local, key_f, value_f)
    dk_far, dv_far = state_pull((back_state, back_norm))
    dq_b = dq_own.reshape(row_count, heads_local * FEAT).astype(jnp.bfloat16)
    dk_b = (dk_own + dk_far).reshape(row_count, heads_local * FEAT).astype(jnp.bfloat16)
    dv_b = (dv_own + dv_far).reshape(row_count, heads_local * head_width).astype(jnp.bfloat16)
    grad_query = contract_rows(h_one, dq_b)
    grad_key = contract_rows(h_one, dk_b)
    grad_value = contract_rows(h_one, dv_b)
    dh_local = (
        contract_cols(dq_b, query_full)
        + contract_cols(dk_b, key_full)
        + contract_cols(dv_b, value_full)
    )
    dh_one = lax.psum(dh_local.astype(jnp.bfloat16), "tp").astype(jnp.float32)
    _, norm_one_pull = jax.vjp(rms_scale, stream_f, first_gf)
    dstream_norm, grad_first = norm_one_pull(dh_one)
    input_grad = dmid + dstream_norm
    reduced = tuple(
        (
            lax.psum_scatter(
                grad_first.astype(jnp.bfloat16), "seq", scatter_dimension=0, tiled=True
            ).astype(jnp.float32),
            lax.psum_scatter(
                grad_query.astype(jnp.bfloat16), "seq", scatter_dimension=0, tiled=True
            ).astype(jnp.float32),
            lax.psum_scatter(
                grad_key.astype(jnp.bfloat16), "seq", scatter_dimension=0, tiled=True
            ).astype(jnp.float32),
            lax.psum_scatter(
                grad_value.astype(jnp.bfloat16), "seq", scatter_dimension=0, tiled=True
            ).astype(jnp.float32),
            lax.psum_scatter(
                grad_out.astype(jnp.bfloat16), "seq", scatter_dimension=1, tiled=True
            ).astype(jnp.float32),
            lax.psum_scatter(
                grad_second.astype(jnp.bfloat16), "seq", scatter_dimension=0, tiled=True
            ).astype(jnp.float32),
            lax.psum_scatter(
                grad_gate.astype(jnp.bfloat16), "seq", scatter_dimension=0, tiled=True
            ).astype(jnp.float32),
            lax.psum_scatter(
                grad_up.astype(jnp.bfloat16), "seq", scatter_dimension=0, tiled=True
            ).astype(jnp.float32),
            lax.psum_scatter(
                grad_down.astype(jnp.bfloat16), "seq", scatter_dimension=1, tiled=True
            ).astype(jnp.float32),
        )
    )
    return (
        activations,
        input_grad,
        reduced[0],
        reduced[1],
        reduced[2],
        reduced[3],
        reduced[4],
        reduced[5],
        reduced[6],
        reduced[7],
        reduced[8],
    )


def solution(mesh):
    placed = (
        P("seq", None),
        P(),
        P("seq"),
        P("seq", "tp"),
        P("seq", "tp"),
        P("seq", "tp"),
        P("tp", "seq"),
        P("seq"),
        P("seq", "tp"),
        P("seq", "tp"),
        P("tp", "seq"),
        P("seq", None),
    )
    return jax.shard_map(
        on_device,
        mesh=mesh,
        in_specs=placed,
        out_specs=(
            P("seq", None),
            P("seq", None),
            P("seq"),
            P("seq", "tp"),
            P("seq", "tp"),
            P("seq", "tp"),
            P("tp", "seq"),
            P("seq"),
            P("seq", "tp"),
            P("seq", "tp"),
            P("tp", "seq"),
        ),
        check_vma=False,
    )
```

profile of v0, /device:TPU:0, one launch (start us, length us, event | category | flops | bytes accessed | tf_op | source)
XLA Modules:
  0.0 1619.6 jit_solution(15310727497498596676)
XLA Ops:
  8.6 22.3 %all-gather.5 = bf16[8,1,256]{2,1,0:T(2,128)(2,1)S(1)} all-gather(bf16[1,1,256]{2,1,0:T(2,128)(2,1)S(1)} %reshape.273), channel_id=1, replica_groups=mesh['seq'=8,'tp'=4] {'seq'}, dimensions={0}, use_global_device_ids=true | all-gather | bytes 4608 | tf_op jit(solution)/shard_map/all_gather | solution.py:141
  33.3 31.9 %all_gather.60 = bf16[2048,64]{0,1:T(8,128)(2,1)S(1)} all-gather(bf16[256,64]{0,1:T(8,128)(2,1)} %param.20), channel_id=1, replica_groups=mesh['seq'=8,'tp'=4] {'seq'}, dimensions={0}, use_global_device_ids=true | all-gather | bytes 294912 | tf_op jit(solution)/shard_map/all_gather | solution.py:143
  91.8 32.0 %all_gather.59 = bf16[2048,64]{0,1:T(8,128)(2,1)S(1)} all-gather(bf16[256,64]{0,1:T(8,128)(2,1)S(1)} %copy-done.42), channel_id=1, replica_groups=mesh['seq'=8,'tp'=4] {'seq'}, dimensions={0}, use_global_device_ids=true | all-gather | bytes 294912 | tf_op jit(solution)/shard_map/all_gather | solution.py:142
  127.9 17.2 %all-reduce = bf16[8]{0:T(256)(128)(2,1)S(1)} all-reduce(bf16[8]{0:T(256)(128)(2,1)S(1)} %dynamic-update-slice), channel_id=3, replica_groups=mesh['seq'=8,'tp'=4] {'seq'}, use_global_device_ids=true, to_apply=%add | all-reduce | flops 8 | bytes 32
  145.0 30.6 %all-gather.6 = bf16[8,4,273]{2,1,0:T(4,128)(2,1)S(1)} all-gather(bf16[1,4,273]{2,1,0:T(4,128)(2,1)S(1)} %bitcast.227), channel_id=4, replica_groups=mesh['seq'=8,'tp'=4] {'seq'}, dimensions={0}, use_global_device_ids=true | all-gather | bytes 19656 | tf_op jit(solution)/shard_map/all_gather | solution.py:18
  186.3 13.6 fusion.38
  221.0 40.1 %all-gather.7 = bf16[8,1,256]{2,1,0:T(2,128)(2,1)S(1)} all-gather(bf16[1,1,256]{2,1,0:T(2,128)(2,1)S(1)} %reshape.277), channel_id=1, replica_groups=mesh['seq'=8,'tp'=4] {'seq'}, dimensions={0}, use_global_device_ids=true | all-gather | bytes 4608 | tf_op jit(solution)/shard_map/all_gather | solution.py:146
  261.1 63.3 %all-reduce.9.cloned.1.call-done = bf16[1024,2048]{1,0:T(8,128)(2,1)} async-done(((bf16[1024,2048]{1,0:T(8,128)(2,1)}), bf16[1024,2048]{1,0:T(8,128)(2,1)}) %all-reduce.9.cloned.1.call-update) | async-done | bytes 4194320 | tf_op jit(solution)/shard_map/psum | solution.py:195
  334.3 84.4 %all-gather.21.cloned.1.call-done = bf16[2048,1376]{0,1:T(8,128)(2,1)} async-done(((bf16[256,1376]{0,1:T(8,128)(2,1)}), bf16[2048,1376]{0,1:T(8,128)(2,1)}) %all-gather.21.cloned.1.call-update) | async-done | bytes 5636112 | tf_op jit(solution)/shard_map/all_gather | solution.py:147
  418.6 10.8 fusion.63
  429.5 81.5 %all-gather.23.cloned.1.call-done = bf16[2048,1376]{0,1:T(8,128)(2,1)} async-done(((bf16[256,1376]{0,1:T(8,128)(2,1)}), bf16[2048,1376]{0,1:T(8,128)(2,1)}) %all-gather.23.cloned.1.call-update) | async-done | bytes 5636112 | tf_op jit(solution)/shard_map/all_gather | solution.py:148
  510.9 10.8 fusion.64
  521.8 81.6 %all-gather.25.cloned.1.call-done = bf16[1376,2048]{1,0:T(8,128)(2,1)} async-done(((bf16[1376,256]{1,0:T(8,128)(2,1)}), bf16[1376,2048]{1,0:T(8,128)(2,1)}) %all-gather.25.cloned.1.call-update) | async-done | bytes 5636112 | tf_op jit(solution)/shard_map/all_gather | solution.py:149
  603.4 15.0 multiply_convert_fusion.1
  618.4 11.6 fusion.65
  639.0 83.7 %all-reduce.11.cloned.1.call-done = bf16[1024,2048]{1,0:T(8,128)(2,1)} async-done(((bf16[1024,2048]{1,0:T(8,128)(2,1)}), bf16[1024,2048]{1,0:T(8,128)(2,1)}) %all-reduce.11.cloned.1.call-update) | async-done | bytes 4194320 | tf_op jit(solution)/shard_map/psum | solution.py:213
  755.9 30.7 %all-gather.8 = bf16[8,4,273]{2,1,0:T(4,128)(2,1)S(1)} all-gather(bf16[1,4,273]{2,1,0:T(4,128)(2,1)S(1)} %bitcast.228), channel_id=6, replica_groups=mesh['seq'=8,'tp'=4] {'seq'}, dimensions={0}, use_global_device_ids=true | all-gather | bytes 19656 | tf_op jit(solution)/shard_map/all_gather | solution.py:40
  786.6 20.2 %fusion.3 = f32[4,1024,1024]{1,2,0:T(8,128)} fusion(f32[4,1024,1024]{1,2,0:T(8,128)} %get-tuple-element.333, bf16[1024,4,128]{0,2,1:T(8,128)(2,1)S(1)} %bitcast.210, f32[4,1024]{1,0:T(4,128)S(1)} %get-tuple-element.322, f32[1024,1024]{0,1:T(8,128)S(1)} %copy-done.19, f32[1024,4]{0,1:T(4,128)S(1)} %get-tuple-element.316, f32[1024,512]{0,1:T(8,128)} %copy-done.26), kind=kOutput, calls=%fused_computation.10 | convolution fusion | flops 6484918272 | bytes 40927232 | tf_op jit(solution)/shard_map/transpose(jvp(hij,jhd->ihd))/dot_general | solution.py:78
  826.4 25.3 %fusion.19 = f32[4,128,1024]{2,1,0:T(8,128)} fusion(f32[4,1024,1024]{1,2,0:T(8,128)} %get-tuple-element.333, f32[1024,1024]{0,1:T(8,128)} %fusion.18, f32[1024,4]{0,1:T(4,128)S(1)} %get-tuple-element.316, f32[1024,512]{0,1:T(8,128)} %copy-done.26), kind=kOutput, calls=%fused_computation.69 | convolution fusion | flops 6468141056 | bytes 25182208 | tf_op jit(solution)/shard_map/transpose(jvp(hij,jhd->ihd))/dot_general | solution.py:78
  858.9 25.9 %while.33 = (s32[]{:T(128)}, f32[4,273,128]{2,1,0:T(8,128)S(1)}, f32[4,273]{1,0:T(4,128)S(1)}, s32[]{:T(128)}, bf16[8,4,273,128]{3,2,1,0:T(8,128)(2,1)}, /*index...) while((s32[]{:T(128)}, f32[4,273,128]{2,1,0:T(8,128)S(1)}, ...), condition=%wide.region_16.17_spmd.clone, body=%wide.region_15.16_spmd.clone.sunk | while | flops 704349 | bytes 1408891 | solution.py:58
  891.5 14.5 fusion.36
  921.7 11.6 convolution_convert_fusion.3
  942.5 10.0 convolution_convert_fusion.1
  954.2 10.1 convolution_convert_fusion
  985.9 62.8 %reduce-scatter.10.cloned.1.call-done = bf16[256,64]{0,1:T(8,128)(2,1)} async-done(((bf16[2048,64]{0,1:T(8,128)(2,1)}), bf16[256,64]{0,1:T(8,128)(2,1)}) %reduce-scatter.10.cloned.1.call-update) | async-done | bytes 32784 | tf_op jit(solution)/shard_map/reduce_scatter | solution.py:251
  1050.1 68.8 %reduce-scatter.12.cloned.1.call-done = bf16[256,512]{1,0:T(8,128)(2,1)} async-done(((bf16[2048,512]{1,0:T(8,128)(2,1)}), bf16[256,512]{1,0:T(8,128)(2,1)}) %reduce-scatter.12.cloned.1.call-update) | async-done | bytes 262160 | tf_op jit(solution)/shard_map/reduce_scatter | solution.py:254
  1120.7 153.5 %all-reduce.13.cloned.1.call-done = (bf16[1024,2048]{1,0:T(8,128)(2,1)}, bf16[1024,2048]{1,0:T(8,128)(2,1)}) async-done(((bf16[1024,2048]{1,0:T(8,128)(2,1)}, bf16[1024,2048]{1,0:T(8,128)(2,1)}), (bf16[1024,2048]{1,0:T(8,128)(2,1)}, bf16[1024,2048]{1,0:T(8,128)(2,1)})) %all-reduce.13.cloned.1.call-update) | async-done | bytes 8388624 | tf_op jit(solution)/shard_map/psum | solution.py:211
  1280.1 22.9 %all-reduce.3 = (bf16[2048]{0:T(1024)(128)(2,1)S(1)}, bf16[2048]{0:T(1024)(128)(2,1)S(1)}) all-reduce(bf16[2048]{0:T(1024)(128)(2,1)S(1)} %get-tuple-element.277, bf16[2048]{0:T(1024)(128)(2,1)S(1)} %copy-done.43), channel_id=7, replica_groups=mesh['seq'=8,'tp'=4] {'seq'}, use_global_device_ids=true, to_apply=%region_22.23.clone | all-reduce | flops 4096 | bytes 16384
  1303.6 14.4 fusion.13
  1318.0 68.7 %reduce-scatter.16.cloned.1.call-done = bf16[256,1376]{0,1:T(8,128)(2,1)} async-done(((bf16[2048,1376]{0,1:T(8,128)(2,1)}), bf16[256,1376]{0,1:T(8,128)(2,1)}) %reduce-scatter.16.cloned.1.call-update) | async-done | bytes 704528 | tf_op jit(solution)/shard_map/reduce_scatter | solution.py:263
  1389.0 109.7 %reduce-scatter.18.cloned.1.call-done = bf16[256,1376]{0,1:T(8,128)(2,1)} async-done(((bf16[2048,1376]{0,1:T(8,128)(2,1)}), bf16[256,1376]{0,1:T(8,128)(2,1)}) %reduce-scatter.18.cloned.1.call-update) | async-done | bytes 704528 | tf_op jit(solution)/shard_map/reduce_scatter | solution.py:266
  1501.0 109.6 %reduce-scatter.20.cloned.1.call-done = bf16[1376,256]{1,0:T(8,128)(2,1)} async-done(((bf16[1376,2048]{1,0:T(8,128)(2,1)}), bf16[1376,256]{1,0:T(8,128)(2,1)}) %reduce-scatter.20.cloned.1.call-update) | async-done | bytes 704528 | tf_op jit(solution)/shard_map/reduce_scatter | solution.py:269
  (248 shorter events, 240.7 us)
Async XLA Ops:
  7.2 68.8 %all-gather.17.cloned.1.call-start = ((), (), s32[]{:S(2)}) async-start(), calls=%async_computation.7 | async-start | bytes 2359296 | tf_op jit(solution)/shard_map/all_gather | solution.py:144
  7.9 192.0 %all-gather.27.cloned.1.call-start = ((), (), s32[]{:S(2)}) async-start(), calls=%async_computation.21 | async-start | bytes 2580480 | tf_op jit(solution)/shard_map/all_gather | solution.py:18
  30.9 38.1 %copy-start.34 = (f32[8,1,256]{2,1,0:T(1,128)}, f32[8,1,256]{2,1,0:T(1,128)S(1)}, u32[]{:S(2)}) copy-start(f32[8,1,256]{2,1,0:T(1,128)S(1)} %convert_element_type.325) | copy-start | bytes 24580
  31.8 37.2 %copy-start = (bf16[1024,2048]{1,0:T(8,128)(2,1)S(1)}, bf16[1024,2048]{1,0:T(8,128)(2,1)}, u32[]{:S(2)}) copy-start(bf16[1024,2048]{1,0:T(8,128)(2,1)} %param.16) | copy-start | bytes 12582916
  81.3 705.2 %copy-start.31 = (bf16[1024,512]{0,1:T(8,128)(2,1)}, bf16[1024,512]{0,1:T(8,128)(2,1)S(1)}, u32[]{:S(2)}) copy-start(bf16[1024,512]{0,1:T(8,128)(2,1)S(1)} %convolution_convert_fusion.9) | copy-start | bytes 3145732
  84.9 127.7 %all-gather.19.cloned.1.call-start = ((), (), s32[]{:S(2)}) async-start(), calls=%async_computation.8 | async-start | bytes 2359296 | tf_op jit(solution)/shard_map/all_gather | solution.py:145
  85.6 238.7 %all-reduce.9.cloned.1.call-start = ((), (), s32[]{:S(2)}) async-start(), calls=%async_computation.9 | async-start | bytes 8388608 | tf_op jit(solution)/shard_map/psum | solution.py:195
  85.7 38.1 %copy-start.4 = (bf16[1024,2048]{1,0:T(8,128)(2,1)S(1)}, bf16[1024,2048]{1,0:T(8,128)(2,1)}, u32[]{:S(2)}) copy-start(bf16[1024,2048]{1,0:T(8,128)(2,1)} %copy-done.3) | copy-start | bytes 12582916
  88.4 37.3 %copy-start.44 = (u32[32]{0:T(128)S(1)}, u32[32]{0:T(128)}, u32[]{:S(2)}) copy-start(u32[32]{0:T(128)} %constant.121) | copy-start | bytes 388
  125.2 61.1 %copy-start.33 = (bf16[1024,64]{0,1:T(8,128)(2,1)}, bf16[1024,64]{0,1:T(8,128)(2,1)S(1)}, u32[]{:S(2)}) copy-start(bf16[1024,64]{0,1:T(8,128)(2,1)S(1)} %get-tuple-element.331) | copy-start | bytes 393220
  145.0 33.2 %copy-start.18 = (f32[1024,1024]{0,1:T(8,128)S(1)}, f32[1024,1024]{0,1:T(8,128)}, u32[]{:S(2)}) copy-start(f32[1024,1024]{0,1:T(8,128)} %fusion.18) | copy-start | bytes 12582916
  219.0 199.6 %all-gather.21.cloned.1.call-start = ((), (), s32[]{:S(2)}) async-start(), calls=%async_computation.10 | async-start | bytes 6340608 | tf_op jit(solution)/shard_map/all_gather | solution.py:147
  219.6 291.4 %all-gather.23.cloned.1.call-start = ((), (), s32[]{:S(2)}) async-start(), calls=%async_computation.11 | async-start | bytes 6340608 | tf_op jit(solution)/shard_map/all_gather | solution.py:148
  220.2 383.2 %all-gather.25.cloned.1.call-start = ((), (), s32[]{:S(2)}) async-start(), calls=%async_computation.12 | async-start | bytes 6340608 | tf_op jit(solution)/shard_map/all_gather | solution.py:149
  220.9 501.8 %all-reduce.11.cloned.1.call-start = ((), (), s32[]{:S(2)}) async-start(), calls=%async_computation.13 | async-start | bytes 8388608 | tf_op jit(solution)/shard_map/psum | solution.py:213
  638.9 220.0 %all-gather.29.cloned.1.call-start = ((), (), s32[]{:S(2)}) async-start(), calls=%async_computation.22 | async-start | bytes 2580480 | tf_op jit(solution)/shard_map/all_gather | solution.py:40
  749.5 227.3 %reduce-scatter.8.cloned.1.call-start = ((), (), s32[]{:S(2)}) async-start(), calls=%async_computation.14 | async-start | bytes 294912 | tf_op jit(solution)/shard_map/reduce_scatter | solution.py:248
  749.5 37.0 %copy-start.19 = (f32[1024,1024]{0,1:T(8,128)S(1)}, f32[1024,1024]{0,1:T(8,128)}, u32[]{:S(2)}) copy-start(f32[1024,1024]{0,1:T(8,128)} %fusion.18) | copy-start | bytes 12582916
  824.8 26.9 %copy-start.28 = (bf16[1024,4,16]{0,2,1:T(8,128)(2,1)}, bf16[1024,4,16]{0,2,1:T(8,128)(2,1)S(1)}, u32[]{:S(2)}) copy-start(bf16[1024,4,16]{0,2,1:T(8,128)(2,1)S(1)} %fusion.35) | copy-start | bytes 393220
  851.7 132.4 %reduce-scatter.14.cloned.1.call-start = ((), (), s32[]{:S(2)}) async-start(), calls=%async_computation.17 | async-start | bytes 2359296 | tf_op jit(solution)/shard_map/reduce_scatter | solution.py:257
  858.8 26.0 %copy-start.32 = (bf16[1024,512]{0,1:T(8,128)(2,1)S(1)}, bf16[1024,512]{0,1:T(8,128)(2,1)}, u32[]{:S(2)}) copy-start(bf16[1024,512]{0,1:T(8,128)(2,1)} %copy-done.31) | copy-start | bytes 3145732
  858.8 26.0 %copy-start.39 = (f32[1024]{0:T(1024)S(1)}, f32[1024]{0:T(1024)}, u32[]{:S(2)}) copy-start(f32[1024]{0:T(1024)} %copy-done.38) | copy-start | bytes 12292
  858.9 189.8 %reduce-scatter.10.cloned.1.call-start = ((), (), s32[]{:S(2)}) async-start(), calls=%async_computation.15 | async-start | bytes 294912 | tf_op jit(solution)/shard_map/reduce_scatter | solution.py:251
  915.6 203.2 %reduce-scatter.12.cloned.1.call-start = ((), (), s32[]{:S(2)}) async-start(), calls=%async_computation.16 | async-start | bytes 2359296 | tf_op jit(solution)/shard_map/reduce_scatter | solution.py:254
  921.7 352.5 %all-reduce.13.cloned.1.call-start = ((), (), s32[]{:S(2)}) async-start(), calls=%async_computation.23 | async-start | bytes 16777216 | tf_op jit(solution)/shard_map/psum | solution.py:211
  940.7 446.1 %reduce-scatter.16.cloned.1.call-start = ((), (), s32[]{:S(2)}) async-start(), calls=%async_computation.18 | async-start | bytes 6340608 | tf_op jit(solution)/shard_map/reduce_scatter | solution.py:263
  952.5 546.2 %reduce-scatter.18.cloned.1.call-start = ((), (), s32[]{:S(2)}) async-start(), calls=%async_computation.19 | async-start | bytes 6340608 | tf_op jit(solution)/shard_map/reduce_scatter | solution.py:266
  964.4 646.3 %reduce-scatter.20.cloned.1.call-start = ((), (), s32[]{:S(2)}) async-start(), calls=%async_computation.20 | async-start | bytes 6340608 | tf_op jit(solution)/shard_map/reduce_scatter | solution.py:269
  976.0 298.1 %copy-start.35 = (f32[8,1,256]{2,1,0:T(1,128)S(1)}, f32[8,1,256]{2,1,0:T(1,128)}, u32[]{:S(2)}) copy-start(f32[8,1,256]{2,1,0:T(1,128)} %copy-done.34) | copy-start | bytes 24580
  976.0 298.1 %copy-start.37 = (f32[1024]{0:T(1024)S(1)}, f32[1024]{0:T(1024)}, u32[]{:S(2)}) copy-start(f32[1024]{0:T(1024)} %copy-done.36) | copy-start | bytes 12292
  1050.1 230.0 %copy-start.43 = (bf16[2048]{0:T(1024)(128)(2,1)S(1)}, bf16[2048]{0:T(1024)(128)(2,1)}, u32[]{:S(2)}) copy-start(bf16[2048]{0:T(1024)(128)(2,1)} %get-tuple-element.275) | copy-start | bytes 12292
  1050.1 253.5 %copy-start.41 = (f32[1024]{0:T(1024)S(1)}, f32[1024]{0:T(1024)}, u32[]{:S(2)}) copy-start(f32[1024]{0:T(1024)} %copy-done.40) | copy-start | bytes 12292
  (40 other events, 286.3 us)
Sparse Core Ops, SparseCore 0:
  10.1 54.6 all-gather.16
  85.0 49.8 all-gather.26
  137.0 50.1 all-gather.18
  219.1 105.1 all-reduce.8
  326.4 92.1 all-gather.20
  420.7 90.1 all-gather.22
  513.2 90.1 all-gather.24
  639.0 83.6 all-reduce.10
  749.6 51.6 all-gather.28
  851.9 61.5 reduce-scatter.7
  917.0 67.0 reduce-scatter.13
  987.9 60.7 reduce-scatter.9
  1052.2 66.6 reduce-scatter.11
  1121.9 152.2 all-reduce.12
  1277.6 109.0 reduce-scatter.15
  1390.2 108.3 reduce-scatter.17
  1502.2 108.3 reduce-scatter.19
where the time goes:
time: 1630 us; the launch traced here: 1620 us
  waiting for transfers between devices  977 us (60%)
  matrix products  272 us (17%)
  blocking collectives  228 us (14%)
  other arithmetic  111 us (7%)
    psum x1, waiting for transfers between devices, on_device(): lax.psum(feed_term.astype(jnp.bfloat16), 'tp').astype(jnp.float32)  153 us
    reduce_scatter x1, waiting for transfers between devices, on_device(): lax.psum_scatter(grad_up.astype(jnp.bfloat16), 'seq', scatter_dimension=0...  110 us
    reduce_scatter x1, waiting for transfers between devices, on_device(): lax.psum_scatter(grad_down.astype(jnp.bfloat16), 'seq', scatter_dimension...  110 us
    all_gather x1, waiting for transfers between devices, on_device(): lax.all_gather(w_gate, 'seq', axis=0, tiled=True)  84.4 us
    psum x1, waiting for transfers between devices, on_device(): lax.psum(dh_local_two.astype(jnp.bfloat16), 'tp').astype(jnp.float32)  83.7 us
    all_gather x1, waiting for transfers between devices, on_device(): lax.all_gather(w_down, 'seq', axis=1, tiled=True)  81.6 us
    all_gather x1, waiting for transfers between devices, on_device(): lax.all_gather(w_up, 'seq', axis=0, tiled=True)  81.5 us
    reduce_scatter x1, waiting for transfers between devices, on_device(): lax.psum_scatter(grad_value.astype(jnp.bfloat16), 'seq', scatter_dimensio...  68.8 us
  transfers between devices with their start and end apart: 17, of which 12 were waited for; matrix products, arithmetic and copies ran while one was open for 19% of the time, Pallas kernels for 0%

commit v1 on v0

--- a/solution.py
+++ b/solution.py
@@ -1,15 +1,510 @@
+import functools
 import math
 
 import jax
 import jax.numpy as jnp
 from jax import lax
+from jax.experimental import pallas as pl
+from jax.experimental.pallas import tpu as pltpu
 from jax.sharding import PartitionSpec as P
 
 FEAT = 16
+MESH = pl.DeviceIdType.MESH
+MIB = 2**20
 
 
 HIGH = lax.Precision.HIGHEST
 EPSILON = 1e-06
+
+
+def remote(src, dst, send, recv, device):
+    return pltpu.make_async_remote_copy(
+        src_ref=src,
+        dst_ref=dst,
+        send_sem=send,
+        recv_sem=recv,
+        device_id=device,
+        device_id_type=MESH,
+    )
+
+
+class Place:
+    def __init__(self, n):
+        self.n, self.m = n, n // 2
+        self.s, self.t = lax.axis_index("seq"), lax.axis_index("tp")
+        self.o, self.i = self.s // 2, lax.rem(self.s, 2)
+        self.right, self.left = (self.s + 2, self.t), (self.s - 2, self.t)
+        self.pair = (self.o * 2 + 1 - self.i, self.t)
+        self.has_right, self.has_left = self.o < self.m - 1, self.o > 0
+        self.balanced = self.m >= 4
+        m, o = self.m, self.o
+        self.end = (o == 0) | (o == m - 1)
+        self.next = (o == 1) | (o == m - 2)
+        self.partner = jnp.where(
+            o == 0, 1, jnp.where(o == m - 1, m - 2, jnp.where(o == 1, 0, m - 1))
+        )
+
+    def greet(self, others=()):
+        barrier = pltpu.get_barrier_semaphore()
+
+        def signal(device):
+            pl.semaphore_signal(barrier, inc=1, device_id=device, device_id_type=MESH)
+
+        pl.when(self.has_right)(lambda: signal(self.right))
+        pl.when(self.has_left)(lambda: signal(self.left))
+        signal(self.pair)
+        for other in others:
+            signal(other)
+        beside = self.has_right.astype(jnp.int32) + self.has_left.astype(jnp.int32)
+        pl.semaphore_wait(barrier, beside + (1 + len(others)))
+
+
+class Gather:
+    def __init__(self, at, own, held, sems):
+        self.at, self.own_ref, self.held = at, own, held
+        self.send, self.recv, self.half_recv, self.local = sems
+
+    @staticmethod
+    def scratch(n):
+        return [
+            pltpu.SemaphoreType.DMA((3, n)),
+            pltpu.SemaphoreType.DMA((n,)),
+            pltpu.SemaphoreType.DMA((1,)),
+            pltpu.SemaphoreType.DMA((1,)),
+        ]
+
+    def copy(self, slot, way, own=False):
+        at = self.at
+        return remote(
+            self.own_ref if own else self.held.at[slot],
+            self.held.at[slot],
+            self.send.at[way, slot],
+            self.recv.at[slot],
+            (at.right, at.left, at.pair)[way],
+        )
+
+    def half(self, slot, way, which):
+        at, rows = self.at, self.held.shape[1] // 2
+        part = pl.ds(which * rows, rows)
+        return remote(
+            self.held.at[slot, part],
+            self.held.at[slot, part],
+            self.send.at[way, slot],
+            self.recv.at[slot] if which == 0 else self.half_recv.at[0],
+            (at.right, at.left, at.pair)[way],
+        )
+
+    def local_copy(self):
+        return pltpu.make_async_copy(self.own_ref, self.held.at[self.at.s], self.local.at[0])
+
+    def own(self):
+        at = self.at
+        self.local_copy().start()
+        pl.when(at.has_right)(lambda: self.copy(at.s, 0, True).start())
+        pl.when(at.has_left)(lambda: self.copy(at.s, 1, True).start())
+        self.copy(at.s, 2, True).start()
+
+    def to_pair(self, slot, act):
+        at = self.at
+        if not at.balanced:
+            act(self.copy(slot, 2))
+            return
+        partner = slot // 2 == at.partner
+        pl.when(jnp.logical_not(partner & (at.end | at.next)))(lambda: act(self.copy(slot, 2)))
+        pl.when(partner & at.end)(lambda: act(self.half(slot, 2, 0)))
+
+    def step(self, k):
+        at = self.at
+        for way in (0, 1):
+            slot = at.s - 2 * k if way == 0 else at.s + 2 * k
+            there = at.o - k >= 0 if way == 0 else at.o + k < at.m
+            on = at.has_right if way == 0 else at.has_left
+
+            @pl.when(there)
+            def _(slot=slot, on=on, way=way):
+                self.copy(slot, 2).wait_recv()
+                pl.when(on)(lambda: self.copy(slot, way).start())
+                self.to_pair(slot, lambda c: c.start())
+
+    def extra_copies(self, act):
+        at = self.at
+        slot = at.o * 2 + 1 - at.i
+        pl.when(at.o == 0)(lambda: act(self.copy(slot, 0)))
+        pl.when(at.o == at.m - 1)(lambda: act(self.copy(slot, 1)))
+        pl.when(at.o == 1)(lambda: act(self.half(slot, 1, 1)))
+        pl.when(at.o == at.m - 2)(lambda: act(self.half(slot, 0, 1)))
+
+    def extra(self):
+        at = self.at
+        if at.balanced:
+            slot = at.o * 2 + 1 - at.i
+            pl.when(at.end | at.next)(lambda: self.copy(slot, 2).wait_recv())
+            self.extra_copies(lambda c: c.start())
+
+    def arrive(self):
+        at = self.at
+        self.local_copy().wait()
+        for layer in range(at.m):
+            slot = layer * 2 + 1 - at.i
+            if not at.balanced:
+                self.copy(slot, 2).wait_recv()
+                continue
+            met = (at.o == layer) & (at.end | at.next)
+            halved = at.end & (at.partner == layer)
+            pl.when(jnp.logical_not(met | halved))(lambda: self.copy(slot, 2).wait_recv())
+
+            @pl.when(halved)
+            def _():
+                self.half(slot, 2, 0).wait_recv()
+                self.half(slot, 2, 1).wait_recv()
+
+    def drain(self):
+        at = self.at
+        pl.when(at.has_right)(lambda: self.copy(at.s, 0, True).wait_send())
+        pl.when(at.has_left)(lambda: self.copy(at.s, 1, True).wait_send())
+        self.copy(at.s, 2, True).wait_send()
+        for k in range(1, at.m):
+            for way in (0, 1):
+                slot = at.s - 2 * k if way == 0 else at.s + 2 * k
+                there = at.o - k >= 0 if way == 0 else at.o + k < at.m
+                on = at.has_right if way == 0 else at.has_left
+
+                @pl.when(there)
+                def _(slot=slot, on=on, way=way):
+                    pl.when(on)(lambda: self.copy(slot, way).wait_send())
+                    self.to_pair(slot, lambda c: c.wait_send())
+
+        if at.balanced:
+            self.extra_copies(lambda c: c.wait_send())
+
+
+def gather_events(groups):
+    m = groups[0].at.m
+    events = [groups[0].own]
+    for g, group in enumerate(groups):
+        for k in range(1, m):
+            if k == max(1, m - 1) and g + 1 < len(groups):
+                events.append(groups[g + 1].own)
+            events.append(functools.partial(group.step, k))
+            if k == 1 and g:
+                events.append(groups[g - 1].extra)
+    events.append(groups[-1].extra)
+    return events
+
+
+def gather_all(n, shards):
+    count = len(shards)
+
+    def kernel(*refs):
+        ins, outs, sems = refs[:count], refs[count : 2 * count], refs[2 * count :]
+        at = Place(n)
+        at.greet()
+        groups = [Gather(at, ins[g], outs[g], sems[4 * g : 4 * g + 4]) for g in range(count)]
+        for event in gather_events(groups):
+            event()
+        for group in groups:
+            group.arrive()
+            group.drain()
+
+    return pl.pallas_call(
+        kernel,
+        out_shape=[jax.ShapeDtypeStruct((n,) + a.shape, a.dtype) for a in shards],
+        in_specs=[pl.BlockSpec(memory_space=pl.ANY)] * count,
+        out_specs=[pl.BlockSpec(memory_space=pl.ANY)] * count,
+        scratch_shapes=Gather.scratch(n) * count,
+        compiler_params=pltpu.CompilerParams(collective_id=0, has_side_effects=True),
+    )(*shards)
+
+
+def add_rows(total, part, start, rows):
+    step = next(size for size in (64, 32, 16, 8) if rows % size == 0)
+
+    @pl.loop(0, rows // step)
+    def _(j):
+        at = pl.ds(pl.multiple_of(start + j * step, 8), step)
+        both = total[at, :].astype(jnp.float32) + part[at, :].astype(jnp.float32)
+        total[at, :] = both.astype(total.dtype)
+
+
+class Scatter:
+    def __init__(self, at, parts, out, bufs, sems):
+        self.at, self.parts, self.out = at, parts, out
+        self.mine, self.from_pair, self.from_line, self.extra_ref = bufs
+        (
+            self.pair_send,
+            self.pair_recv,
+            self.line_send,
+            self.line_recv,
+            self.extra_send,
+            self.extra_recv,
+            self.local,
+        ) = sems
+        self.rows = self.mine.shape[1]
+
+    @staticmethod
+    def scratch(n, shape, dtype):
+        m = n // 2
+        return [pltpu.VMEM((size,) + shape, dtype) for size in (m, m, m + 1, 2)] + [
+            pltpu.SemaphoreType.DMA((m,)),
+            pltpu.SemaphoreType.DMA((m,)),
+            pltpu.SemaphoreType.DMA((m,)),
+            pltpu.SemaphoreType.DMA((m + 1,)),
+            pltpu.SemaphoreType.DMA((2,)),
+            pltpu.SemaphoreType.DMA((2,)),
+            pltpu.SemaphoreType.DMA((m + 2,)),
+        ]
+
+    def load(self, layer):
+        return pltpu.make_async_copy(
+            self.parts.at[layer * 2 + self.at.i], self.mine.at[layer], self.local.at[layer]
+        )
+
+    def load_extra(self):
+        at = self.at
+        return pltpu.make_async_copy(
+            self.parts.at[at.o * 2 + 1 - at.i], self.extra_ref.at[1], self.local.at[at.m]
+        )
+
+    def store(self):
+        at = self.at
+        return pltpu.make_async_copy(self.mine.at[at.o], self.out, self.local.at[at.m + 1])
+
+    def to_pair(self, layer):
+        return remote(
+            self.parts.at[layer * 2 + 1 - self.at.i],
+            self.from_pair.at[layer],
+            self.pair_send.at[layer],
+            self.pair_recv.at[layer],
+            self.at.pair,
+        )
+
+    def half_to_pair(self, layer, which, src):
+        half = self.rows // 2
+        part = pl.ds(which * half, half)
+        return remote(
+            src.at[part],
+            self.from_pair.at[layer, part],
+            self.pair_send.at[layer] if which == 0 else self.extra_send.at[1],
+            self.pair_recv.at[layer] if which == 0 else self.extra_recv.at[1],
+            self.at.pair,
+        )
+
+    def sum_to_pair(self):
+        return remote(
+            self.extra_ref.at[1],
+            self.from_pair.at[self.at.o],
+            self.pair_send.at[self.at.o],
+            self.pair_recv.at[self.at.o],
+            self.at.pair,
+        )
+
+    def along(self, layer, way):
+        at = self.at
+        there = layer if way == 0 else jnp.where(layer == at.o - 1, at.m, layer)
+        return remote(
+            self.mine.at[layer],
+            self.from_line.at[there],
+            self.line_send.at[layer],
+            self.line_recv.at[there],
+            (at.right, at.left)[way],
+        )
+
+    def wait_line(self, place):
+        remote(
+            self.mine.at[0],
+            self.from_line.at[place],
+            self.line_send.at[0],
+            self.line_recv.at[place],
+            self.at.right,
+        ).wait_recv()
+
+    def shifted(self, way, which=None):
+        at, half = self.at, self.rows // 2
+        src, dst = self.parts.at[at.partner * 2 + 1 - at.i], self.extra_ref.at[0]
+        if which is not None:
+            src, dst = src.at[pl.ds(half, half)], dst.at[pl.ds(half, half)]
+        return remote(
+            src, dst, self.extra_send.at[0], self.extra_recv.at[0], (at.right, at.left)[way]
+        )
+
+    def far_first(self):
+        at = self.at
+        for d in range(at.m - 1, 0, -1):
+            yield at.o + d, at.o + d < at.m
+            yield at.o - d, at.o - d >= 0
+
+    def pair_copies(self, act):
+        at = self.at
+        for layer, there in self.far_first():
+            if not at.balanced:
+                pl.when(there)(lambda: act(self.to_pair(layer)))
+                continue
+            partner = layer == at.partner
+            pl.when(there & jnp.logical_not(partner & (at.end | at.next)))(
+                lambda: act(self.to_pair(layer))
+            )
+            pl.when(there & partner & at.end)(
+                lambda: act(self.half_to_pair(layer, 0, self.parts.at[layer * 2 + 1 - at.i]))
+            )
+        if not at.balanced:
+            act(self.to_pair(at.o))
+            return
+        pl.when(jnp.logical_not(at.end | at.next))(lambda: act(self.to_pair(at.o)))
+        pl.when(at.next)(
+            lambda: act(self.half_to_pair(at.o, 0, self.parts.at[at.o * 2 + 1 - at.i]))
+        )
+
+    def shift_copies(self, act):
+        at = self.at
+        if at.balanced:
+            pl.when(at.o == 0)(lambda: act(self.shifted(0, 1)))
+            pl.when(at.o == at.m - 1)(lambda: act(self.shifted(1, 1)))
+            pl.when(at.o == 1)(lambda: act(self.shifted(1)))
+            pl.when(at.o == at.m - 2)(lambda: act(self.shifted(0)))
+
+    def start(self):
+        at = self.at
+        self.shift_copies(lambda c: c.start())
+        self.pair_copies(lambda c: c.start())
+        for layer in range(at.m):
+            self.load(layer).start()
+        if at.balanced:
+            self.load_extra().start()
+
+    def extra(self):
+        at = self.at
+        if not at.balanced:
+            return
+        self.load_extra().wait()
+        half = self.rows // 2
+
+        @pl.when(at.end)
+        def _():
+            self.shifted(0).wait_recv()
+            add_rows(self.extra_ref.at[1], self.extra_ref.at[0], 0, self.rows)
+            self.sum_to_pair().start()
+
+        @pl.when(at.next)
+        def _():
+            self.shifted(0, 1).wait_recv()
+            add_rows(self.extra_ref.at[1], self.extra_ref.at[0], half, half)
+            self.half_to_pair(at.o, 1, self.extra_ref.at[1]).start()
+
+    def wait_pair(self, layer):
+        at = self.at
+        if not at.balanced:
+            self.to_pair(layer).wait_recv()
+            return
+        partner, own = layer == at.partner, layer == at.o
+        parted = (partner & at.end) | (own & at.next)
+        pl.when(jnp.logical_not((partner & (at.end | at.next)) | (own & at.next)))(
+            lambda: self.to_pair(layer).wait_recv()
+        )
+        pl.when(parted)(lambda: self.half_to_pair(layer, 0, self.extra_ref.at[1]).wait_recv())
+        pl.when(own & at.next)(
+            lambda: self.half_to_pair(layer, 1, self.extra_ref.at[1]).wait_recv()
+        )
+
+    def step(self, d):
+        at = self.at
+        for way in (0, 1):
+            layer = at.o + d if way == 0 else at.o - d
+            there = layer < at.m if way == 0 else layer >= 0
+            behind = at.has_left if way == 0 else at.has_right
+
+            @pl.when(there)
+            def _(layer=layer, behind=behind, way=way):
+                mine = self.mine.at[layer]
+                self.load(layer).wait()
+                self.wait_pair(layer)
+                if at.balanced:
+                    partner = layer == at.partner
+                    pl.when(jnp.logical_not(partner & (at.end | at.next)))(
+                        lambda: add_rows(mine, self.from_pair.at[layer], 0, self.rows)
+                    )
+                    pl.when(partner & at.end)(
+                        lambda: add_rows(mine, self.from_pair.at[layer], 0, self.rows // 2)
+                    )
+                else:
+                    add_rows(mine, self.from_pair.at[layer], 0, self.rows)
+
+                @pl.when(behind)
+                def _():
+                    self.wait_line(layer)
+                    add_rows(mine, self.from_line.at[layer], 0, self.rows)
+
+                self.along(layer, way).start()
+
+    def final(self):
+        at = self.at
+        mine = self.mine.at[at.o]
+        self.load(at.o).wait()
+        self.wait_pair(at.o)
+        add_rows(mine, self.from_pair.at[at.o], 0, self.rows)
+
+        @pl.when(at.has_left)
+        def _():
+            self.wait_line(at.o)
+            add_rows(mine, self.from_line.at[at.o], 0, self.rows)
+
+        @pl.when(at.has_right)
+        def _():
+            self.wait_line(at.m)
+            add_rows(mine, self.from_line.at[at.m], 0, self.rows)
+
+        self.store().start()
+
+    def drain(self):
+        at = self.at
+        self.pair_copies(lambda c: c.wait_send())
+        if at.balanced:
+            pl.when(at.end)(lambda: self.sum_to_pair().wait_send())
+            pl.when(at.next)(
+                lambda: self.half_to_pair(at.o, 1, self.extra_ref.at[1]).wait_send()
+            )
+        self.shift_copies(lambda c: c.wait_send())
+        for d in range(1, at.m):
+            pl.when(at.o + d < at.m)(lambda: self.along(at.o + d, 0).wait_send())
+            pl.when(at.o - d >= 0)(lambda: self.along(at.o - d, 1).wait_send())
+        self.store().wait()
+
+
+def scatter_all(n, parts):
+    count = len(parts)
+    shapes = [(a.shape[1:], a.dtype) for a in parts]
+
+    def kernel(*refs):
+        ins, outs, rest = refs[:count], refs[count : 2 * count], refs[2 * count :]
+        at = Place(n)
+        at.greet()
+        groups = [
+            Scatter(at, ins[g], outs[g], rest[11 * g : 11 * g + 4], rest[11 * g + 4 : 11 * g + 11])
+            for g in range(count)
+        ]
+        groups[0].start()
+        groups[1].start()
+        for g, group in enumerate(groups):
+            for d in range(at.m - 1, 0, -1):
+                group.step(d)
+                if d == at.m - 1 and g + 2 < count:
+                    groups[g + 2].start()
+            group.extra()
+            if g:
+                groups[g - 1].final()
+        groups[-1].final()
+        for group in groups:
+            group.drain()
+
+    return pl.pallas_call(
+        kernel,
+        out_shape=[jax.ShapeDtypeStruct(*kind) for kind in shapes],
+        in_specs=[pl.BlockSpec(memory_space=pl.ANY)] * count,
+        out_specs=[pl.BlockSpec(memory_space=pl.ANY)] * count,
+        scratch_shapes=sum((Scatter.scratch(n, *kind) for kind in shapes), []),
+        compiler_params=pltpu.CompilerParams(
+            collective_id=1, has_side_effects=True, vmem_limit_bytes=60 * MIB
+        ),
+    )(*parts)
 
 
 def entering(value, axis, join, neutral):
@@ -137,28 +632,25 @@
     w_down,
     cotangent,
 ):
-    gathered = (
-        lax.all_gather(first_gain, "seq", axis=0, tiled=True),
-        lax.all_gather(w_query, "seq", axis=0, tiled=True),
-        lax.all_gather(w_key, "seq", axis=0, tiled=True),
-        lax.all_gather(w_value, "seq", axis=0, tiled=True),
-        lax.all_gather(w_out, "seq", axis=1, tiled=True),
-        lax.all_gather(second_gain, "seq", axis=0, tiled=True),
-        lax.all_gather(w_gate, "seq", axis=0, tiled=True),
-        lax.all_gather(w_up, "seq", axis=0, tiled=True),
-        lax.all_gather(w_down, "seq", axis=1, tiled=True),
-    )
-    (
-        first_full,
-        query_full,
-        key_full,
-        value_full,
-        out_full,
-        second_full,
-        gate_full,
-        up_full,
-        down_full,
-    ) = gathered
+    n = lax.axis_size("seq")
+    qkv_own = jnp.concatenate([w_query, w_key, w_value], axis=1)
+    gains_own = jnp.concatenate([first_gain, second_gain]).astype(jnp.float32)
+    gains_own = jnp.broadcast_to(gains_own[None], (16, gains_own.shape[0]))
+    gains, qkv_full, out_full, gate_full, up_full, down_full = gather_all(
+        n, (gains_own, qkv_own, w_out, w_gate, w_up, w_down)
+    )
+    depth = first_gain.shape[0]
+    first_full = gains[:, 0, :depth].reshape(-1).astype(jnp.bfloat16)
+    second_full = gains[:, 0, depth:].reshape(-1).astype(jnp.bfloat16)
+    qkv_full = qkv_full.reshape(-1, qkv_full.shape[-1])
+    q_wide, k_wide = w_query.shape[1], w_key.shape[1]
+    query_full = qkv_full[:, :q_wide]
+    key_full = qkv_full[:, q_wide : q_wide + k_wide]
+    value_full = qkv_full[:, q_wide + k_wide :]
+    gate_full = gate_full.reshape(-1, gate_full.shape[-1])
+    up_full = up_full.reshape(-1, up_full.shape[-1])
+    out_full = jnp.swapaxes(out_full, 0, 1).reshape(out_full.shape[1], -1)
+    down_full = jnp.swapaxes(down_full, 0, 1).reshape(down_full.shape[1], -1)
     row_count = stream_in.shape[0]
     heads_local = query_full.shape[1] // FEAT
     head_width = value_full.shape[1] // heads_local
@@ -240,49 +732,42 @@
     _, norm_one_pull = jax.vjp(rms_scale, stream_f, first_gf)
     dstream_norm, grad_first = norm_one_pull(dh_one)
     input_grad = dmid + dstream_norm
-    reduced = tuple(
+    def rows_of(g):
+        return g.astype(jnp.bfloat16).reshape((n, g.shape[0] // n) + g.shape[1:])
+
+    def cols_of(g):
+        g = g.astype(jnp.bfloat16).reshape(g.shape[0], n, g.shape[1] // n)
+        return jnp.swapaxes(g, 0, 1)
+
+    grad_qkv = jnp.concatenate([grad_query, grad_key, grad_value], axis=1)
+    gains_part = jnp.concatenate(
+        [grad_first.reshape(n, 1, depth), grad_second.reshape(n, 1, depth)], axis=2
+    )
+    gains_part = jnp.broadcast_to(gains_part, (n, 16, 2 * depth))
+    own_down, own_gate, own_up, own_out, own_qkv, own_gains = scatter_all(
+        n,
         (
-            lax.psum_scatter(
-                grad_first.astype(jnp.bfloat16), "seq", scatter_dimension=0, tiled=True
-            ).astype(jnp.float32),
-            lax.psum_scatter(
-                grad_query.astype(jnp.bfloat16), "seq", scatter_dimension=0, tiled=True
-            ).astype(jnp.float32),
-            lax.psum_scatter(
-                grad_key.astype(jnp.bfloat16), "seq", scatter_dimension=0, tiled=True
-            ).astype(jnp.float32),
-            lax.psum_scatter(
-                grad_value.astype(jnp.bfloat16), "seq", scatter_dimension=0, tiled=True
-            ).astype(jnp.float32),
-            lax.psum_scatter(
-                grad_out.astype(jnp.bfloat16), "seq", scatter_dimension=1, tiled=True
-            ).astype(jnp.float32),
-            lax.psum_scatter(
-                grad_second.astype(jnp.bfloat16), "seq", scatter_dimension=0, tiled=True
-            ).astype(jnp.float32),
-            lax.psum_scatter(
-                grad_gate.astype(jnp.bfloat16), "seq", scatter_dimension=0, tiled=True
-            ).astype(jnp.float32),
-            lax.psum_scatter(
-                grad_up.astype(jnp.bfloat16), "seq", scatter_dimension=0, tiled=True
-            ).astype(jnp.float32),
-            lax.psum_scatter(
-                grad_down.astype(jnp.bfloat16), "seq", scatter_dimension=1, tiled=True
-            ).astype(jnp.float32),
-        )
-    )
+            cols_of(grad_down),
+            rows_of(grad_gate),
+            rows_of(grad_up),
+            cols_of(grad_out),
+            rows_of(grad_qkv),
+            gains_part,
+        ),
+    )
+    own_qkv = own_qkv.astype(jnp.float32)
     return (
         activations,
         input_grad,
-        reduced[0],
-        reduced[1],
-        reduced[2],
-        reduced[3],
-        reduced[4],
-        reduced[5],
-        reduced[6],
-        reduced[7],
-        reduced[8],
+        own_gains[0, :depth],
+        own_qkv[:, :q_wide],
+        own_qkv[:, q_wide : q_wide + k_wide],
+        own_qkv[:, q_wide + k_wide :],
+        own_out.astype(jnp.float32),
+        own_gains[0, depth:],
+        own_gate.astype(jnp.float32),
+        own_up.astype(jnp.float32),
+        own_down.astype(jnp.float32),
     )
 
 

time: 1630 us -> 1260 us (0.77)
  waiting for transfers between devices: 977 us -> 228 us
  Pallas kernels: 0 us -> 461 us
  blocking collectives: 228 us -> 80.3 us
  local copies, waits for them, and re-layouts: 15.2 us -> 89.5 us
    pallas_call x0 -> x2, Pallas kernels: none -> 461 us  [the longest x1 234 us: scatter_all(): pl.pallas_call(kernel, out_shape=[jax.ShapeDtypeStruct(*kind) for kind in...]
    reduce_scatter x7 -> x0, waiting for transfers between devices: 426 us -> none  [the longest x1 110 us: on_device(): lax.psum_scatter(grad_up.astype(jnp.bfloat16), 'seq', scatter_dimension=0...]
    all_gather x5 -> x0, waiting for transfers between devices: 247 us -> none  [the longest x1 84.4 us: on_device(): lax.all_gather(w_gate, 'seq', axis=0, tiled=True)]
    all_gather x4 -> x0, blocking collectives: 126 us -> none  [the longest x1 40.1 us: on_device(): lax.all_gather(second_gain, 'seq', axis=0, tiled=True)]
    psum x1, waiting for transfers between devices: 153 us -> 93.5 us  [on_device(): dh_one = lax.psum(dh_local.astype(jnp.bfloat16), 'tp').astype(jnp.float32)]
    convert_element_type x0 -> x4, local copies, waits for them, and re-layouts: none -> 28.1 us  [the longest x2 16.7 us: rows_of(): return g.astype(jnp.bfloat16).reshape((n, g.shape[0] // n) + g.shape[1:])]
    psum x1, waiting for transfers between devices: 83.7 us -> 55.8 us  [on_device(): lax.psum(dh_local_two.astype(jnp.bfloat16), 'tp').astype(jnp.float32)]
    unnamed x2 -> x1, blocking collectives: 40 us -> 19 us
  transfers between devices with their start and end apart: 17 -> 5, of which waited for: 12 -> 3; matrix products, arithmetic and copies ran while one was open for 19% -> 16% of each run, Pallas kernels for 0% -> 0%
where the time goes in v1:
time: 1260 us; the launch traced here: 1250 us
  Pallas kernels  461 us (37%)
  matrix products  279 us (22%)
  waiting for transfers between devices  228 us (18%)
  other arithmetic  97.3 us (8%)
  local copies, waits for them, and re-layouts  89.5 us (7%)
  blocking collectives  80.3 us (6%)
  between operations  15.2 us (1%)
    pallas_call x1, Pallas kernels, scatter_all(): pl.pallas_call(kernel, out_shape=[jax.ShapeDtypeStruct(*kind) for kind in...  234 us
    pallas_call x1, Pallas kernels, gather_all(): pl.pallas_call(kernel, out_shape=[jax.ShapeDtypeStruct((n,) + a.shape, a....  226 us
    psum x1, waiting for transfers between devices, on_device(): dh_one = lax.psum(dh_local.astype(jnp.bfloat16), 'tp').astype(jnp.float32)  93.5 us
    psum x1, waiting for transfers between devices, on_device(): lax.psum(attn_term.astype(jnp.bfloat16), 'tp').astype(jnp.float32)  78.9 us
    dot_general x3, matrix products, attend(): numerator = jnp.einsum('hij,jhd->ihd', weights, value_rows, precision=HIGH)  56 us
    psum x1, waiting for transfers between devices, on_device(): lax.psum(dh_local_two.astype(jnp.bfloat16), 'tp').astype(jnp.float32)  55.8 us
    dot_general x7, matrix products, contract_cols(): lax.dot_general(left, right, (((1,), (1,)), ((), ())), preferred_element_...  55.7 us
    dot_general x7, matrix products, contract_rows(): lax.dot_general(left, right, (((0,), (0,)), ((), ())), preferred_element_...  45.8 us
  transfers between devices with their start and end apart: 5, of which 3 were waited for; matrix products, arithmetic and copies ran while one was open for 16% of the time, Pallas kernels for 0%

profile of v1, /device:TPU:0, one launch (start us, length us, event | category | flops | bytes accessed | tf_op | source)
XLA Modules:
  0.0 1252.0 jit_solution(11778845566038569952)
XLA Ops:
  16.6 226.4 %shard_map.203 = (f32[8,16,512]{2,1,0:T(8,128)}, bf16[8,256,640]{2,1,0:T(8,128)(2,1)}, bf16[8,512,256]{2,1,0:T(8,128)(2,1)}, bf16[8,256,1376]{2,1,0:T(8,128)(2,1...) custom-call(f32[16,512]{1,0:T(8,128)} %broadcast_in_dim.40.refs_0_, ...), custom_call_target="tpu_custom_call" | custom-call | tf_op jit(solution)/shard_map/pallas_call | solution.py:209
  262.6 19.0 %all-reduce = bf16[8]{0:T(256)(128)(2,1)S(1)} all-reduce(bf16[8]{0:T(256)(128)(2,1)S(1)} %dynamic-update-slice), channel_id=3, replica_groups=mesh['seq'=8,'tp'=4] {'seq'}, use_global_device_ids=true, to_apply=%add | all-reduce | flops 8 | bytes 32
  287.5 30.4 %all-gather.5 = bf16[8,4,273]{2,1,0:T(4,128)(2,1)S(1)} all-gather(bf16[1,4,273]{2,1,0:T(4,128)(2,1)S(1)} %bitcast.260), channel_id=4, replica_groups=mesh['seq'=8,'tp'=4] {'seq'}, dimensions={0}, use_global_device_ids=true | all-gather | bytes 19656 | tf_op jit(solution)/shard_map/all_gather | solution.py:513
  324.1 8.0 fusion.41
  332.1 13.6 %fusion.42 = f32[4,128,1024]{2,1,0:T(8,128)} fusion(bf16[1024,4,128]{0,2,1:T(8,128)(2,1)S(1)} %bitcast.233, f32[4,1024,1024]{1,2,0:T(8,128)} %get-tuple-element.415, f32[1024,1024]{0,1:T(8,128)S(1)} %fusion.24), kind=kOutput, calls=%fused_computation.102 | convolution fusion | flops 6467616768 | bytes 24117248 | tf_op jit(solution)/shard_map/jvp(hij,jhd->ihd)/dot_general | solution.py:573
  369.6 8.2 copy.151
  377.8 11.5 fusion.76
  389.4 78.9 %all-reduce.6.cloned.1.call-done = bf16[1024,2048]{1,0:T(8,128)(2,1)} async-done(((bf16[1024,2048]{1,0:T(8,128)(2,1)}), bf16[1024,2048]{1,0:T(8,128)(2,1)}) %all-reduce.6.cloned.1.call-update) | async-done | bytes 4194320 | tf_op jit(solution)/shard_map/psum | solution.py:687
  476.9 8.1 fusion.75
  485.0 15.3 %multiply_convert_fusion.1 = (bf16[1024,1376]{0,1:T(8,128)(2,1)}, bf16[1024,1376]{0,1:T(8,128)(2,1)}, bf16[1024,1376]{0,1:T(8,128)(2,1)}) fusion(f32[1024,1376]{0,1:T(8,128)} %fusion.75, f32[1376,1024]{1,0:T(8,128)} %fusion.76, bf16[1024,2048]{1,0:T(8,128)(2,1)S(1)} %multiply_convert_fusion, bf16[2048,1376]{1,0:T(8,128)(2,1)} %bitcast.264), kind=kOutput, calls=%fused_computation.49 | convolution fusion | flops 5792497664 | bytes 29556736 | tf_op jit(solution)/shard_map/dot_general | solution.py:690
  500.2 9.8 fusion.77
  510.1 11.1 add_convert_fusion.1
  521.3 10.5 convolution_convert_fusion.1
  531.7 8.3 copy.162
  540.1 11.1 convolution_convert_fusion.3
  551.2 55.8 %all-reduce.8.cloned.1.call-done = bf16[1024,2048]{1,0:T(8,128)(2,1)} async-done(((bf16[1024,2048]{1,0:T(8,128)(2,1)}), bf16[1024,2048]{1,0:T(8,128)(2,1)}) %all-reduce.8.cloned.1.call-update) | async-done | bytes 4194320 | tf_op jit(solution)/shard_map/psum | solution.py:705
  607.0 8.7 fusion.10
  634.0 20.4 %fusion.3 = f32[4,1024,1024]{1,2,0:T(8,128)} fusion(f32[4,1024,1024]{1,2,0:T(8,128)} %get-tuple-element.415, bf16[1024,4,128]{0,2,1:T(8,128)(2,1)S(1)} %bitcast.234, f32[4,1024]{1,0:T(4,128)S(1)} %get-tuple-element.406, f32[1024,1024]{0,1:T(8,128)} %copy-done.19, f32[1024,4,128]{0,2,1:T(8,128)} %copy-done.61, f32[4,1024]{1,0:T(4,128)S(1)} %get-tuple-element.393), kind=kOutput, calls=%fused_computation.10 | convolution fusion | flops 6484918272 | bytes 40927232 | tf_op jit(solution)/shard_map/transpose(jvp(hij,jhd->ihd))/dot_general | solution.py:573
  666.3 30.9 %all-gather.6 = bf16[8,4,273]{2,1,0:T(4,128)(2,1)S(1)} all-gather(bf16[1,4,273]{2,1,0:T(4,128)(2,1)S(1)} %bitcast.261), channel_id=6, replica_groups=mesh['seq'=8,'tp'=4] {'seq'}, dimensions={0}, use_global_device_ids=true | all-gather | bytes 19656 | tf_op jit(solution)/shard_map/all_gather | solution.py:535
  701.0 9.2 fusion.38
  716.0 22.1 %fusion.40 = f32[4,128,1024]{2,1,0:T(8,128)S(1)} fusion(f32[4,1024,1024]{1,2,0:T(8,128)} %get-tuple-element.415, f32[1024,1024]{0,1:T(8,128)S(1)} %copy-done.20, f32[1024,4,128]{0,2,1:T(8,128)S(1)} %copy-done.63, f32[4,1024]{1,0:T(4,128)S(1)} %copy-done.51), kind=kOutput, calls=%fused_computation.100 | convolution fusion | flops 6468141056 | bytes 25182208 | tf_op jit(solution)/shard_map/transpose(jvp(hij,jhd->ihd))/dot_general | solution.py:573
  738.2 26.2 %while.33 = (s32[]{:T(128)}, f32[4,273,128]{2,1,0:T(8,128)S(1)}, f32[4,273]{1,0:T(4,128)S(1)}, s32[]{:T(128)}, bf16[8,4,273,128]{3,2,1,0:T(8,128)(2,1)}, /*index...) while((s32[]{:T(128)}, f32[4,273,128]{2,1,0:T(8,128)S(1)}, ...), condition=%wide.region_16.17_spmd.clone, body=%wide.region_15.16_spmd.clone.sunk | while | flops 704349 | bytes 1408891 | solution.py:553
  784.3 11.5 fusion.39
  795.8 9.3 add_convert_fusion
  806.9 9.9 convolution_convert_fusion
  816.8 8.4 copy.163
  825.2 9.9 convolution_convert_fusion.2
  835.1 8.5 copy.160
  843.6 8.7 copy.161
  864.9 93.5 %all-reduce.10.cloned.1.call-done = (bf16[1024,2048]{1,0:T(8,128)(2,1)}, bf16[1024,2048]{1,0:T(8,128)(2,1)}) async-done(((bf16[1024,2048]{1,0:T(8,128)(2,1)}, bf16[1024,2048]{1,0:T(8,128)(2,1)}), (bf16[1024,2048]{1,0:T(8,128)(2,1)}, bf16[1024,2048]{1,0:T(8,128)(2,1)})) %all-reduce.10.cloned.1.call-update) | async-done | bytes 8388624 | tf_op jit(solution)/shard_map/psum | solution.py:731
  964.3 15.7 %fusion.67 = (bf16[2048,1024]{0,1:T(8,128)(2,1)}, f32[1024,2048]{1,0:T(8,128)}, bf16[1024,2048]{1,0:T(8,128)(2,1)}) fusion(f32[2048]{0:T(1024)S(1)} %bitcast.258, f32[1024]{0:T(1024)S(1)} %copy-done.46, bf16[1024,2048]{1,0:T(8,128)(2,1)} %param.16, f32[1024,2048]{1,0:T(8,128)} %copy-done.8, f32[1024]{0:T(1024)S(1)} %multiply_multiply_fusion.2, ...), kind=kLoop, calls=%fused_computation.152 | loop fusion | flops 33554432 | bytes 41959424 | tf_op jit(solution)/shard_map/dot_general | solution.py:610
  998.5 234.1 %shard_map.204 = (bf16[1376,256]{1,0:T(8,128)(2,1)}, bf16[256,1376]{1,0:T(8,128)(2,1)}, bf16[256,1376]{1,0:T(8,128)(2,1)}, bf16[512,256]{1,0:T(8,128)(2,1)}, bf1...) custom-call(bf16[8,1376,256]{2,1,0:T(8,128)(2,1)} %bitcast.202, bf16[8,256,1376]{2,1,0:T(8,128)(2,1)} %bitcast.200, ...), custom_call_target="tpu_custom_call" | custom-call | tf_op jit(solution)/shard_map/pallas_call | solution.py:498
  (261 shorter events, 209.3 us)
Async XLA Ops:
  7.2 338.5 %all-gather.10.cloned.1.call-start = ((), (), s32[]{:S(2)}) async-start(), calls=%async_computation.2 | async-start | bytes 2580480 | tf_op jit(solution)/shard_map/all_gather | solution.py:513
  11.1 307.4 %copy-start.45 = (f32[1024]{0:T(1024)}, f32[1024]{0:T(1024)S(1)}, u32[]{:S(2)}) copy-start(f32[1024]{0:T(1024)S(1)} %fusion.56) | copy-start | bytes 12292
  244.2 74.3 %copy-start.41 = (f32[8,1,256]{2,1,0:T(1,128)}, f32[8,1,256]{2,1,0:T(1,128)S(1)}, u32[]{:S(2)}) copy-start(f32[8,1,256]{2,1,0:T(1,128)S(1)} %get-tuple-element.403) | copy-start | bytes 24580
  248.6 35.4 %copy-start.13 = (f32[1024,64]{0,1:T(8,128)}, f32[1024,64]{0,1:T(8,128)S(1)}, u32[]{:S(2)}) copy-start(f32[1024,64]{0,1:T(8,128)S(1)} %get-tuple-element.410) | copy-start | bytes 786436
  248.6 75.5 %copy-start.39 = (bf16[1024,64]{0,1:T(8,128)(2,1)}, bf16[1024,64]{0,1:T(8,128)(2,1)S(1)}, u32[]{:S(2)}) copy-start(bf16[1024,64]{0,1:T(8,128)(2,1)S(1)} %get-tuple-element.411) | copy-start | bytes 393220
  253.7 30.3 %copy-start.43 = (f32[1024]{0:T(1024)}, f32[1024]{0:T(1024)S(1)}, u32[]{:S(2)}) copy-start(f32[1024]{0:T(1024)S(1)} %get-tuple-element.409) | copy-start | bytes 12292
  254.3 27.2 %copy-start.15 = (bf16[8,512,256]{2,1,0:T(8,128)(2,1)S(1)}, bf16[8,512,256]{2,1,0:T(8,128)(2,1)}, u32[]{:S(2)}) copy-start(bf16[8,512,256]{2,1,0:T(8,128)(2,1)} %get-tuple-element.263) | copy-start | bytes 6291460
  260.0 208.3 %all-reduce.6.cloned.1.call-start = ((), (), s32[]{:S(2)}) async-start(), calls=%async_computation | async-start | bytes 8388608 | tf_op jit(solution)/shard_map/psum | solution.py:687
  284.0 34.5 %copy-start.1 = (bf16[1024,2048]{1,0:T(8,128)(2,1)S(1)}, bf16[1024,2048]{1,0:T(8,128)(2,1)}, u32[]{:S(2)}) copy-start(bf16[1024,2048]{1,0:T(8,128)(2,1)} %param.16) | copy-start | bytes 12582916
  318.5 13.6 %copy-start.19 = (f32[1024,1024]{0,1:T(8,128)}, f32[1024,1024]{0,1:T(8,128)S(1)}, u32[]{:S(2)}) copy-start(f32[1024,1024]{0,1:T(8,128)S(1)} %fusion.24) | copy-start | bytes 12582916
  321.5 10.6 copy-start.37
  351.4 302.9 %copy-start.50 = (f32[4,1024]{1,0:T(4,128)}, f32[4,1024]{1,0:T(4,128)S(1)}, u32[]{:S(2)}) copy-start(f32[4,1024]{1,0:T(4,128)S(1)} %get-tuple-element.393) | copy-start | bytes 49156
  363.8 243.2 %all-reduce.8.cloned.1.call-start = ((), (), s32[]{:S(2)}) async-start(), calls=%async_computation.1 | async-start | bytes 8388608 | tf_op jit(solution)/shard_map/psum | solution.py:705
  500.2 9.8 copy-start.65
  521.2 216.9 %all-gather.12.cloned.1.call-start = ((), (), s32[]{:S(2)}) async-start(), calls=%async_computation.3 | async-start | bytes 2580480 | tf_op jit(solution)/shard_map/all_gather | solution.py:535
  607.0 8.7 copy-start.5
  607.0 8.7 copy-start.11
  634.0 20.4 %copy-start.62 = (f32[1024,4,128]{0,2,1:T(8,128)S(1)}, f32[1024,4,128]{0,2,1:T(8,128)}, u32[]{:S(2)}) copy-start(f32[1024,4,128]{0,2,1:T(8,128)} %copy-done.61) | copy-start | bytes 6291460
  660.1 298.3 %all-reduce.10.cloned.1.call-start = ((), (), s32[]{:S(2)}) async-start(), calls=%async_computation.4 | async-start | bytes 16777216 | tf_op jit(solution)/shard_map/psum | solution.py:731
  660.1 37.1 %copy-start.12 = (f32[1024,4,273]{0,2,1:T(8,128)S(1)}, f32[1024,4,273]{0,2,1:T(8,128)}, u32[]{:S(2)}) copy-start(f32[1024,4,273]{0,2,1:T(8,128)} %multiply_bitcast_fusion.1) | copy-start | bytes 13418500
  716.0 22.1 %copy-start.9 = (f32[4,273,128]{2,1,0:T(8,128)S(1)}, f32[4,273,128]{2,1,0:T(8,128)}, u32[]{:S(2)}) copy-start(f32[4,273,128]{2,1,0:T(8,128)} %custom-call) | copy-start | bytes 1677316
  716.0 22.1 %copy-start.36 = (f32[4,273]{1,0:T(4,128)S(1)}, f32[4,273]{1,0:T(4,128)}, u32[]{:S(2)}) copy-start(f32[4,273]{1,0:T(4,128)} %custom-call.1) | copy-start | bytes 13108
  716.0 22.1 %copy-start.58 = (bf16[8,1]{0,1:T(2,128)(2,1)S(1)}, bf16[8,1]{0,1:T(2,128)(2,1)}, u32[]{:S(2)}) copy-start(bf16[8,1]{0,1:T(2,128)(2,1)} %copy-done.57) | copy-start | bytes 52
  738.1 26.3 %copy-start.14 = (f32[1024,64]{0,1:T(8,128)S(1)}, f32[1024,64]{0,1:T(8,128)}, u32[]{:S(2)}) copy-start(f32[1024,64]{0,1:T(8,128)} %copy-done.13) | copy-start | bytes 786436
  738.1 26.3 %copy-start.44 = (f32[1024]{0:T(1024)S(1)}, f32[1024]{0:T(1024)}, u32[]{:S(2)}) copy-start(f32[1024]{0:T(1024)} %copy-done.43) | copy-start | bytes 12292
  843.6 8.8 copy-start.49
  843.6 8.8 copy-start.56
  859.6 98.8 %copy-start.42 = (f32[8,1,256]{2,1,0:T(1,128)S(1)}, f32[8,1,256]{2,1,0:T(1,128)}, u32[]{:S(2)}) copy-start(f32[8,1,256]{2,1,0:T(1,128)} %copy-done.41) | copy-start | bytes 24580
  859.6 98.8 %copy-start.46 = (f32[1024]{0:T(1024)S(1)}, f32[1024]{0:T(1024)}, u32[]{:S(2)}) copy-start(f32[1024]{0:T(1024)} %copy-done.45) | copy-start | bytes 12292
  864.9 99.4 %copy-start.48 = (f32[1024]{0:T(1024)S(1)}, f32[1024]{0:T(1024)}, u32[]{:S(2)}) copy-start(f32[1024]{0:T(1024)} %copy-done.47) | copy-start | bytes 12292
  1232.6 9.8 copy-start.29
  1232.6 11.2 copy-start.32
  (42 other events, 228.4 us)
Sparse Core Ops, SparseCore 0:
  260.1 49.9 all-gather.9
  363.9 104.2 all-reduce.5
  521.3 85.6 all-reduce.7
  660.2 51.6 all-gather.11
  805.2 153.0 all-reduce.9

commit v2 on v1

v2 whole, which is shorter than its diff:
```python
import functools

import jax
import jax.numpy as jnp
import numpy as np
from jax import lax
from jax.experimental import pallas as pl
from jax.experimental.pallas import tpu as pltpu
from jax.sharding import PartitionSpec as P

FEAT = 16
EPSILON = 1e-06
MESH = pl.DeviceIdType.MESH
MIB = 2**20


def remote(src, dst, send, recv, device):
    return pltpu.make_async_remote_copy(
        src_ref=src,
        dst_ref=dst,
        send_sem=send,
        recv_sem=recv,
        device_id=device,
        device_id_type=MESH,
    )


class Place:
    def __init__(self, n):
        self.n, self.m = n, n // 2
        self.s, self.t = lax.axis_index("seq"), lax.axis_index("tp")
        self.o, self.i = self.s // 2, lax.rem(self.s, 2)
        self.right, self.left = (self.s + 2, self.t), (self.s - 2, self.t)
        self.pair = (self.o * 2 + 1 - self.i, self.t)
        self.has_right, self.has_left = self.o < self.m - 1, self.o > 0
        self.balanced = self.m >= 4
        m, o = self.m, self.o
        self.end = (o == 0) | (o == m - 1)
        self.next = (o == 1) | (o == m - 2)
        self.partner = jnp.where(
            o == 0, 1, jnp.where(o == m - 1, m - 2, jnp.where(o == 1, 0, m - 1))
        )

    def greet(self, others=()):
        barrier = pltpu.get_barrier_semaphore()

        def signal(device):
            pl.semaphore_signal(barrier, inc=1, device_id=device, device_id_type=MESH)

        pl.when(self.has_right)(lambda: signal(self.right))
        pl.when(self.has_left)(lambda: signal(self.left))
        signal(self.pair)
        for other in others:
            signal(other)
        beside = self.has_right.astype(jnp.int32) + self.has_left.astype(jnp.int32)
        pl.semaphore_wait(barrier, beside + (1 + len(others)))


class Gather:
    def __init__(self, at, own, held, sems):
        self.at, self.own_ref, self.held = at, own, held
        self.send, self.recv, self.half_recv, self.local = sems

    @staticmethod
    def scratch(n):
        return [
            pltpu.SemaphoreType.DMA((3, n)),
            pltpu.SemaphoreType.DMA((n,)),
            pltpu.SemaphoreType.DMA((1,)),
            pltpu.SemaphoreType.DMA((1,)),
        ]

    def slot(self, slot, start=0, rows=None):
        if self.held.ndim == 3:
            return self.held.at[slot] if rows is None else self.held.at[slot, pl.ds(start, rows)]
        tall = self.own_ref.shape[0]
        first = pl.multiple_of(slot * tall, 16) + start
        return self.held.at[pl.ds(first, tall if rows is None else rows)]

    def copy(self, slot, way, own=False):
        at = self.at
        return remote(
            self.own_ref if own else self.slot(slot),
            self.slot(slot),
            self.send.at[way, slot],
            self.recv.at[slot],
            (at.right, at.left, at.pair)[way],
        )

    def half(self, slot, way, which):
        at, rows = self.at, self.own_ref.shape[0] // 2
        part = self.slot(slot, which * rows, rows)
        return remote(
            part,
            part,
            self.send.at[way, slot],
            self.recv.at[slot] if which == 0 else self.half_recv.at[0],
            (at.right, at.left, at.pair)[way],
        )

    def local_copy(self):
        return pltpu.make_async_copy(self.own_ref, self.slot(self.at.s), self.local.at[0])

    def own(self):
        at = self.at
        self.local_copy().start()
        pl.when(at.has_right)(lambda: self.copy(at.s, 0, True).start())
        pl.when(at.has_left)(lambda: self.copy(at.s, 1, True).start())
        self.copy(at.s, 2, True).start()

    def to_pair(self, slot, act):
        at = self.at
        if not at.balanced:
            act(self.copy(slot, 2))
            return
        partner = slot // 2 == at.partner
        pl.when(jnp.logical_not(partner & (at.end | at.next)))(lambda: act(self.copy(slot, 2)))
        pl.when(partner & at.end)(lambda: act(self.half(slot, 2, 0)))

    def step(self, k):
        at = self.at
        for way in (0, 1):
            slot = at.s - 2 * k if way == 0 else at.s + 2 * k
            there = at.o - k >= 0 if way == 0 else at.o + k < at.m
            on = at.has_right if way == 0 else at.has_left

            @pl.when(there)
            def _(slot=slot, on=on, way=way):
                self.copy(slot, 2).wait_recv()
                pl.when(on)(lambda: self.copy(slot, way).start())
                self.to_pair(slot, lambda c: c.start())

    def extra_copies(self, act):
        at = self.at
        slot = at.o * 2 + 1 - at.i
        pl.when(at.o == 0)(lambda: act(self.copy(slot, 0)))
        pl.when(at.o == at.m - 1)(lambda: act(self.copy(slot, 1)))
        pl.when(at.o == 1)(lambda: act(self.half(slot, 1, 1)))
        pl.when(at.o == at.m - 2)(lambda: act(self.half(slot, 0, 1)))

    def extra(self):
        at = self.at
        if at.balanced:
            slot = at.o * 2 + 1 - at.i
            pl.when(at.end | at.next)(lambda: self.copy(slot, 2).wait_recv())
            self.extra_copies(lambda c: c.start())

    def arrive(self):
        at = self.at
        self.local_copy().wait()
        for layer in range(at.m):
            slot = layer * 2 + 1 - at.i
            if not at.balanced:
                self.copy(slot, 2).wait_recv()
                continue
            met = (at.o == layer) & (at.end | at.next)
            halved = at.end & (at.partner == layer)
            pl.when(jnp.logical_not(met | halved))(lambda: self.copy(slot, 2).wait_recv())

            @pl.when(halved)
            def _():
                self.half(slot, 2, 0).wait_recv()
                self.half(slot, 2, 1).wait_recv()

    def drain(self):
        at = self.at
        pl.when(at.has_right)(lambda: self.copy(at.s, 0, True).wait_send())
        pl.when(at.has_left)(lambda: self.copy(at.s, 1, True).wait_send())
        self.copy(at.s, 2, True).wait_send()
        for k in range(1, at.m):
            for way in (0, 1):
                slot = at.s - 2 * k if way == 0 else at.s + 2 * k
                there = at.o - k >= 0 if way == 0 else at.o + k < at.m
                on = at.has_right if way == 0 else at.has_left

                @pl.when(there)
                def _(slot=slot, on=on, way=way):
                    pl.when(on)(lambda: self.copy(slot, way).wait_send())
                    self.to_pair(slot, lambda c: c.wait_send())

        if at.balanced:
            self.extra_copies(lambda c: c.wait_send())


def gather_events(groups):
    m = groups[0].at.m
    events = [groups[0].own]
    for g, group in enumerate(groups):
        for k in range(1, m):
            if k == max(1, m - 1) and g + 1 < len(groups):
                events.append(groups[g + 1].own)
            events.append(functools.partial(group.step, k))
            if k == 1 and g:
                events.append(groups[g - 1].extra)
    events.append(groups[-1].extra)
    return events


def add_rows(total, part, start, rows):
    step = next(size for size in (64, 32, 16, 8) if rows % size == 0)

    @pl.loop(0, rows // step)
    def _(j):
        at = pl.ds(pl.multiple_of(start + j * step, 8), step)
        both = total[at, :].astype(jnp.float32) + part[at, :].astype(jnp.float32)
        total[at, :] = both.astype(total.dtype)


class Scatter:
    def __init__(self, at, parts, out, landing, bufs, sems):
        self.at, self.parts, self.out = at, parts, out
        self.from_pair, self.from_line, self.shifted_in = landing
        self.mine, self.aside, self.stage = bufs
        (
            self.pair_send,
            self.pair_recv,
            self.line_send,
            self.line_recv,
            self.extra_send,
            self.extra_recv,
            self.local,
        ) = sems
        self.rows = self.mine.shape[1]

    @staticmethod
    def landing(n, shape, dtype):
        m = n // 2
        return [jax.ShapeDtypeStruct((size,) + shape, dtype) for size in (m, m + 1, 1)]

    @staticmethod
    def scratch(n, shape, dtype):
        m = n // 2
        return [pltpu.VMEM((size,) + shape, dtype) for size in (m, 1)] + [
            pltpu.SemaphoreType.DMA((m,)),
            pltpu.SemaphoreType.DMA((m,)),
            pltpu.SemaphoreType.DMA((m,)),
            pltpu.SemaphoreType.DMA((m + 1,)),
            pltpu.SemaphoreType.DMA((2,)),
            pltpu.SemaphoreType.DMA((2,)),
            pltpu.SemaphoreType.DMA((m + 4,)),
        ]

    def load(self, layer):
        return pltpu.make_async_copy(
            self.parts.at[layer * 2 + self.at.i], self.mine.at[layer], self.local.at[layer]
        )

    def load_aside(self):
        at = self.at
        return pltpu.make_async_copy(
            self.parts.at[at.o * 2 + 1 - at.i], self.aside.at[0], self.local.at[at.m]
        )

    def store(self):
        at = self.at
        return pltpu.make_async_copy(self.mine.at[at.o], self.out, self.local.at[at.m + 1])

    def to_stage(self, src, which, start=0, rows=None):
        part = pl.ds(start, self.rows if rows is None else rows)
        return pltpu.make_async_copy(
            src.at[part], self.stage.at[which, part], self.local.at[self.at.m + 2 + which]
        )

    def to_pair(self, layer):
        return remote(
            self.parts.at[layer * 2 + 1 - self.at.i],
            self.from_pair.at[layer],
            self.pair_send.at[layer],
            self.pair_recv.at[layer],
            self.at.pair,
        )

    def half_to_pair(self, layer, which, src):
        half = self.rows // 2
        part = pl.ds(which * half, half)
        return remote(
            src.at[part],
            self.from_pair.at[layer, part],
            self.pair_send.at[layer] if which == 0 else self.extra_send.at[1],
            self.pair_recv.at[layer] if which == 0 else self.extra_recv.at[1],
            self.at.pair,
        )

    def sum_to_pair(self):
        return remote(
            self.aside.at[0],
            self.from_pair.at[self.at.o],
            self.pair_send.at[self.at.o],
            self.pair_recv.at[self.at.o],
            self.at.pair,
        )

    def along(self, layer, way):
        at = self.at
        there = layer if way == 0 else jnp.where(layer == at.o - 1, at.m, layer)
        return remote(
            self.mine.at[layer],
            self.from_line.at[there],
            self.line_send.at[layer],
            self.line_recv.at[there],
            (at.right, at.left)[way],
        )

    def wait_line(self, place):
        remote(
            self.mine.at[0],
            self.from_line.at[place],
            self.line_send.at[0],
            self.line_recv.at[place],
            self.at.right,
        ).wait_recv()

    def shifted(self, way, which=None):
        at, half = self.at, self.rows // 2
        src, dst = self.parts.at[at.partner * 2 + 1 - at.i], self.shifted_in.at[0]
        if which is not None:
            src, dst = src.at[pl.ds(half, half)], dst.at[pl.ds(half, half)]
        return remote(
            src, dst, self.extra_send.at[0], self.extra_recv.at[0], (at.right, at.left)[way]
        )

    def far_first(self):
        at = self.at
        for d in range(at.m - 1, 0, -1):
            yield at.o + d, at.o + d < at.m
            yield at.o - d, at.o - d >= 0

    def pair_copies(self, act):
        at = self.at
        for layer, there in self.far_first():
            if not at.balanced:
                pl.when(there)(lambda: act(self.to_pair(layer)))
                continue
            partner = layer == at.partner
            pl.when(there & jnp.logical_not(partner & (at.end | at.next)))(
                lambda: act(self.to_pair(layer))
            )
            pl.when(there & partner & at.end)(
                lambda: act(self.half_to_pair(layer, 0, self.parts.at[layer * 2 + 1 - at.i]))
            )
        if not at.balanced:
            act(self.to_pair(at.o))
            return
        pl.when(jnp.logical_not(at.end | at.next))(lambda: act(self.to_pair(at.o)))
        pl.when(at.next)(
            lambda: act(self.half_to_pair(at.o, 0, self.parts.at[at.o * 2 + 1 - at.i]))
        )

    def shift_copies(self, act):
        at = self.at
        if at.balanced:
            pl.when(at.o == 0)(lambda: act(self.shifted(0, 1)))
            pl.when(at.o == at.m - 1)(lambda: act(self.shifted(1, 1)))
            pl.when(at.o == 1)(lambda: act(self.shifted(1)))
            pl.when(at.o == at.m - 2)(lambda: act(self.shifted(0)))

    def start(self):
        at = self.at
        self.shift_copies(lambda c: c.start())
        self.pair_copies(lambda c: c.start())
        for layer in range(at.m):
            self.load(layer).start()
        if at.balanced:
            self.load_aside().start()

    def extra(self):
        at = self.at
        if not at.balanced:
            return
        self.load_aside().wait()
        half, landed = self.rows // 2, self.shifted_in.at[0]

        @pl.when(at.end)
        def _():
            self.shifted(0).wait_recv()
            self.to_stage(landed, 0).start()
            self.to_stage(landed, 0).wait()
            add_rows(self.aside.at[0], self.stage.at[0], 0, self.rows)
            self.sum_to_pair().start()

        @pl.when(at.next)
        def _():
            self.shifted(0, 1).wait_recv()
            self.to_stage(landed, 0, half, half).start()
            self.to_stage(landed, 0, half, half).wait()
            add_rows(self.aside.at[0], self.stage.at[0], half, half)
            self.half_to_pair(at.o, 1, self.aside.at[0]).start()

    def wait_pair(self, layer):
        at = self.at
        if not at.balanced:
            self.to_pair(layer).wait_recv()
            return
        partner, own = layer == at.partner, layer == at.o
        parted = (partner & at.end) | (own & at.next)
        pl.when(jnp.logical_not((partner & (at.end | at.next)) | (own & at.next)))(
            lambda: self.to_pair(layer).wait_recv()
        )
        pl.when(parted)(lambda: self.half_to_pair(layer, 0, self.aside.at[0]).wait_recv())
        pl.when(own & at.next)(lambda: self.half_to_pair(layer, 1, self.aside.at[0]).wait_recv())

    def step(self, d):
        at = self.at
        for way in (0, 1):
            layer = at.o + d if way == 0 else at.o - d
            there = layer < at.m if way == 0 else layer >= 0
            behind = at.has_left if way == 0 else at.has_right

            @pl.when(there)
            def _(layer=layer, behind=behind, way=way):
                mine, paired, half = self.mine.at[layer], self.from_pair.at[layer], self.rows // 2
                self.load(layer).wait()
                self.wait_pair(layer)
                partner = (layer == at.partner) & at.balanced
                whole = jnp.logical_not(partner & (at.end | at.next))
                halved = partner & at.end
                pl.when(whole)(lambda: self.to_stage(paired, 0).start())
                pl.when(halved)(lambda: self.to_stage(paired, 0, 0, half).start())

                @pl.when(behind)
                def _():
                    self.wait_line(layer)
                    self.to_stage(self.from_line.at[layer], 1).start()

                @pl.when(whole)
                def _():
                    self.to_stage(paired, 0).wait()
                    add_rows(mine, self.stage.at[0], 0, self.rows)

                @pl.when(halved)
                def _():
                    self.to_stage(paired, 0, 0, half).wait()
                    add_rows(mine, self.stage.at[0], 0, half)

                @pl.when(behind)
                def _():
                    self.to_stage(self.from_line.at[layer], 1).wait()
                    add_rows(mine, self.stage.at[1], 0, self.rows)

                self.along(layer, way).start()

    def final(self):
        at = self.at
        mine = self.mine.at[at.o]
        self.load(at.o).wait()
        self.wait_pair(at.o)
        self.to_stage(self.from_pair.at[at.o], 0).start()

        @pl.when(at.has_left)
        def _():
            self.wait_line(at.o)
            self.to_stage(self.from_line.at[at.o], 1).start()

        self.to_stage(self.from_pair.at[at.o], 0).wait()
        add_rows(mine, self.stage.at[0], 0, self.rows)

        @pl.when(at.has_right)
        def _():
            self.wait_line(at.m)
            self.to_stage(self.from_line.at[at.m], 0).start()

        @pl.when(at.has_left)
        def _():
            self.to_stage(self.from_line.at[at.o], 1).wait()
            add_rows(mine, self.stage.at[1], 0, self.rows)

        @pl.when(at.has_right)
        def _():
            self.to_stage(self.from_line.at[at.m], 0).wait()
            add_rows(mine, self.stage.at[0], 0, self.rows)

        self.store().start()

    def drain(self):
        at = self.at
        self.pair_copies(lambda c: c.wait_send())
        if at.balanced:
            pl.when(at.end)(lambda: self.sum_to_pair().wait_send())
            pl.when(at.next)(lambda: self.half_to_pair(at.o, 1, self.aside.at[0]).wait_send())
        self.shift_copies(lambda c: c.wait_send())
        for d in range(1, at.m):
            pl.when(at.o + d < at.m)(lambda: self.along(at.o + d, 0).wait_send())
            pl.when(at.o - d >= 0)(lambda: self.along(at.o - d, 1).wait_send())
        self.store().wait()


def fetch(src, dst, sem):
    return pltpu.make_async_copy(src, dst, sem)


def dot(a, b, dims=((1,), (0,))):
    return lax.dot_general(a, b, (dims, ((), ())), preferred_element_type=jnp.float32)


ROWS, COLS, BOTH = ((1,), (0,)), ((1,), (1,)), ((0,), (0,))


def row_start(lengths, position):
    at, start = jnp.int32(0), jnp.zeros_like(position)
    for k in range(lengths.shape[0]):
        start = jnp.maximum(start, jnp.where(at <= position, at, 0))
        at = at + lengths[k]
    return start


def lanes(shape):
    return lax.broadcasted_iota(jnp.int32, shape, len(shape) - 1)


def feature_maps(width):
    count = FEAT + 1 + FEAT * (FEAT + 1) // 2
    wide = -(-count // 128) * 128
    first, second = np.zeros((width, wide), np.float32), np.zeros((width, wide), np.float32)
    plus = np.zeros((3, wide), np.float32)
    plus[:, 0] = 1.0
    heads = np.arange(width // FEAT) * FEAT
    for i in range(FEAT):
        first[heads + i, 1 + i] = 1.0
        plus[1:, 1 + i] = 1.0, 0.25
    at = 1 + FEAT
    for i in range(FEAT):
        for j in range(i, FEAT):
            first[heads + i, at] = 1.0
            second[heads + j, at] = 1.0
            plus[2, at] = 1 / 32 if i == j else 1 / 16
            at += 1
    tall = -(-count // 16) * 16
    return (
        jnp.asarray(np.stack([first, second]), jnp.bfloat16),
        jnp.asarray(np.stack([first.T, second.T])[:, :tall], jnp.bfloat16),
        jnp.asarray(np.repeat(plus[:, None], 8, 1)),
        jnp.asarray(np.repeat(plus[:, :tall, None], 128, 2)),
    )


class Team:
    def __init__(self, at, rows):
        self.at, self.half, self.quarter = at, rows // 2, rows // 4
        t = at.t
        low, high = lax.rem(t, 2), t // 2
        self.near, self.far = (at.s, t + 1 - 2 * low), (at.s, lax.rem(t + 2, 4))
        self.half_at, self.other_half_at = low * self.half, (1 - low) * self.half
        self.quarter_at = self.half_at + high * self.quarter
        self.other_quarter_at = self.half_at + (1 - high) * self.quarter
        self.in_half, self.other_in_half = high * self.quarter, (1 - high) * self.quarter
        self.near_quarter_at = self.other_half_at + high * self.quarter
        self.near_other_at = self.other_half_at + (1 - high) * self.quarter


class Sum:
    pieces = 4

    def __init__(self, team, part, from_near, from_far, sems):
        self.team, self.part, self.from_near, self.from_far = team, part, from_near, from_far
        self.near_send, self.near_recv, self.far_send, self.far_recv = sems
        self.wide = part.shape[1] // self.pieces

    @staticmethod
    def scratch(rows, columns):
        return [
            pltpu.VMEM((rows // 2, columns), jnp.bfloat16),
            pltpu.VMEM((rows // 4, columns), jnp.bfloat16),
        ] + [pltpu.SemaphoreType.DMA((Sum.pieces,))] * 4

    def near(self, j):
        team, columns = self.team, pl.ds(j * self.wide, self.wide)
        return remote(
            self.part.at[pl.ds(pl.multiple_of(team.other_half_at, team.half), team.half), columns],
            self.from_near.at[:, columns],
            self.near_send.at[j],
            self.near_recv.at[j],
            team.near,
        )

    def far(self, j):
        team, columns = self.team, pl.ds(j * self.wide, self.wide)
        at = pl.multiple_of(team.other_quarter_at, team.quarter)
        return remote(
            self.part.at[pl.ds(at, team.quarter), columns],
            self.from_far.at[:, columns],
            self.far_send.at[j],
            self.far_recv.at[j],
            team.far,
        )

    def fold(self, j):
        team, columns = self.team, pl.ds(j * self.wide, self.wide)
        self.near(j).wait_recv()
        step = 64

        @pl.loop(0, team.quarter // step)
        def _(r):
            to = pl.ds(pl.multiple_of(team.other_quarter_at + r * step, step), step)
            of = pl.ds(pl.multiple_of(team.other_in_half + r * step, step), step)
            both = self.part[to, columns].astype(jnp.float32)
            both = both + self.from_near[of, columns].astype(jnp.float32)
            self.part[to, columns] = both.astype(jnp.bfloat16)

        self.far(j).start()

    def arrive(self):
        for j in range(self.pieces):
            self.far(j).wait_recv()

    def rows(self, start, count):
        team = self.team
        a = self.part[pl.ds(pl.multiple_of(team.quarter_at + start, 16), count), :]
        b = self.from_near[pl.ds(pl.multiple_of(team.in_half + start, 16), count), :]
        c = self.from_far[pl.ds(pl.multiple_of(start, 16), count), :]
        return a.astype(jnp.float32) + b.astype(jnp.float32) + c.astype(jnp.float32)

    def drain(self):
        for j in range(self.pieces):
            self.near(j).wait_send()
            self.far(j).wait_send()


class Spread:
    pieces = 4

    def __init__(self, team, whole, sems):
        self.team, self.whole = team, whole
        self.far_send, self.far_recv, self.near_send, self.near_recv, self.on_send, self.on_recv = (
            sems
        )
        self.tall = team.quarter // self.pieces

    @staticmethod
    def scratch():
        return [pltpu.SemaphoreType.DMA((Spread.pieces,))] * 6

    def copy(self, start, j, send, recv, device):
        rows = self.whole.at[pl.ds(pl.multiple_of(start + j * self.tall, self.tall), self.tall)]
        return remote(rows, rows, send.at[j], recv.at[j], device)

    def far(self, j):
        team = self.team
        return self.copy(team.quarter_at, j, self.far_send, self.far_recv, team.far)

    def near(self, j):
        team = self.team
        return self.copy(team.quarter_at, j, self.near_send, self.near_recv, team.near)

    def on(self, j):
        team = self.team
        return self.copy(team.other_quarter_at, j, self.on_send, self.on_recv, team.near)

    def send(self, j):
        self.far(j).start()
        self.near(j).start()

    def pass_on(self, j):
        self.far(j).wait_recv()
        self.on(j).start()

    def arrive(self):
        for j in range(self.pieces):
            self.near(j).wait_recv()
            self.on(j).wait_recv()

    def drain(self):
        for j in range(self.pieces):
            self.far(j).wait_send()
            self.near(j).wait_send()
            self.on(j).wait_send()


class Pump:
    def __init__(self, events):
        self.events = list(events)

    def __call__(self, count):
        for _ in range(min(count, len(self.events))):
            self.events.pop(0)()

    def until(self, event):
        while event in self.events:
            self.events.pop(0)()

    def rest(self):
        self(len(self.events))


def gain_row(gains, which, row):
    n, depth = gains.shape[0], gains.shape[2] // 2
    for s in range(n):
        part = gains[s, 0:8, which * depth : (which + 1) * depth]
        row[:, s * depth : (s + 1) * depth] = part


def scores(query, key, mask):
    s = dot(query, key, COLS) * 0.25
    return 1.0 + s, jnp.where(mask, 1.0 + s + 0.5 * s * s, 0.0)


def pair_mask(row_starts, column_starts, first_row, first_column):
    shape = (row_starts.shape[0], column_starts.shape[1])
    rows = lax.broadcasted_iota(jnp.int32, shape, 0) + first_row
    columns = lax.broadcasted_iota(jnp.int32, shape, 1) + first_column
    return (row_starts == column_starts) & (columns <= rows)


def of_head(values, h):
    lane = lanes((1, values.shape[1]))
    mine = (lane >= h * FEAT) & (lane < (h + 1) * FEAT)
    return jnp.where(mine, values, jnp.zeros_like(values))


def with_ones(values):
    return jnp.concatenate([values, jnp.ones_like(values)], axis=1)


def forward_kernel(n, sizes, *refs):
    (
        lengths, stream_h, cot_h, maps, maps_t, plus, plus_t,
        gains_own, qkv_own, out_own, gate_own, up_own, down_own,
        gains_h, qkv_h, out_h, gate_h, up_h, down_h,
        h_one_h, heads_h, mixed_h, rden_h, state_h, mid_h, h_two_h, gate_v_h, up_v_h, hid_h, part_h,
        stream, h_one, heads, w_qkv, w_out, mixed, rden, numer, mid, h_two, w_ff,
        gate_v, up_v, hid, part, gains, gain,
        t_own, t_pair, t_line, t_next, state, t_send, t_recv, local, part_sem,
        *sems,
    ) = refs
    rows, width = stream.shape
    heads_here = mixed.shape[1] // 128
    q_wide = heads_here * FEAT
    at = Place(n)
    team = Team(at, rows)
    near_sum, sems = sems[:6], sems[6:]
    spread_sems, sems = sems[:6], sems[6:]
    shards = (gains_own, qkv_own, out_own, gate_own, up_own, down_own)
    wholes = (gains_h, qkv_h, out_h, gate_h, up_h, down_h)
    groups = [
        Gather(at, shards[g], wholes[g], sems[4 * g : 4 * g + 4]) for g in range(len(shards))
    ]
    g_gains, g_qkv, g_out, g_gate, g_up, g_down = groups
    at.greet((team.near, team.far))
    pump = Pump(gather_events(groups))
    cell = iter(range(local.shape[0]))
    copies = []

    def load(src, dst):
        copy = fetch(src, dst, local.at[next(cell)])
        copy.start()
        return copy

    def save(src, dst):
        copies.append(load(src, dst))

    get_stream = load(stream_h, stream)
    pump.until(g_gains.extra)
    g_gains.arrive()
    load(gains_h, gains).wait()
    gain_row(gains, 0, gain.at[0])
    gain_row(gains, 1, gain.at[1])
    get_stream.wait()

    @pl.loop(0, rows // 64)
    def _(j):
        here = pl.ds(pl.multiple_of(j * 64, 64), 64)
        x = stream[here, :].astype(jnp.float32)
        scale = lax.rsqrt(jnp.mean(x * x, axis=1, keepdims=True) + EPSILON)
        h_one[here, :] = (x * scale * gain[0, 0:1, :]).astype(jnp.bfloat16)

    save(h_one, h_one_h)
    pump.until(g_qkv.extra)
    g_qkv.arrive()
    load(qkv_h, w_qkv).wait()

    @pl.loop(0, rows // 256)
    def _(j):
        here = pl.ds(pl.multiple_of(j * 256, 256), 256)
        heads[here, :] = dot(h_one[here, :], w_qkv[...]).astype(jnp.bfloat16)

    save(heads, heads_h)
    pump(1)
    first = at.s * rows
    starts_col = row_start(lengths, first + lax.broadcasted_iota(jnp.int32, (rows, 1), 0))
    starts_row = row_start(lengths, first + lax.broadcasted_iota(jnp.int32, (1, rows), 1))
    last = row_start(lengths, first + rows - 1)
    keep = jnp.where(starts_row == last, 1.0, 0.0)
    tall = t_own.shape[1]

    def values_of(h):
        return pl.ds(pl.multiple_of(2 * q_wide + h * 128, 128), 128)

    t_sum = numer.at[0, 0:tall, 0:128]
    t_sum[...] = jnp.zeros((tall, 128), jnp.float32)

    @pl.loop(0, heads_here)
    def _(h):
        key = of_head(heads[:, q_wide : 2 * q_wide], h)
        one = dot(maps_t[0], key, COLS) + plus_t[0][:, 0:1]
        two = dot(maps_t[1], key, COLS) + plus_t[1][:, 0:1]
        phi = (one * two * keep).astype(jnp.bfloat16)
        total = dot(phi, with_ones(heads[:, values_of(h)]))
        t_own[h] = total[:, :128].astype(jnp.bfloat16)
        t_sum[...] += jnp.where(lanes((tall, 128)) == h, total[:, 128:], 0.0)

    t_own[heads_here] = t_sum[...].astype(jnp.bfloat16)
    to_pair = remote(t_own, t_pair, t_send.at[0], t_recv.at[0], at.pair)
    to_right = remote(t_next, t_line, t_send.at[1], t_recv.at[1], at.right)
    to_pair.start()
    pump(1)
    tile = 256

    @pl.loop(0, heads_here)
    def _(h):
        key = heads[:, q_wide : 2 * q_wide]
        for j in range(rows // tile):
            upto = (j + 1) * tile
            query = of_head(heads[j * tile : upto, 0:q_wide], h)
            mask = pair_mask(starts_col[j * tile : upto], starts_row[:, :upto], j * tile, 0)
            _, weights = scores(query, key[:upto], mask)
            values = with_ones(heads[0:upto, values_of(h)])
            numer[h, j * tile : upto, :] = dot(weights.astype(jnp.bfloat16), values)

    pump(1)

    def closed(s):
        return jnp.where(row_start(lengths, (s + 1) * rows - 1) >= s * rows, 0.0, 1.0)

    on_one, on_two = closed(at.o * 2), closed(at.o * 2 + 1)

    @pl.when(at.o == 0)
    def _():
        t_line[...] = jnp.zeros_like(t_line)

    to_pair.wait_recv()
    pl.when(at.has_left)(lambda: to_right.wait_recv())
    for h in range(heads_here + 1):
        mine, other = t_own[h].astype(jnp.float32), t_pair[h].astype(jnp.float32)
        t_one, t_two = jnp.where(at.i == 0, mine, other), jnp.where(at.i == 0, other, mine)
        come = t_line[h].astype(jnp.float32)
        middle = t_one + on_one * come
        t_next[h] = (t_two + on_two * middle).astype(jnp.bfloat16)
        state[h] = jnp.where(at.i == 0, come, middle).astype(jnp.bfloat16)
    pl.when(at.has_right)(lambda: to_right.start())
    save(state, state_h)
    pump(1)

    @pl.loop(0, heads_here)
    def _(h):
        own = lanes((tall, 128)) == h
        dens = jnp.sum(jnp.where(own, state[heads_here].astype(jnp.float32), 0.0), 1, keepdims=True)
        dens = jnp.broadcast_to(dens, (tall, 128)).astype(jnp.bfloat16)
        table = jnp.concatenate([state[h], dens], axis=1)
        table = jnp.concatenate(
            [table, jnp.zeros((maps.shape[2] - tall, 256), jnp.bfloat16)], axis=0
        )
        for j in range(rows // tile):
            here = slice(j * tile, (j + 1) * tile)
            query = of_head(heads[here, 0:q_wide], h)
            one = dot(query, maps[0]) + plus[0, 0:1, :]
            two = dot(query, maps[1]) + plus[1, 0:1, :]
            carried = jnp.where(starts_col[here] < first, 1.0, 0.0)
            phi = (one * two * plus[2, 0:1, :] * carried).astype(jnp.bfloat16)
            total = numer[h, here, :] + dot(phi, table)
            inverse = 1.0 / total[:, 128:]
            rden[h, here, :] = inverse
            mixed[here, pl.ds(pl.multiple_of(h * 128, 128), 128)] = (
                total[:, :128] * inverse
            ).astype(jnp.bfloat16)

    save(mixed, mixed_h)
    save(rden, rden_h)
    pump.until(g_out.extra)
    g_out.arrive()
    load(out_h, w_out).wait()
    for copy in copies:
        copy.wait()
    copies.clear()

    part_sum = Sum(team, h_one, *near_sum[:2], near_sum[2:])
    for j in range(Sum.pieces):
        columns = slice(j * part_sum.wide, (j + 1) * part_sum.wide)

        @pl.loop(0, rows // 256)
        def _(r):
            here = pl.ds(pl.multiple_of(r * 256, 256), 256)
            h_one[here, columns] = dot(mixed[here, :], w_out[columns, :], COLS).astype(jnp.bfloat16)

        part_sum.near(j).start()
        if j:
            part_sum.fold(j - 1)
            pump(1)
    part_sum.fold(Sum.pieces - 1)
    pump(1)
    part_sum.arrive()
    spread = Spread(team, h_two, spread_sems)
    for j in range(Spread.pieces):
        for k in range(spread.tall // 32):
            down = j * spread.tall + k * 32
            here = pl.ds(pl.multiple_of(team.quarter_at + down, 32), 32)
            x = part_sum.rows(down, 32) + stream[here, :].astype(jnp.float32)
            mid[down : down + 32, :] = x
            scale = lax.rsqrt(jnp.mean(x * x, axis=1, keepdims=True) + EPSILON)
            h_two[here, :] = (x * scale * gain[1, 0:1, :]).astype(jnp.bfloat16)
        spread.send(j)
    save(mid, mid_h)
    for j in range(Spread.pieces):
        pump(1)
        spread.pass_on(j)
    get_cot = load(cot_h, stream)
    spread.arrive()
    part_sum.drain()
    spread.drain()
    save(h_two, h_two_h)
    pump.until(g_gate.extra)
    g_gate.arrive()
    get_gate = load(gate_h, w_ff.at[0])
    pump.until(g_up.extra)
    g_up.arrive()
    load(up_h, w_ff.at[1]).wait()
    get_gate.wait()
    stages = 4
    for stage in range(stages):

        @pl.loop(0, rows // 128 // stages)
        def _(r):
            start = pl.multiple_of((stage * (rows // 128 // stages) + r) * 128, 128)
            here = pl.ds(start, 128)
            gate = dot(h_two[here, :], w_ff[0])
            up = dot(h_two[here, :], w_ff[1])
            hidden = gate * jax.nn.sigmoid(gate) * up
            gate_v[here, :] = gate.astype(jnp.bfloat16)
            up_v[here, :] = up.astype(jnp.bfloat16)
            hid[here, :] = hidden.astype(jnp.bfloat16)

        pump(1)
    save(gate_v, gate_v_h)
    save(up_v, up_v_h)
    save(hid, hid_h)
    get_cot.wait()
    deep = part.shape[1]
    for s in range(n):
        if s > 1:
            fetch(part.at[s % 2], part_h.at[s - 2], part_sem.at[s % 2]).wait()
        columns = stream[:, s * deep : (s + 1) * deep]
        for low in range(0, hid.shape[1], 512):
            high = min(hid.shape[1], low + 512)
            part[s % 2, :, low:high] = dot(columns, hid[:, low:high], BOTH).astype(jnp.bfloat16)
        fetch(part.at[s % 2], part_h.at[s], part_sem.at[s % 2]).start()
        if s % max(1, n // 4) == 0:
            pump(1)
    for s in range(n - 2, n):
        fetch(part.at[s % 2], part_h.at[s], part_sem.at[s % 2]).wait()
    pump.rest()
    g_down.arrive()
    for group in groups:
        group.drain()
    to_pair.wait_send()
    pl.when(at.has_right)(lambda: to_right.wait_send())
    for copy in copies:
        copy.wait()


def forward(n, lengths, stream, cot, maps, shards):
    rows, width = stream.shape
    gains, qkv, out, gate, up, down = shards
    hidden = gate.shape[1]
    values = out.shape[1]
    heads_here = values // 128
    tall = maps[1].shape[1]
    bf, f32 = jnp.bfloat16, jnp.float32
    shape = jax.ShapeDtypeStruct
    wholes = [
        shape((n,) + gains.shape, f32),
        shape((n * qkv.shape[0], qkv.shape[1]), bf),
        shape((width, values), bf),
        shape((width, hidden), bf),
        shape((width, hidden), bf),
        shape((width, hidden), bf),
    ]
    kept = [
        shape((rows, width), bf),
        shape((rows, qkv.shape[1]), bf),
        shape((rows, values), bf),
        shape((heads_here, rows, 128), f32),
        shape((heads_here + 1, tall, 128), bf),
        shape((rows // 4, width), f32),
        shape((rows, width), bf),
        shape((rows, hidden), bf),
        shape((rows, hidden), bf),
        shape((rows, hidden), bf),
        shape((n,) + down.shape, bf),
    ]
    state = (heads_here + 1, tall, 128)
    scratch = [
        pltpu.VMEM((rows, width), bf),
        pltpu.VMEM((rows, width), bf),
        pltpu.VMEM((rows, qkv.shape[1]), bf),
        pltpu.VMEM((width, qkv.shape[1]), bf),
        pltpu.VMEM((width, values), bf),
        pltpu.VMEM((rows, values), bf),
        pltpu.VMEM((heads_here, rows, 128), f32),
        pltpu.VMEM((heads_here, rows, 256), f32),
        pltpu.VMEM((rows // 4, width), f32),
        pltpu.VMEM((rows, width), bf),
        pltpu.VMEM((2, width, hidden), bf),
        pltpu.VMEM((rows, hidden), bf),
        pltpu.VMEM((rows, hidden), bf),
        pltpu.VMEM((rows, hidden), bf),
        pltpu.VMEM((2,) + down.shape, bf),
        pltpu.VMEM((n,) + gains.shape, f32),
        pltpu.VMEM((2, 8, width), f32),
        pltpu.VMEM(state, bf),
        pltpu.VMEM(state, bf),
        pltpu.VMEM(state, bf),
        pltpu.VMEM(state, bf),
        pltpu.VMEM(state, bf),
        pltpu.SemaphoreType.DMA((2,)),
        pltpu.SemaphoreType.DMA((2,)),
        pltpu.SemaphoreType.DMA((24,)),
        pltpu.SemaphoreType.DMA((2,)),
    ]
    scratch += Sum.scratch(rows, width) + Spread.scratch() + Gather.scratch(n) * len(shards)
    anywhere, inside = pl.BlockSpec(memory_space=pl.ANY), pl.BlockSpec(memory_space=pltpu.VMEM)
    result = pl.pallas_call(
        functools.partial(forward_kernel, n, None),
        out_shape=wholes + kept,
        in_specs=[pl.BlockSpec(memory_space=pltpu.SMEM), anywhere, anywhere]
        + [inside] * 4
        + [anywhere] * 6,
        out_specs=[anywhere] * (len(wholes) + len(kept)),
        scratch_shapes=scratch,
        compiler_params=pltpu.CompilerParams(
            collective_id=0, has_side_effects=True, vmem_limit_bytes=62 * MIB
        ),
    )(lengths, stream, cot, *maps, *shards)
    return result[: len(wholes)], result[len(wholes) :]


class SpreadOut(Spread):
    def __init__(self, team, quarter, whole, sems):
        super().__init__(team, whole, sems[:-1])
        self.own, self.kept = quarter, sems[-1]

    @staticmethod
    def scratch():
        return Spread.scratch() + [pltpu.SemaphoreType.DMA((1,))]

    def own_copy(self, j, send, recv, device):
        start = self.team.quarter_at + j * self.tall
        rows = self.whole.at[pl.ds(pl.multiple_of(start, self.tall), self.tall)]
        src = self.own.at[pl.ds(j * self.tall, self.tall)]
        return remote(src, rows, send.at[j], recv.at[j], device)

    def far(self, j):
        return self.own_copy(j, self.far_send, self.far_recv, self.team.far)

    def near(self, j):
        return self.own_copy(j, self.near_send, self.near_recv, self.team.near)

    def keep(self):
        team = self.team
        rows = self.whole.at[pl.ds(pl.multiple_of(team.quarter_at, team.quarter), team.quarter)]
        return pltpu.make_async_copy(self.own, rows, self.kept.at[0])


def backward_kernel(n, *refs):
    (
        lengths, maps, maps_t, plus, plus_t,
        stream_h, cot_h, gains_h, qkv_h, out_h, gate_h, up_h, down_h,
        h_one_h, heads_h, mixed_h, rden_h, state_h, mid_h, h_two_h, gate_v_h, up_v_h, hid_h, part_h,
        *refs,
    ) = refs
    act_h, ig_h, *refs = refs
    outs, refs = refs[:6], refs[6:]
    parts, refs = [part_h] + refs[:5], refs[5:]
    landings, refs = refs[:18], refs[18:]
    (
        part, arena, d_mid, dm, gains, gain, gain_sum, gain_near, gain_far, gain_parts,
        t_own, t_pair, t_line, t_next, state, back, t_send, t_recv, gain_send, gain_recv, local,
        stage_g, stage_o, stage_q, stage_n,
        *sems,
    ) = refs
    rows, width = arena.shape
    hidden = gate_v_h.shape[1]
    values_wide = mixed_h.shape[1]
    heads_here = values_wide // 128
    q_wide = heads_here * FEAT
    at = Place(n)
    team = Team(at, rows)

    def take(count):
        nonlocal sems
        taken, sems = sems[:count], sems[count:]
        return taken

    sums = [take(6) for _ in range(2)]
    first_sems = take(4)
    dm_sems, act_sems, ig_sems = take(6), take(7), take(7)
    stages = (stage_g, stage_g, stage_g, stage_o, stage_q, stage_n)
    groups = []
    for g in range(6):
        mine, aside, *own_sems = take(9)
        groups.append(
            Scatter(
                at,
                parts[g],
                outs[g],
                landings[3 * g : 3 * g + 3],
                (mine, aside, stages[g]),
                own_sems,
            )
        )
    s_down, s_gate, s_up, s_out, s_qkv, s_gains = groups
    at.greet((team.near, team.far))
    cell = iter(range(local.shape[0]))

    def load(src, dst):
        copy = fetch(src, dst, local.at[next(cell)])
        copy.start()
        return copy

    pump = Pump([])
    begun = []

    def begin(group):
        group.start()
        last = begun[-1] if begun else None
        begun.append(group)
        for d in range(at.m - 1, 0, -1):
            pump.events.append(functools.partial(group.step, d))
            if d == max(1, at.m - 2) and last is not None:
                pump.events.append(last.final)
        pump.events.append(group.extra)

    begin(s_down)
    get_gains = load(gains_h, gains)
    get_mid = load(mid_h, d_mid)
    part_sum = Sum(team, part, *sums[0][:2], sums[0][2:])
    feed_sum = Sum(team, part, *sums[1][:2], sums[1][2:])
    first_sum = Sum(team, part, *sums[0][:2], first_sems)
    spread = Spread(team, dm, dm_sems)
    ig_rows, act_rows = team.quarter, 2 * team.quarter
    ig_spread = SpreadOut(team, arena.at[pl.ds(ig_rows, team.quarter)], ig_h, ig_sems)
    act_spread = SpreadOut(team, arena.at[pl.ds(act_rows, team.quarter)], act_h, act_sems)
    piece = part_sum.wide

    def staged(count, sem, tile, parts_h, compute, between):
        for s in range(count):
            if s > 1:
                fetch(tile.at[s % 2], parts_h.at[s - 2], sem.at[s % 2]).wait()
            compute(s, tile.at[s % 2])
            fetch(tile.at[s % 2], parts_h.at[s], sem.at[s % 2]).start()
            between(s)
        for s in range(count - 2, count):
            fetch(tile.at[s % 2], parts_h.at[s], sem.at[s % 2]).wait()

    def now_and_then(s):
        if s % max(1, n // 4) == n // 4 - 1:
            pump(1)

    def norm_back(x, grad, gain_ref, which):
        scale = lax.rsqrt(jnp.mean(x * x, axis=1, keepdims=True) + EPSILON)
        unit = x * scale
        total = jnp.sum((grad * unit).reshape(-1, 8, width), axis=0)
        gain_sum[8 * which : 8 * which + 8, :] += total
        scaled = grad * gain_ref[0:1, :]
        return scale * (scaled - unit * jnp.mean(scaled * unit, axis=1, keepdims=True))

    gain_sum[...] = jnp.zeros_like(gain_sum)

    def feed_forward(w_down, w_ff, ff, w_sem, tile_sem):
        get_cot, get_down = load(cot_h, arena), load(down_h, w_down)
        get_gate, get_up = load(gate_v_h, ff.at[0]), load(up_v_h, ff.at[1])
        tall = w_ff.shape[2]

        def weights(j, which):
            here = pl.ds(j * tall, tall)
            return fetch(
                (gate_h, up_h)[which].at[here], w_ff.at[j % 2, which], w_sem.at[j % 2, which]
            )

        for which in (0, 1):
            weights(0, which).start()
        get_cot.wait()
        get_down.wait()
        get_gate.wait()
        get_up.wait()
        block = 256
        for low in range(0, hidden, 512):
            high = min(hidden, low + 512)

            @pl.loop(0, rows // block)
            def _(r):
                here = pl.ds(pl.multiple_of(r * block, block), block)
                grad = dot(arena[here, :], w_down[:, low:high])
                gate = ff[0, here, low:high].astype(jnp.float32)
                sigma = jax.nn.sigmoid(gate)
                silu = gate * sigma
                up = ff[1, here, low:high].astype(jnp.float32)
                ff[0, here, low:high] = (grad * up * (sigma + silu * (1.0 - sigma))).astype(
                    jnp.bfloat16
                )
                ff[1, here, low:high] = (grad * silu).astype(jnp.bfloat16)

            pump(1)
        get_two = load(h_two_h, arena)
        count = width // tall
        for j in range(count):
            for which in (0, 1):
                if j + 1 < count:
                    weights(j + 1, which).start()
                weights(j, which).wait()

            @pl.loop(0, rows // 256)
            def _(r):
                here = pl.ds(pl.multiple_of(r * 256, 256), 256)
                grad = dot(ff[0, here, :], w_ff[j % 2, 0], COLS)
                grad += dot(ff[1, here, :], w_ff[j % 2, 1], COLS)
                part[here, j * tall : (j + 1) * tall] = grad.astype(jnp.bfloat16)

            if (j + 1) * tall % piece == 0:
                p = (j + 1) * tall // piece - 1
                part_sum.near(p).start()
                if p:
                    part_sum.fold(p - 1)
            if j % 4 == 3:
                pump(1)
        part_sum.fold(Sum.pieces - 1)
        get_two.wait()
        pump(1)
        down = width // n
        tile = w_ff.at[0, :, 0:down]

        def grads(which):
            def compute(s, to):
                columns = arena[:, s * down : (s + 1) * down]
                for low in range(0, hidden, 512):
                    high = min(hidden, low + 512)
                    grad = dot(columns, ff[which, :, low:high], BOTH)
                    to[:, low:high] = grad.astype(jnp.bfloat16)

            return compute

        staged(n, tile_sem, tile, parts[1], grads(0), now_and_then)
        begin(s_gate)
        get_gains.wait()
        gain_row(gains, 0, gain.at[0])
        gain_row(gains, 1, gain.at[1])
        get_mid.wait()
        part_sum.arrive()
        for j in range(Spread.pieces):
            for k in range(spread.tall // 32):
                down_at = j * spread.tall + k * 32
                here = pl.ds(pl.multiple_of(team.quarter_at + down_at, 32), 32)
                x = d_mid[down_at : down_at + 32, :]
                grad = norm_back(x, part_sum.rows(down_at, 32), gain.at[1], 1)
                d_mid[down_at : down_at + 32, :] = grad
        quarter = pl.ds(pl.multiple_of(team.quarter_at, team.quarter), team.quarter)
        get = load(cot_h.at[quarter], dm.at[quarter])
        get.wait()
        for j in range(Spread.pieces):
            for k in range(spread.tall // 32):
                down_at = j * spread.tall + k * 32
                here = pl.ds(pl.multiple_of(team.quarter_at + down_at, 32), 32)
                grad = d_mid[down_at : down_at + 32, :]
                grad = grad + dm[here, :].astype(jnp.float32)
                d_mid[down_at : down_at + 32, :] = grad
                dm[here, :] = grad.astype(jnp.bfloat16)
            spread.send(j)
        part_sum.drain()
        staged(n, tile_sem, tile, parts[2], grads(1), now_and_then)
        begin(s_up)
        get_hid = load(hid_h, ff.at[0])
        get_hid.wait()
        for j in range(Sum.pieces):
            columns = slice(j * piece, (j + 1) * piece)

            @pl.loop(0, rows // 256)
            def _(r):
                here = pl.ds(pl.multiple_of(r * 256, 256), 256)
                feed = dot(ff[0, here, :], w_down[columns, :], COLS)
                part[here, columns] = feed.astype(jnp.bfloat16)

            feed_sum.near(j).start()
            spread.pass_on(j)

    pl.run_scoped(
        feed_forward,
        pltpu.VMEM(down_h.shape, jnp.bfloat16),
        pltpu.VMEM((2, 2, 256, hidden), jnp.bfloat16),
        pltpu.VMEM((2, rows, hidden), jnp.bfloat16),
        pltpu.SemaphoreType.DMA((2, 2)),
        pltpu.SemaphoreType.DMA((2,)),
    )

    def attention(
        heads, d_heads, mixed, w_out, w_qkv, delta, g, delta_row, d_query, d_key,
        dens, tile_o, tile_q, tile_sem, d_values,
    ):
        gets = [
            load(heads_h, heads),
            load(mixed_h, mixed),
            load(out_h, w_out),
            load(rden_h, delta),
            load(qkv_h, w_qkv),
            load(state_h, state),
        ]
        get_one = load(h_one_h, arena)
        for get in gets:
            get.wait()
        spread.arrive()

        @pl.loop(0, rows // 256)
        def _(r):
            here = pl.ds(pl.multiple_of(r * 256, 256), 256)
            d_values[here, :] = dot(dm[here, :], w_out[...])

        for j in range(Sum.pieces):
            feed_sum.fold(j)

        @pl.loop(0, heads_here)
        def _(h):
            across = pl.ds(pl.multiple_of(h * 128, 128), 128)
            grad = d_values[:, across] * delta[h]
            g[h] = grad.astype(jnp.bfloat16)
            sums_of = jnp.sum(grad * mixed[:, across].astype(jnp.float32), axis=1, keepdims=True)
            wide = jnp.broadcast_to(sums_of, (rows, 128))
            delta[h] = wide
            delta_row[h] = wide.T[0:8]

        pump(1)
        first = at.s * rows
        starts_col = row_start(lengths, first + lax.broadcasted_iota(jnp.int32, (rows, 1), 0))
        starts_row = row_start(lengths, first + lax.broadcasted_iota(jnp.int32, (1, rows), 1))
        last = row_start(lengths, first + rows - 1)
        tall = t_own.shape[1]
        wide = maps.shape[2]
        carried_row = jnp.where(starts_row < first, 1.0, 0.0)
        dens[1, 0:tall, 0:128] = jnp.zeros((tall, 128), jnp.float32)

        def values_of(h):
            return pl.ds(pl.multiple_of(2 * q_wide + h * 128, 128), 128)

        def head_at(h):
            return pl.ds(pl.multiple_of(h * 128, 128), 128)

        @pl.loop(0, heads_here)
        def _(h):
            query = of_head(heads[:, 0:q_wide], h)
            one = dot(maps_t[0], query, COLS) + plus_t[0][:, 0:1]
            two = dot(maps_t[1], query, COLS) + plus_t[1][:, 0:1]
            phi = one * two * plus_t[2][:, 0:1] * carried_row
            t_own[h] = dot(phi.astype(jnp.bfloat16), g[h]).astype(jnp.bfloat16)
            below = -jnp.sum(phi * delta_row[h][0:1, :], axis=1, keepdims=True)
            dens[1, 0:tall, 0:128] += jnp.where(lanes((tall, 128)) == h, below, 0.0)

        t_own[heads_here] = dens[1, 0:tall, 0:128].astype(jnp.bfloat16)
        to_pair = remote(t_own, t_pair, t_send.at[0], t_recv.at[0], at.pair)
        to_left = remote(t_next, t_line, t_send.at[1], t_recv.at[1], at.left)
        to_pair.start()
        pump(1)

        d_query[...] = jnp.zeros_like(d_query)
        tile = 128

        def intra(h):
            key, query = of_head(heads[:, q_wide : 2 * q_wide], h), of_head(heads[:, 0:q_wide], h)
            across = values_of(h)
            for j in range(rows // tile):
                here, upto = slice(j * tile, (j + 1) * tile), (j + 1) * tile
                mask = pair_mask(starts_col[here], starts_row[:, :upto], j * tile, 0)
                more, _ = scores(query[here], key[:upto], mask)
                d_weight = dot(g[h, here, :], heads[0:upto, across], COLS) - delta[h, here, 0:1]
                d_score = jnp.where(mask, d_weight * more, 0.0).astype(jnp.bfloat16)
                d_query[here, :] += dot(d_score, key[:upto]) * 0.25
            for j in range(rows // tile):
                here, after = slice(j * tile, (j + 1) * tile), j * tile
                shape = (tile, rows - after)
                key_at = lax.broadcasted_iota(jnp.int32, shape, 0)
                query_at = lax.broadcasted_iota(jnp.int32, shape, 1)
                mask = (starts_col[here] == starts_row[:, after:]) & (key_at <= query_at)
                more, weight = scores(key[here], query[after:], mask)
                d_weight = dot(heads[here, across], g[h, after:, :], COLS)
                d_weight = d_weight - delta_row[h, 0:1, after:]
                d_score = jnp.where(mask, d_weight * more, 0.0).astype(jnp.bfloat16)
                d_values[here, head_at(h)] = dot(weight.astype(jnp.bfloat16), g[h, after:, :])
                grad = dot(d_score, query[after:]) * 0.25
                d_key[here, :] = jnp.where(h == 0, grad, d_key[here, :] + grad)

        d_key[...] = jnp.zeros_like(d_key)
        per = max(1, heads_here // 2)
        for part_of in range(0, heads_here, per):

            @pl.loop(part_of, part_of + per)
            def _(h):
                intra(h)

            pump(1)

        def closed(s):
            return jnp.where(row_start(lengths, (s + 1) * rows - 1) >= s * rows, 0.0, 1.0)

        on_one, on_two = closed(at.o * 2), closed(at.o * 2 + 1)

        @pl.when(at.o == at.m - 1)
        def _():
            t_line[...] = jnp.zeros_like(t_line)

        to_pair.wait_recv()
        pl.when(at.has_right)(lambda: to_left.wait_recv())
        for h in range(heads_here + 1):
            mine, other = t_own[h].astype(jnp.float32), t_pair[h].astype(jnp.float32)
            t_one, t_two = jnp.where(at.i == 0, mine, other), jnp.where(at.i == 0, other, mine)
            come = t_line[h].astype(jnp.float32)
            middle = t_two + on_two * come
            t_next[h] = (t_one + on_one * middle).astype(jnp.bfloat16)
            back[h] = jnp.where(at.i == 0, middle, come).astype(jnp.bfloat16)
        pl.when(at.has_left)(lambda: to_left.start())
        pump(1)

        dens[0] = jnp.zeros_like(dens[0])
        dens[1] = jnp.zeros_like(dens[1])
        dens[0, 0:128, 0:tall] = state[heads_here].astype(jnp.float32).T
        dens[1, 0:128, 0:tall] = back[heads_here].astype(jnp.float32).T
        filler = jnp.zeros((wide - tall, 128), jnp.bfloat16)

        def through(u, h, grad):
            one = dot(u, maps[0]) + plus[0, 0:1, :]
            two = dot(u, maps[1]) + plus[1, 0:1, :]
            grad = grad()
            left = dot((grad * two).astype(jnp.bfloat16), maps[0], COLS)
            left += dot((grad * one).astype(jnp.bfloat16), maps[1], COLS)
            return one * two, of_head(left, h)

        for j in range(rows // tile):
            here = slice(j * tile, (j + 1) * tile)
            carried = jnp.where(starts_col[here] < first, 1.0, 0.0)
            keep = jnp.where(starts_col[here] == last, 1.0, 0.0)

            @pl.loop(0, heads_here)
            def _(h):
                table = jnp.concatenate([state[h], filler], axis=0)
                below = dens[0, pl.ds(h, 1), :]

                def grad_query():
                    grad = dot(g[h, here, :], table, COLS) - delta[h, here, 0:1] * below
                    return grad * plus[2, 0:1, :] * carried

                _, grad = through(of_head(heads[here, 0:q_wide], h), h, grad_query)
                d_query[here, :] += grad
                table_back = jnp.concatenate([back[h], filler], axis=0)
                below_back = dens[1, pl.ds(h, 1), :]

                def grad_key():
                    return (dot(heads[here, values_of(h)], table_back, COLS) + below_back) * keep

                phi, grad = through(of_head(heads[here, q_wide : 2 * q_wide], h), h, grad_key)
                d_key[here, :] += grad
                far = dot((phi * keep).astype(jnp.bfloat16), table_back)
                d_heads[here, values_of(h)] = (d_values[here, head_at(h)] + far).astype(
                    jnp.bfloat16
                )

            d_heads[here, 0:q_wide] = d_query[here, :].astype(jnp.bfloat16)
            d_heads[here, q_wide : 2 * q_wide] = d_key[here, :].astype(jnp.bfloat16)
        pump(1)

        feed_sum.arrive()
        feed_sum.drain()
        for start in range(0, team.quarter, 32):
            feed_sum.from_far[start : start + 32, :] = feed_sum.rows(start, 32).astype(bf)
        for j in range(Sum.pieces):
            columns = slice(j * piece, (j + 1) * piece)

            @pl.loop(0, rows // 256)
            def _(r):
                here = pl.ds(pl.multiple_of(r * 256, 256), 256)
                grad = dot(d_heads[here, :], w_qkv[columns, :], COLS)
                part[here, columns] = grad.astype(jnp.bfloat16)

            first_sum.near(j).start()
            if j:
                first_sum.fold(j - 1)
        first_sum.fold(Sum.pieces - 1)

        down = width // n

        def grad_out(s, to):
            columns = dm[:, s * down : (s + 1) * down]
            to[...] = dot(columns, mixed[...], BOTH).astype(jnp.bfloat16)

        staged(n, tile_sem, tile_o, parts[3], grad_out, lambda s: None)
        begin(s_out)
        pump(1)
        get_one.wait()

        def grad_qkv(s, to):
            columns = arena[:, s * down : (s + 1) * down]
            to[...] = dot(columns, d_heads[...], BOTH).astype(jnp.bfloat16)

        staged(n, tile_sem, tile_q, parts[4], grad_qkv, lambda s: None)
        begin(s_qkv)
        to_pair.wait_send()
        pl.when(at.has_left)(lambda: to_left.wait_send())

    bf, f32 = jnp.bfloat16, jnp.float32
    pl.run_scoped(
        attention,
        pltpu.VMEM((rows, heads_h.shape[1]), bf),
        pltpu.VMEM((rows, heads_h.shape[1]), bf),
        pltpu.VMEM((rows, values_wide), bf),
        pltpu.VMEM(out_h.shape, bf),
        pltpu.VMEM(qkv_h.shape, bf),
        pltpu.VMEM((heads_here, rows, 128), f32),
        pltpu.VMEM((heads_here, rows, 128), bf),
        pltpu.VMEM((heads_here, 8, rows), f32),
        pltpu.VMEM((rows, q_wide), f32),
        pltpu.VMEM((rows, q_wide), f32),
        pltpu.VMEM((2, maps.shape[2], maps.shape[2]), f32),
        pltpu.VMEM((2, width // n, values_wide), bf),
        pltpu.VMEM((2, width // n, heads_h.shape[1]), bf),
        pltpu.SemaphoreType.DMA((2,)),
        pltpu.VMEM((rows, values_wide), f32),
    )

    quarter = pl.ds(pl.multiple_of(team.quarter_at, team.quarter), team.quarter)
    stream_q = arena.at[0 : team.quarter]
    get_stream = load(stream_h.at[quarter], stream_q)
    get_stream.wait()
    first_sum.arrive()
    for j in range(Spread.pieces):
        for k in range(ig_spread.tall // 32):
            down_at = j * ig_spread.tall + k * 32
            here = slice(down_at, down_at + 32)
            x = arena[here, :].astype(f32)
            grad = norm_back(x, first_sum.rows(down_at, 32), gain.at[0], 0)
            to = slice(ig_rows + down_at, ig_rows + down_at + 32)
            arena[to, :] = (d_mid[here, :] + grad).astype(bf)
        ig_spread.send(j)
    ig_spread.keep().start()
    gain_to_near = remote(gain_sum, gain_near, gain_send.at[0], gain_recv.at[0], team.near)
    gain_to_near.start()
    load(mid_h, d_mid).wait()
    for j in range(Spread.pieces):
        for k in range(act_spread.tall // 32):
            down_at = j * act_spread.tall + k * 32
            here = slice(down_at, down_at + 32)
            to = slice(act_rows + down_at, act_rows + down_at + 32)
            arena[to, :] = (d_mid[here, :] + feed_sum.from_far[here, :].astype(f32)).astype(bf)
        act_spread.send(j)
    act_spread.keep().start()
    gain_to_near.wait()
    gain_sum[...] += gain_near[...]
    gain_to_far = remote(gain_sum, gain_far, gain_send.at[1], gain_recv.at[1], team.far)
    gain_to_far.start()
    pump(1)
    gain_to_far.wait()
    gain_near[...] = gain_sum[...] + gain_far[...]
    deep = width // n
    for s in range(n):
        gain_parts[s] = gain_near[:, s * deep : (s + 1) * deep]
    load(gain_parts, parts[5]).wait()
    begin(s_gains)
    for j in range(Spread.pieces):
        pump(1)
        ig_spread.pass_on(j)
    for j in range(Spread.pieces):
        pump(1)
        act_spread.pass_on(j)
    pump.rest()
    s_gains.final()
    for spread_of in (ig_spread, act_spread):
        spread_of.arrive()
        spread_of.drain()
        spread_of.keep().wait()
    spread.drain()
    first_sum.drain()
    for group in groups:
        group.drain()


def backward(n, lengths, maps, stream, cot, wholes, kept):
    rows, width = stream.shape
    gains, qkv, out, gate, up, down = wholes
    heads_here = out.shape[1] // 128
    hidden = gate.shape[1]
    tall = maps[1].shape[1]
    bf, f32 = jnp.bfloat16, jnp.float32
    shape = jax.ShapeDtypeStruct
    deep = width // n
    kinds = [
        ((deep, hidden), bf),
        ((deep, hidden), bf),
        ((deep, hidden), bf),
        ((deep, out.shape[1]), bf),
        ((deep, qkv.shape[1]), bf),
        ((16, deep), f32),
    ]
    results = [shape((rows, width), bf)] * 2 + [shape(*kind) for kind in kinds]
    work = [shape((n,) + size, kind) for size, kind in kinds[1:]]
    work += sum((Scatter.landing(n, *kind) for kind in kinds), [])
    state = (heads_here + 1, tall, 128)
    scratch = [
        pltpu.VMEM((rows, width), bf),
        pltpu.VMEM((rows, width), bf),
        pltpu.VMEM((rows // 4, width), f32),
        pltpu.VMEM((rows, width), bf),
        pltpu.VMEM(gains.shape, f32),
        pltpu.VMEM((2, 8, width), f32),
        pltpu.VMEM((16, width), f32),
        pltpu.VMEM((16, width), f32),
        pltpu.VMEM((16, width), f32),
        pltpu.VMEM((n, 16, deep), f32),
    ]
    scratch += [pltpu.VMEM(state, bf)] * 6
    scratch += [pltpu.SemaphoreType.DMA((2,))] * 4
    scratch += [pltpu.SemaphoreType.DMA((24,))]
    scratch += [pltpu.VMEM((2,) + kinds[k][0], kinds[k][1]) for k in (0, 3, 4, 5)]
    scratch += Sum.scratch(rows, width) * 2 + Sum.scratch(rows, width)[2:] + Spread.scratch() + SpreadOut.scratch() * 2
    scratch += sum((Scatter.scratch(n, *kind) for kind in kinds), [])
    anywhere, inside = pl.BlockSpec(memory_space=pl.ANY), pl.BlockSpec(memory_space=pltpu.VMEM)
    given = [stream, cot, *wholes, *kept]
    result = pl.pallas_call(
        functools.partial(backward_kernel, n),
        out_shape=results + work,
        in_specs=[pl.BlockSpec(memory_space=pltpu.SMEM)] + [inside] * 4 + [anywhere] * len(given),
        out_specs=[anywhere] * (len(results) + len(work)),
        scratch_shapes=scratch,
        compiler_params=pltpu.CompilerParams(
            collective_id=1, has_side_effects=True, vmem_limit_bytes=63 * MIB
        ),
    )(lengths, *maps, *given)
    return result[: len(results)]


def on_device(
    stream_in,
    doc_lengths,
    first_gain,
    w_query,
    w_key,
    w_value,
    w_out,
    second_gain,
    w_gate,
    w_up,
    w_down,
    cotangent,
):
    n = lax.axis_size("seq")
    f32 = jnp.float32
    q_wide, k_wide = w_query.shape[1], w_key.shape[1]
    qkv_own = jnp.concatenate([w_query, w_key, w_value], axis=1)
    gains_own = jnp.concatenate([first_gain, second_gain]).astype(f32)
    gains_own = jnp.broadcast_to(gains_own[None], (16, gains_own.shape[0]))
    maps = feature_maps(q_wide)
    shards = (gains_own, qkv_own, w_out.T, w_gate, w_up, w_down.T)
    wholes, kept = forward(n, doc_lengths, stream_in, cotangent, maps, shards)
    activations, input_grad, g_down, g_gate, g_up, g_out, g_qkv, g_gains = backward(
        n, doc_lengths, maps, stream_in, cotangent, wholes, kept
    )
    g_qkv = g_qkv.astype(f32)
    return (
        activations,
        input_grad.astype(f32),
        jnp.sum(g_gains[:8], axis=0),
        g_qkv[:, :q_wide],
        g_qkv[:, q_wide : q_wide + k_wide],
        g_qkv[:, q_wide + k_wide :],
        g_out.astype(f32).T,
        jnp.sum(g_gains[8:], axis=0),
        g_gate.astype(f32),
        g_up.astype(f32),
        g_down.astype(f32).T,
    )


def solution(mesh):
    placed = (
        P("seq", None),
        P(),
        P("seq"),
        P("seq", "tp"),
        P("seq", "tp"),
        P("seq", "tp"),
        P("tp", "seq"),
        P("seq"),
        P("seq", "tp"),
        P("seq", "tp"),
        P("tp", "seq"),
        P("seq", None),
    )
    return jax.shard_map(
        on_device,
        mesh=mesh,
        in_specs=placed,
        out_specs=(
            P("seq", None),
            P("seq", None),
            P("seq"),
            P("seq", "tp"),
            P("seq", "tp"),
            P("seq", "tp"),
            P("tp", "seq"),
            P("seq"),
            P("seq", "tp"),
            P("seq", "tp"),
            P("tp", "seq"),
        ),
        check_vma=False,
    )
```

time: 1260 us -> 646 us (0.51)
  matrix products: 279 us -> 0 us
  waiting for transfers between devices: 228 us -> 0 us
  Pallas kernels: 461 us -> 607 us
  other arithmetic: 97.3 us -> 11.9 us
  blocking collectives: 80.3 us -> 0 us
  local copies, waits for them, and re-layouts: 89.5 us -> 20.2 us
  between operations: 15.2 us -> 1.22 us
    dot_general x35 -> x0, matrix products: 279 us -> none  [the longest x3 56 us: attend(): numerator = jnp.einsum('hij,jhd->ihd', weights, value_rows, precision=HIGH)]
    psum x3 -> x0, waiting for transfers between devices: 228 us -> none  [the longest x1 93.5 us: on_device(): dh_one = lax.psum(dh_local.astype(jnp.bfloat16), 'tp').astype(jnp.float32)]
    pallas_call x2, Pallas kernels: 461 us -> 607 us  [the longest x1 361 us: backward(): pl.pallas_call(functools.partial(backward_kernel, n), out_shape=results +...]
    all_gather x2 -> x0, blocking collectives: 61.3 us -> none  [the longest x1 30.9 us: entering_2(): lax.all_gather(part.astype(kind), axis)]
    reduce_sum x7 -> x1, other arithmetic: 32.7 us -> 1.36 us  [on_device(): jnp.sum(g_gains[8:], axis=0)]
    convert_element_type x4 -> x0, local copies, waits for them, and re-layouts: 28.1 us -> none  [the longest x2 16.7 us: rows_of(): return g.astype(jnp.bfloat16).reshape((n, g.shape[0] // n) + g.shape[1:])]
    select_n x16 -> x0, other arithmetic: 20.8 us -> none  [step(): return jax.tree.map(lambda a, b: jnp.where(reached, a, b), new, before)]
    unnamed x1 -> x0, blocking collectives: 19 us -> none
  transfers between devices with their start and end apart: 5 -> 0, of which waited for: 3 -> 0; matrix products, arithmetic and copies ran while one was open for 16% -> 0% of each run, Pallas kernels for 0% -> 0%
where the time goes in v2:
time: 646 us; the launch traced here: 640 us
  Pallas kernels  607 us (94%)
  local copies, waits for them, and re-layouts  20.2 us (3%)
  other arithmetic  11.9 us (2%)
    pallas_call x1, Pallas kernels, backward(): pl.pallas_call(functools.partial(backward_kernel, n), out_shape=results +...  361 us
    pallas_call x1, Pallas kernels, forward(): pl.pallas_call(functools.partial(forward_kernel, n, None), out_shape=whol...  246 us
    unnamed x25, local copies, waits for them, and re-layouts  16.7 us

profile of v2, /device:TPU:0, one launch (start us, length us, event | category | flops | bytes accessed | tf_op | source)
XLA Modules:
  0.0 640.2 jit_solution(12730858628817811132)
XLA Ops:
  0.6 0.0 copy-start.5
  0.7 0.0 copy-start.4
  0.7 0.8 maximum_convert_fusion
  1.4 0.6 broadcast_in_dim.2.refs_7_
  2.1 0.9 copy.27
  2.9 0.9 copy.28
  3.8 1.8 pad_maximum_fusion.refs_8_
  5.6 1.8 copy.29
  7.4 2.2 copy.31.refs_10_
  9.6 0.0 copy-done.4
  9.6 1.1 copy.32.refs_11_
  10.8 0.0 copy-done.5
  10.8 1.1 copy.30
  11.9 246.1 %shard_map.239 = (f32[8,16,512]{2,1,0:T(8,128)}, bf16[2048,640]{1,0:T(8,128)(2,1)}, bf16[2048,512]{1,0:T(8,128)(2,1)}, bf16[2048,1376]{1,0:T(8,128)(2,1)}, bf16[...) custom-call(s32[4]{0:T(128)} %refs_0_.3, ...), custom_call_target="tpu_custom_call" | custom-call | tf_op jit(solution)/shard_map/pallas_call | solution.py:1019
  258.0 360.8 %shard_map.240 = (bf16[1024,2048]{1,0:T(8,128)(2,1)}, bf16[1024,2048]{1,0:T(8,128)(2,1)}, bf16[256,1376]{1,0:T(8,128)(2,1)}, bf16[256,1376]{1,0:T(8,128)(2,1)}, ...) custom-call(s32[4]{0:T(128)} %refs_0_.3, ...), custom_call_target="tpu_custom_call" | custom-call | tf_op jit(solution)/shard_map/pallas_call | solution.py:1618
  618.8 0.0 copy-start.3
  618.8 1.4 slice_reduce_fusion
  620.2 1.0 fusion
  621.2 0.7 copy.34
  621.9 0.7 copy.33
  622.6 1.8 slice.22
  624.4 1.1 convert_bitcast_fusion.1
  625.5 1.0 copy.35
  626.5 0.0 copy-done.3
  626.5 1.4 copy.36
  627.9 0.0 copy-done.2
  627.9 1.4 copy.37
  629.3 0.1 convert_bitcast_fusion
  629.4 1.5 copy.38
  630.9 6.8 %convert_element_type.22 = f32[1024,2048]{1,0:T(8,128)} convert(bf16[1024,2048]{1,0:T(8,128)(2,1)} %get-tuple-element.54) | non-fusion elementwise | flops 2097152 | bytes 12582912 | tf_op jit(solution)/shard_map/convert_element_type | solution.py:1660
  637.7 0.0 copy-done
  637.7 2.0 copy.40
  (4 shorter events, 0.0 us)
Async XLA Ops:
  0.6 10.1 %copy-start.5 = (bf16[1376,256]{1,0:T(8,128)(2,1)S(1)}, bf16[1376,256]{1,0:T(8,128)(2,1)}, u32[]{:S(2)}) copy-start(bf16[1376,256]{1,0:T(8,128)(2,1)} %param.26) | copy-start | bytes 2113540
  0.7 9.0 %copy-start.4 = (bf16[256,1376]{0,1:T(8,128)(2,1)S(1)}, bf16[256,1376]{0,1:T(8,128)(2,1)}, u32[]{:S(2)}) copy-start(bf16[256,1376]{0,1:T(8,128)(2,1)} %param.25) | copy-start | bytes 2113540
  618.8 7.7 %copy-start.3 = (bf16[256,1376]{1,0:T(8,128)(2,1)S(1)}, bf16[256,1376]{1,0:T(8,128)(2,1)}, u32[]{:S(2)}) copy-start(bf16[256,1376]{1,0:T(8,128)(2,1)} %get-tuple-element.58) | copy-start | bytes 2113540
  620.2 7.7 %copy-start.2 = (bf16[256,1376]{1,0:T(8,128)(2,1)S(1)}, bf16[256,1376]{1,0:T(8,128)(2,1)}, u32[]{:S(2)}) copy-start(bf16[256,1376]{1,0:T(8,128)(2,1)} %get-tuple-element.59) | copy-start | bytes 2113540
  624.4 4.8 copy-start.1
  630.9 6.8 %copy-start = (bf16[1024,2048]{1,0:T(8,128)(2,1)S(1)}, bf16[1024,2048]{1,0:T(8,128)(2,1)}, u32[]{:S(2)}) copy-start(bf16[1024,2048]{1,0:T(8,128)(2,1)} %get-tuple-element.87) | copy-start | bytes 12582916

commit v3 on v2

--- a/solution.py
+++ b/solution.py
@@ -240,15 +240,20 @@
             pltpu.SemaphoreType.DMA((m + 4,)),
         ]
 
+    def slot(self, slot):
+        if self.parts.ndim == 3:
+            return self.parts.at[slot]
+        return self.parts.at[pl.ds(pl.multiple_of(slot * self.rows, 16), self.rows)]
+
     def load(self, layer):
         return pltpu.make_async_copy(
-            self.parts.at[layer * 2 + self.at.i], self.mine.at[layer], self.local.at[layer]
+            self.slot(layer * 2 + self.at.i), self.mine.at[layer], self.local.at[layer]
         )
 
     def load_aside(self):
         at = self.at
         return pltpu.make_async_copy(
-            self.parts.at[at.o * 2 + 1 - at.i], self.aside.at[0], self.local.at[at.m]
+            self.slot(at.o * 2 + 1 - at.i), self.aside.at[0], self.local.at[at.m]
         )
 
     def store(self):
@@ -263,7 +268,7 @@
 
     def to_pair(self, layer):
         return remote(
-            self.parts.at[layer * 2 + 1 - self.at.i],
+            self.slot(layer * 2 + 1 - self.at.i),
             self.from_pair.at[layer],
             self.pair_send.at[layer],
             self.pair_recv.at[layer],
@@ -312,7 +317,7 @@
 
     def shifted(self, way, which=None):
         at, half = self.at, self.rows // 2
-        src, dst = self.parts.at[at.partner * 2 + 1 - at.i], self.shifted_in.at[0]
+        src, dst = self.slot(at.partner * 2 + 1 - at.i), self.shifted_in.at[0]
         if which is not None:
             src, dst = src.at[pl.ds(half, half)], dst.at[pl.ds(half, half)]
         return remote(
@@ -336,14 +341,14 @@
                 lambda: act(self.to_pair(layer))
             )
             pl.when(there & partner & at.end)(
-                lambda: act(self.half_to_pair(layer, 0, self.parts.at[layer * 2 + 1 - at.i]))
+                lambda: act(self.half_to_pair(layer, 0, self.slot(layer * 2 + 1 - at.i)))
             )
         if not at.balanced:
             act(self.to_pair(at.o))
             return
         pl.when(jnp.logical_not(at.end | at.next))(lambda: act(self.to_pair(at.o)))
         pl.when(at.next)(
-            lambda: act(self.half_to_pair(at.o, 0, self.parts.at[at.o * 2 + 1 - at.i]))
+            lambda: act(self.half_to_pair(at.o, 0, self.slot(at.o * 2 + 1 - at.i)))
         )
 
     def shift_copies(self, act):
@@ -706,6 +711,10 @@
     return jnp.where(mine, values, jnp.zeros_like(values))
 
 
+def column(values, h):
+    return jnp.sum(jnp.where(lanes((1, 128)) == h, values, 0.0), axis=1, keepdims=True)
+
+
 def with_ones(values):
     return jnp.concatenate([values, jnp.ones_like(values)], axis=1)
 
@@ -713,9 +722,11 @@
 def forward_kernel(n, sizes, *refs):
     (
         lengths, stream_h, cot_h, maps, maps_t, plus, plus_t,
-        gains_own, qkv_own, out_own, gate_own, up_own, down_own,
+        gains_own, query_h, key_h, value_h, out_raw_h, gate_raw_h, up_raw_h, down_raw_h,
         gains_h, qkv_h, out_h, gate_h, up_h, down_h,
         h_one_h, heads_h, mixed_h, rden_h, state_h, mid_h, h_two_h, gate_v_h, up_v_h, hid_h, part_h,
+        query_own, key_own, value_own, out_raw, gate_raw, up_raw, down_raw,
+        qkv_own, out_own, gate_own, up_own, down_own,
         stream, h_one, heads, w_qkv, w_out, mixed, rden, numer, mid, h_two, w_ff,
         gate_v, up_v, hid, part, gains, gain,
         t_own, t_pair, t_line, t_next, state, t_send, t_recv, local, part_sem,
@@ -734,8 +745,6 @@
         Gather(at, shards[g], wholes[g], sems[4 * g : 4 * g + 4]) for g in range(len(shards))
     ]
     g_gains, g_qkv, g_out, g_gate, g_up, g_down = groups
-    at.greet((team.near, team.far))
-    pump = Pump(gather_events(groups))
     cell = iter(range(local.shape[0]))
     copies = []
 
@@ -747,7 +756,30 @@
     def save(src, dst):
         copies.append(load(src, dst))
 
+    raw = [
+        load(query_h, query_own),
+        load(key_h, key_own),
+        load(value_h, value_own),
+        load(out_raw_h, out_raw),
+        load(gate_raw_h, gate_raw),
+        load(up_raw_h, up_raw),
+        load(down_raw_h, down_raw),
+    ]
     get_stream = load(stream_h, stream)
+    at.greet((team.near, team.far))
+    pump = Pump(gather_events(groups))
+    pump(1)
+    for copy in raw[:3]:
+        copy.wait()
+    qkv_own[:, 0:q_wide] = query_own[...].T
+    qkv_own[:, q_wide : 2 * q_wide] = key_own[...].T
+    qkv_own[:, 2 * q_wide :] = value_own[...]
+    pump.until(g_qkv.own)
+    for copy, turned, own in zip(
+        raw[3:], (out_raw, gate_raw, up_raw, down_raw), (out_own, gate_own, up_own, down_own)
+    ):
+        copy.wait()
+        own[...] = turned[...].T
     pump.until(g_gains.extra)
     g_gains.arrive()
     load(gains_h, gains).wait()
@@ -839,6 +871,7 @@
     save(state, state_h)
     pump(1)
 
+    rden[...] = jnp.zeros_like(rden)
     @pl.loop(0, heads_here)
     def _(h):
         own = lanes((tall, 128)) == h
@@ -857,7 +890,7 @@
             phi = (one * two * plus[2, 0:1, :] * carried).astype(jnp.bfloat16)
             total = numer[h, here, :] + dot(phi, table)
             inverse = 1.0 / total[:, 128:]
-            rden[h, here, :] = inverse
+            rden[here, :] = jnp.where(lanes((1, 128)) == h, inverse, rden[here, :])
             mixed[here, pl.ds(pl.multiple_of(h * 128, 128), 128)] = (
                 total[:, :128] * inverse
             ).astype(jnp.bfloat16)
@@ -932,19 +965,24 @@
     save(up_v, up_v_h)
     save(hid, hid_h)
     get_cot.wait()
-    deep = part.shape[1]
-    for s in range(n):
-        if s > 1:
-            fetch(part.at[s % 2], part_h.at[s - 2], part_sem.at[s % 2]).wait()
-        columns = stream[:, s * deep : (s + 1) * deep]
-        for low in range(0, hid.shape[1], 512):
-            high = min(hid.shape[1], low + 512)
-            part[s % 2, :, low:high] = dot(columns, hid[:, low:high], BOTH).astype(jnp.bfloat16)
-        fetch(part.at[s % 2], part_h.at[s], part_sem.at[s % 2]).start()
-        if s % max(1, n // 4) == 0:
-            pump(1)
-    for s in range(n - 2, n):
-        fetch(part.at[s % 2], part_h.at[s], part_sem.at[s % 2]).wait()
+    def to_hbm(s, slot):
+        here = pl.ds(pl.multiple_of(s * 256, 256), 256)
+        return fetch(part.at[slot], part_h.at[here], part_sem.at[slot])
+
+    count = width // 256
+    for half in range(2):
+
+        @pl.loop(half * (count // 2), (half + 1) * (count // 2))
+        def _(s):
+            slot = lax.rem(s, 2)
+            pl.when(s > 1)(lambda: to_hbm(s - 2, slot).wait())
+            columns = pl.ds(pl.multiple_of(s * 256, 256), 256)
+            part[slot] = dot(stream[:, columns], hid[...], BOTH).astype(jnp.bfloat16)
+            to_hbm(s, slot).start()
+
+        pump(1)
+    for s in range(count - 2, count):
+        to_hbm(s, s % 2).wait()
     pump.rest()
     g_down.arrive()
     for group in groups:
@@ -957,16 +995,17 @@
 
 def forward(n, lengths, stream, cot, maps, shards):
     rows, width = stream.shape
-    gains, qkv, out, gate, up, down = shards
-    hidden = gate.shape[1]
-    values = out.shape[1]
+    gains, query, key, value, out, gate, up, down = shards
+    hidden, deep = gate.shape
+    values = out.shape[0]
+    qkv_wide = 2 * query.shape[0] + values
     heads_here = values // 128
     tall = maps[1].shape[1]
     bf, f32 = jnp.bfloat16, jnp.float32
     shape = jax.ShapeDtypeStruct
     wholes = [
         shape((n,) + gains.shape, f32),
-        shape((n * qkv.shape[0], qkv.shape[1]), bf),
+        shape((width, qkv_wide), bf),
         shape((width, values), bf),
         shape((width, hidden), bf),
         shape((width, hidden), bf),
@@ -974,26 +1013,28 @@
     ]
     kept = [
         shape((rows, width), bf),
-        shape((rows, qkv.shape[1]), bf),
+        shape((rows, qkv_wide), bf),
         shape((rows, values), bf),
-        shape((heads_here, rows, 128), f32),
+        shape((rows, 128), f32),
         shape((heads_here + 1, tall, 128), bf),
         shape((rows // 4, width), f32),
         shape((rows, width), bf),
         shape((rows, hidden), bf),
         shape((rows, hidden), bf),
         shape((rows, hidden), bf),
-        shape((n,) + down.shape, bf),
+        shape((width, hidden), bf),
     ]
     state = (heads_here + 1, tall, 128)
-    scratch = [
+    scratch = [pltpu.VMEM(a.shape, bf) for a in shards[1:]]
+    scratch += [pltpu.VMEM((deep, wide), bf) for wide in (qkv_wide, values, hidden, hidden, hidden)]
+    scratch += [
         pltpu.VMEM((rows, width), bf),
         pltpu.VMEM((rows, width), bf),
-        pltpu.VMEM((rows, qkv.shape[1]), bf),
-        pltpu.VMEM((width, qkv.shape[1]), bf),
+        pltpu.VMEM((rows, qkv_wide), bf),
+        pltpu.VMEM((width, qkv_wide), bf),
         pltpu.VMEM((width, values), bf),
         pltpu.VMEM((rows, values), bf),
-        pltpu.VMEM((heads_here, rows, 128), f32),
+        pltpu.VMEM((rows, 128), f32),
         pltpu.VMEM((heads_here, rows, 256), f32),
         pltpu.VMEM((rows // 4, width), f32),
         pltpu.VMEM((rows, width), bf),
@@ -1001,7 +1042,7 @@
         pltpu.VMEM((rows, hidden), bf),
         pltpu.VMEM((rows, hidden), bf),
         pltpu.VMEM((rows, hidden), bf),
-        pltpu.VMEM((2,) + down.shape, bf),
+        pltpu.VMEM((2, 256, hidden), bf),
         pltpu.VMEM((n,) + gains.shape, f32),
         pltpu.VMEM((2, 8, width), f32),
         pltpu.VMEM(state, bf),
@@ -1011,17 +1052,17 @@
         pltpu.VMEM(state, bf),
         pltpu.SemaphoreType.DMA((2,)),
         pltpu.SemaphoreType.DMA((2,)),
-        pltpu.SemaphoreType.DMA((24,)),
+        pltpu.SemaphoreType.DMA((32,)),
         pltpu.SemaphoreType.DMA((2,)),
     ]
-    scratch += Sum.scratch(rows, width) + Spread.scratch() + Gather.scratch(n) * len(shards)
+    scratch += Sum.scratch(rows, width) + Spread.scratch() + Gather.scratch(n) * len(wholes)
     anywhere, inside = pl.BlockSpec(memory_space=pl.ANY), pl.BlockSpec(memory_space=pltpu.VMEM)
     result = pl.pallas_call(
         functools.partial(forward_kernel, n, None),
         out_shape=wholes + kept,
         in_specs=[pl.BlockSpec(memory_space=pltpu.SMEM), anywhere, anywhere]
         + [inside] * 4
-        + [anywhere] * 6,
+        + [anywhere] * len(shards),
         out_specs=[anywhere] * (len(wholes) + len(kept)),
         scratch_shapes=scratch,
         compiler_params=pltpu.CompilerParams(
@@ -1115,16 +1156,11 @@
         return copy
 
     pump = Pump([])
-    begun = []
 
     def begin(group):
         group.start()
-        last = begun[-1] if begun else None
-        begun.append(group)
         for d in range(at.m - 1, 0, -1):
             pump.events.append(functools.partial(group.step, d))
-            if d == max(1, at.m - 2) and last is not None:
-                pump.events.append(last.final)
         pump.events.append(group.extra)
 
     begin(s_down)
@@ -1134,24 +1170,28 @@
     feed_sum = Sum(team, part, *sums[1][:2], sums[1][2:])
     first_sum = Sum(team, part, *sums[0][:2], first_sems)
     spread = Spread(team, dm, dm_sems)
-    ig_rows, act_rows = team.quarter, 2 * team.quarter
+    ig_rows = team.quarter
     ig_spread = SpreadOut(team, arena.at[pl.ds(ig_rows, team.quarter)], ig_h, ig_sems)
-    act_spread = SpreadOut(team, arena.at[pl.ds(act_rows, team.quarter)], act_h, act_sems)
+    act_spread = SpreadOut(team, feed_sum.from_far, act_h, act_sems)
     piece = part_sum.wide
 
-    def staged(count, sem, tile, parts_h, compute, between):
-        for s in range(count):
-            if s > 1:
-                fetch(tile.at[s % 2], parts_h.at[s - 2], sem.at[s % 2]).wait()
-            compute(s, tile.at[s % 2])
-            fetch(tile.at[s % 2], parts_h.at[s], sem.at[s % 2]).start()
-            between(s)
+    def staged(sem, tile, parts_h, compute):
+        count = width // 256
+
+        def to_hbm(s, slot):
+            here = pl.ds(pl.multiple_of(s * 256, 256), 256)
+            return fetch(tile.at[slot], parts_h.at[here], sem.at[slot])
+
+        @pl.loop(0, count)
+        def _(s):
+            slot = lax.rem(s, 2)
+            pl.when(s > 1)(lambda: to_hbm(s - 2, slot).wait())
+            columns = pl.ds(pl.multiple_of(s * 256, 256), 256)
+            tile[slot] = compute(columns).astype(jnp.bfloat16)
+            to_hbm(s, slot).start()
+
         for s in range(count - 2, count):
-            fetch(tile.at[s % 2], parts_h.at[s], sem.at[s % 2]).wait()
-
-    def now_and_then(s):
-        if s % max(1, n // 4) == n // 4 - 1:
-            pump(1)
+            to_hbm(s, s % 2).wait()
 
     def norm_back(x, grad, gain_ref, which):
         scale = lax.rsqrt(jnp.mean(x * x, axis=1, keepdims=True) + EPSILON)
@@ -1197,7 +1237,7 @@
                 )
                 ff[1, here, low:high] = (grad * silu).astype(jnp.bfloat16)
 
-            pump(1)
+        pump(1)
         get_two = load(h_two_h, arena)
         count = width // tall
         for j in range(count):
@@ -1206,9 +1246,9 @@
                     weights(j + 1, which).start()
                 weights(j, which).wait()
 
-            @pl.loop(0, rows // 256)
+            @pl.loop(0, rows // 512)
             def _(r):
-                here = pl.ds(pl.multiple_of(r * 256, 256), 256)
+                here = pl.ds(pl.multiple_of(r * 512, 512), 512)
                 grad = dot(ff[0, here, :], w_ff[j % 2, 0], COLS)
                 grad += dot(ff[1, here, :], w_ff[j % 2, 1], COLS)
                 part[here, j * tall : (j + 1) * tall] = grad.astype(jnp.bfloat16)
@@ -1218,66 +1258,56 @@
                 part_sum.near(p).start()
                 if p:
                     part_sum.fold(p - 1)
-            if j % 4 == 3:
-                pump(1)
         part_sum.fold(Sum.pieces - 1)
         get_two.wait()
         pump(1)
-        down = width // n
-        tile = w_ff.at[0, :, 0:down]
+        tile = w_ff.at[0]
 
         def grads(which):
-            def compute(s, to):
-                columns = arena[:, s * down : (s + 1) * down]
-                for low in range(0, hidden, 512):
-                    high = min(hidden, low + 512)
-                    grad = dot(columns, ff[which, :, low:high], BOTH)
-                    to[:, low:high] = grad.astype(jnp.bfloat16)
-
-            return compute
-
-        staged(n, tile_sem, tile, parts[1], grads(0), now_and_then)
+            return lambda columns: dot(arena[:, columns], ff[which], BOTH)
+
+        staged(tile_sem, tile, parts[1], grads(0))
         begin(s_gate)
         get_gains.wait()
         gain_row(gains, 0, gain.at[0])
         gain_row(gains, 1, gain.at[1])
         get_mid.wait()
         part_sum.arrive()
+        quarter = pl.ds(pl.multiple_of(team.quarter_at, team.quarter), team.quarter)
+        load(cot_h.at[quarter], dm.at[quarter]).wait()
         for j in range(Spread.pieces):
-            for k in range(spread.tall // 32):
-                down_at = j * spread.tall + k * 32
-                here = pl.ds(pl.multiple_of(team.quarter_at + down_at, 32), 32)
-                x = d_mid[down_at : down_at + 32, :]
-                grad = norm_back(x, part_sum.rows(down_at, 32), gain.at[1], 1)
-                d_mid[down_at : down_at + 32, :] = grad
-        quarter = pl.ds(pl.multiple_of(team.quarter_at, team.quarter), team.quarter)
-        get = load(cot_h.at[quarter], dm.at[quarter])
-        get.wait()
-        for j in range(Spread.pieces):
-            for k in range(spread.tall // 32):
-                down_at = j * spread.tall + k * 32
-                here = pl.ds(pl.multiple_of(team.quarter_at + down_at, 32), 32)
-                grad = d_mid[down_at : down_at + 32, :]
+
+            @pl.loop(0, spread.tall // 32)
+            def _(r):
+                start = pl.multiple_of(j * spread.tall + r * 32, 32)
+                here = pl.ds(pl.multiple_of(team.quarter_at + start, 32), 32)
+                x = d_mid[pl.ds(start, 32), :]
+                grad = norm_back(x, part_sum.rows(start, 32), gain.at[1], 1)
                 grad = grad + dm[here, :].astype(jnp.float32)
-                d_mid[down_at : down_at + 32, :] = grad
+                d_mid[pl.ds(start, 32), :] = grad
                 dm[here, :] = grad.astype(jnp.bfloat16)
+
             spread.send(j)
         part_sum.drain()
-        staged(n, tile_sem, tile, parts[2], grads(1), now_and_then)
-        begin(s_up)
+        pump(1)
+        staged(tile_sem, tile, parts[2], grads(1))
+        pump(1)
         get_hid = load(hid_h, ff.at[0])
         get_hid.wait()
         for j in range(Sum.pieces):
             columns = slice(j * piece, (j + 1) * piece)
 
-            @pl.loop(0, rows // 256)
+            @pl.loop(0, rows // 512)
             def _(r):
-                here = pl.ds(pl.multiple_of(r * 256, 256), 256)
+                here = pl.ds(pl.multiple_of(r * 512, 512), 512)
                 feed = dot(ff[0, here, :], w_down[columns, :], COLS)
                 part[here, columns] = feed.astype(jnp.bfloat16)
 
             feed_sum.near(j).start()
             spread.pass_on(j)
+            if j == Sum.pieces - 2:
+                pump(1)
+
 
     pl.run_scoped(
         feed_forward,
@@ -1290,17 +1320,28 @@
 
     def attention(
         heads, d_heads, mixed, w_out, w_qkv, delta, g, delta_row, d_query, d_key,
-        dens, tile_o, tile_q, tile_sem, d_values,
+        dens, tile_o, tile_q, tile_sem, d_values, mid_part, mid_sem, qkv_sem,
     ):
         gets = [
             load(heads_h, heads),
             load(mixed_h, mixed),
             load(out_h, w_out),
             load(rden_h, delta),
-            load(qkv_h, w_qkv),
             load(state_h, state),
         ]
         get_one = load(h_one_h, arena)
+
+        def mid_rows(j):
+            here = pl.ds(j * act_spread.tall, act_spread.tall)
+            return fetch(mid_h.at[here], mid_part.at[j % 2], mid_sem.at[j % 2])
+
+        def qkv_rows(j):
+            here = pl.ds(j * piece, piece)
+            return fetch(qkv_h.at[here], w_qkv.at[j % 2], qkv_sem.at[j % 2])
+
+        for j in range(2):
+            mid_rows(j).start()
+            qkv_rows(j).start()
         for get in gets:
             get.wait()
         spread.arrive()
@@ -1316,14 +1357,13 @@
         @pl.loop(0, heads_here)
         def _(h):
             across = pl.ds(pl.multiple_of(h * 128, 128), 128)
-            grad = d_values[:, across] * delta[h]
+            grad = d_values[:, across] * column(delta[...], h)
             g[h] = grad.astype(jnp.bfloat16)
             sums_of = jnp.sum(grad * mixed[:, across].astype(jnp.float32), axis=1, keepdims=True)
             wide = jnp.broadcast_to(sums_of, (rows, 128))
-            delta[h] = wide
+            delta[...] = jnp.where(lanes((1, 128)) == h, wide, delta[...])
             delta_row[h] = wide.T[0:8]
 
-        pump(1)
         first = at.s * rows
         starts_col = row_start(lengths, first + lax.broadcasted_iota(jnp.int32, (rows, 1), 0))
         starts_row = row_start(lengths, first + lax.broadcasted_iota(jnp.int32, (1, rows), 1))
@@ -1353,9 +1393,40 @@
         to_pair = remote(t_own, t_pair, t_send.at[0], t_recv.at[0], at.pair)
         to_left = remote(t_next, t_line, t_send.at[1], t_recv.at[1], at.left)
         to_pair.start()
-        pump(1)
+        begin(s_up)
+
+        @pl.when(at.o == at.m - 1)
+        def _():
+            t_line[...] = jnp.zeros_like(t_line)
+
+        def closed(s):
+            return jnp.where(row_start(lengths, (s + 1) * rows - 1) >= s * rows, 0.0, 1.0)
+
+        on_one, on_two = closed(at.o * 2), closed(at.o * 2 + 1)
+
+        def relay():
+            to_pair.wait_recv()
+            pl.when(at.has_right)(lambda: to_left.wait_recv())
+
+            @pl.loop(0, heads_here + 1)
+            def _(h):
+                mine, other = t_own[h].astype(jnp.float32), t_pair[h].astype(jnp.float32)
+                t_one, t_two = jnp.where(at.i == 0, mine, other), jnp.where(at.i == 0, other, mine)
+                come = t_line[h].astype(jnp.float32)
+                middle = t_two + on_two * come
+                t_next[h] = (t_one + on_one * middle).astype(jnp.bfloat16)
+                back[h] = jnp.where(at.i == 0, middle, come).astype(jnp.bfloat16)
+
+            pl.when(at.has_left)(lambda: to_left.start())
+
+        turns = min(4, at.m)
+
+        def turn(p):
+            mine = at.o == at.m - 1 - p if p < turns - 1 else at.o <= at.m - turns
+            pl.when(mine)(relay)
 
         d_query[...] = jnp.zeros_like(d_query)
+        d_key[...] = jnp.zeros_like(d_key)
         tile = 128
 
         def intra(h):
@@ -1365,7 +1436,7 @@
                 here, upto = slice(j * tile, (j + 1) * tile), (j + 1) * tile
                 mask = pair_mask(starts_col[here], starts_row[:, :upto], j * tile, 0)
                 more, _ = scores(query[here], key[:upto], mask)
-                d_weight = dot(g[h, here, :], heads[0:upto, across], COLS) - delta[h, here, 0:1]
+                d_weight = dot(g[h, here, :], heads[0:upto, across], COLS) - column(delta[here, :], h)
                 d_score = jnp.where(mask, d_weight * more, 0.0).astype(jnp.bfloat16)
                 d_query[here, :] += dot(d_score, key[:upto]) * 0.25
             for j in range(rows // tile):
@@ -1382,42 +1453,13 @@
                 grad = dot(d_score, query[after:]) * 0.25
                 d_key[here, :] = jnp.where(h == 0, grad, d_key[here, :] + grad)
 
-        d_key[...] = jnp.zeros_like(d_key)
-        per = max(1, heads_here // 2)
-        for part_of in range(0, heads_here, per):
-
-            @pl.loop(part_of, part_of + per)
+        for half in range(2):
+            @pl.loop(half * heads_here // 2, (half + 1) * heads_here // 2)
             def _(h):
                 intra(h)
 
-            pump(1)
-
-        def closed(s):
-            return jnp.where(row_start(lengths, (s + 1) * rows - 1) >= s * rows, 0.0, 1.0)
-
-        on_one, on_two = closed(at.o * 2), closed(at.o * 2 + 1)
-
-        @pl.when(at.o == at.m - 1)
-        def _():
-            t_line[...] = jnp.zeros_like(t_line)
-
-        to_pair.wait_recv()
-        pl.when(at.has_right)(lambda: to_left.wait_recv())
-        for h in range(heads_here + 1):
-            mine, other = t_own[h].astype(jnp.float32), t_pair[h].astype(jnp.float32)
-            t_one, t_two = jnp.where(at.i == 0, mine, other), jnp.where(at.i == 0, other, mine)
-            come = t_line[h].astype(jnp.float32)
-            middle = t_two + on_two * come
-            t_next[h] = (t_one + on_one * middle).astype(jnp.bfloat16)
-            back[h] = jnp.where(at.i == 0, middle, come).astype(jnp.bfloat16)
-        pl.when(at.has_left)(lambda: to_left.start())
+        turn(0)
         pump(1)
-
-        dens[0] = jnp.zeros_like(dens[0])
-        dens[1] = jnp.zeros_like(dens[1])
-        dens[0, 0:128, 0:tall] = state[heads_here].astype(jnp.float32).T
-        dens[1, 0:128, 0:tall] = back[heads_here].astype(jnp.float32).T
-        filler = jnp.zeros((wide - tall, 128), jnp.bfloat16)
 
         def through(u, h, grad):
             one = dot(u, maps[0]) + plus[0, 0:1, :]
@@ -1427,74 +1469,112 @@
             left += dot((grad * one).astype(jnp.bfloat16), maps[1], COLS)
             return one * two, of_head(left, h)
 
-        for j in range(rows // tile):
-            here = slice(j * tile, (j + 1) * tile)
-            carried = jnp.where(starts_col[here] < first, 1.0, 0.0)
-            keep = jnp.where(starts_col[here] == last, 1.0, 0.0)
-
+        wider = 256
+
+        def each_tile(body):
             @pl.loop(0, heads_here)
             def _(h):
+                @pl.loop(0, rows // wider)
+                def _(j):
+                    here = pl.ds(pl.multiple_of(j * wider, wider), wider)
+                    at_row = first + j * wider + lax.broadcasted_iota(jnp.int32, (wider, 1), 0)
+                    body(h, here, row_start(lengths, at_row))
+
+        filler = jnp.zeros((wide - tall, 128), jnp.bfloat16)
+        dens[0] = jnp.zeros_like(dens[0])
+        dens[0, 0:128, 0:tall] = state[heads_here].astype(jnp.float32).T
+
+        def through_in(h, here, starts):
+            carried = jnp.where(starts < first, 1.0, 0.0)
+
+            def grad_phi():
                 table = jnp.concatenate([state[h], filler], axis=0)
-                below = dens[0, pl.ds(h, 1), :]
-
-                def grad_query():
-                    grad = dot(g[h, here, :], table, COLS) - delta[h, here, 0:1] * below
-                    return grad * plus[2, 0:1, :] * carried
-
-                _, grad = through(of_head(heads[here, 0:q_wide], h), h, grad_query)
-                d_query[here, :] += grad
-                table_back = jnp.concatenate([back[h], filler], axis=0)
-                below_back = dens[1, pl.ds(h, 1), :]
-
-                def grad_key():
-                    return (dot(heads[here, values_of(h)], table_back, COLS) + below_back) * keep
-
-                phi, grad = through(of_head(heads[here, q_wide : 2 * q_wide], h), h, grad_key)
-                d_key[here, :] += grad
-                far = dot((phi * keep).astype(jnp.bfloat16), table_back)
-                d_heads[here, values_of(h)] = (d_values[here, head_at(h)] + far).astype(
-                    jnp.bfloat16
-                )
-
-            d_heads[here, 0:q_wide] = d_query[here, :].astype(jnp.bfloat16)
-            d_heads[here, q_wide : 2 * q_wide] = d_key[here, :].astype(jnp.bfloat16)
+                grad = dot(g[h, here, :], table, COLS)
+                grad = grad - column(delta[here, :], h) * dens[0, pl.ds(h, 1), :]
+                return grad * plus[2, 0:1, :] * carried
+
+            _, grad = through(of_head(heads[here, 0:q_wide], h), h, grad_phi)
+            d_query[here, :] += grad
+
+        each_tile(through_in)
+        turn(1)
+
+        def grad_out(columns):
+            return dot(dm[:, columns], mixed[...], BOTH)
+
+        staged(tile_sem, tile_o, parts[3], grad_out)
+        begin(s_out)
+        turn(2)
         pump(1)
-
         feed_sum.arrive()
+        for j in range(Spread.pieces):
+            mid_rows(j).wait()
+
+            @pl.loop(0, act_spread.tall // 32)
+            def _(r):
+                start = pl.multiple_of(j * act_spread.tall + r * 32, 32)
+                x = mid_part[j % 2, pl.ds(pl.multiple_of(r * 32, 32), 32), :]
+                x = x + feed_sum.rows(start, 32)
+                feed_sum.from_far[pl.ds(start, 32), :] = x.astype(bf)
+
+            if j + 2 < Spread.pieces:
+                mid_rows(j + 2).start()
+            act_spread.send(j)
+        act_spread.keep().start()
         feed_sum.drain()
-        for start in range(0, team.quarter, 32):
-            feed_sum.from_far[start : start + 32, :] = feed_sum.rows(start, 32).astype(bf)
+        pump(2)
+        for p in range(3, turns):
+            turn(p)
+
+        dens[1] = jnp.zeros_like(dens[1])
+        dens[1, 0:128, 0:tall] = back[heads_here].astype(jnp.float32).T
+
+        def through_out(h, here, starts):
+            keep = jnp.where(starts == last, 1.0, 0.0)
+            table = jnp.concatenate([back[h], filler], axis=0)
+
+            def grad_phi():
+                grad = dot(heads[here, values_of(h)], table, COLS)
+                return (grad + dens[1, pl.ds(h, 1), :]) * keep
+
+            phi, grad = through(of_head(heads[here, q_wide : 2 * q_wide], h), h, grad_phi)
+            d_key[here, :] += grad
+            far = dot((phi * keep).astype(jnp.bfloat16), table)
+            d_heads[here, values_of(h)] = (d_values[here, head_at(h)] + far).astype(jnp.bfloat16)
+
+        each_tile(through_out)
+        d_heads[:, 0:q_wide] = d_query[...].astype(jnp.bfloat16)
+        d_heads[:, q_wide : 2 * q_wide] = d_key[...].astype(jnp.bfloat16)
+        pump(1)
         for j in range(Sum.pieces):
             columns = slice(j * piece, (j + 1) * piece)
+            qkv_rows(j).wait()
 
             @pl.loop(0, rows // 256)
             def _(r):
                 here = pl.ds(pl.multiple_of(r * 256, 256), 256)
-                grad = dot(d_heads[here, :], w_qkv[columns, :], COLS)
+                grad = dot(d_heads[here, :], w_qkv[j % 2], COLS)
                 part[here, columns] = grad.astype(jnp.bfloat16)
 
             first_sum.near(j).start()
+            if j + 2 < Sum.pieces:
+                qkv_rows(j + 2).start()
             if j:
                 first_sum.fold(j - 1)
         first_sum.fold(Sum.pieces - 1)
 
-        down = width // n
-
-        def grad_out(s, to):
-            columns = dm[:, s * down : (s + 1) * down]
-            to[...] = dot(columns, mixed[...], BOTH).astype(jnp.bfloat16)
-
-        staged(n, tile_sem, tile_o, parts[3], grad_out, lambda s: None)
-        begin(s_out)
         pump(1)
         get_one.wait()
 
-        def grad_qkv(s, to):
-            columns = arena[:, s * down : (s + 1) * down]
-            to[...] = dot(columns, d_heads[...], BOTH).astype(jnp.bfloat16)
-
-        staged(n, tile_sem, tile_q, parts[4], grad_qkv, lambda s: None)
+        def grad_qkv(columns):
+            return dot(arena[:, columns], d_heads[...], BOTH)
+
+        staged(tile_sem, tile_q, parts[4], grad_qkv)
         begin(s_qkv)
+        s_down.final()
+        pump(2)
+        for j in range(Spread.pieces):
+            act_spread.pass_on(j)
         to_pair.wait_send()
         pl.when(at.has_left)(lambda: to_left.wait_send())
 
@@ -1505,50 +1585,43 @@
         pltpu.VMEM((rows, heads_h.shape[1]), bf),
         pltpu.VMEM((rows, values_wide), bf),
         pltpu.VMEM(out_h.shape, bf),
-        pltpu.VMEM(qkv_h.shape, bf),
-        pltpu.VMEM((heads_here, rows, 128), f32),
+        pltpu.VMEM((2, piece, qkv_h.shape[1]), bf),
+        pltpu.VMEM((rows, 128), f32),
         pltpu.VMEM((heads_here, rows, 128), bf),
         pltpu.VMEM((heads_here, 8, rows), f32),
         pltpu.VMEM((rows, q_wide), f32),
         pltpu.VMEM((rows, q_wide), f32),
         pltpu.VMEM((2, maps.shape[2], maps.shape[2]), f32),
-        pltpu.VMEM((2, width // n, values_wide), bf),
-        pltpu.VMEM((2, width // n, heads_h.shape[1]), bf),
+        pltpu.VMEM((2, 256, values_wide), bf),
+        pltpu.VMEM((2, 256, heads_h.shape[1]), bf),
         pltpu.SemaphoreType.DMA((2,)),
         pltpu.VMEM((rows, values_wide), f32),
+        pltpu.VMEM((2, act_spread.tall, width), f32),
+        pltpu.SemaphoreType.DMA((2,)),
+        pltpu.SemaphoreType.DMA((2,)),
     )
 
     quarter = pl.ds(pl.multiple_of(team.quarter_at, team.quarter), team.quarter)
-    stream_q = arena.at[0 : team.quarter]
-    get_stream = load(stream_h.at[quarter], stream_q)
-    get_stream.wait()
+    load(stream_h.at[quarter], arena.at[0 : team.quarter]).wait()
     first_sum.arrive()
-    for j in range(Spread.pieces):
-        for k in range(ig_spread.tall // 32):
-            down_at = j * ig_spread.tall + k * 32
-            here = slice(down_at, down_at + 32)
-            x = arena[here, :].astype(f32)
-            grad = norm_back(x, first_sum.rows(down_at, 32), gain.at[0], 0)
-            to = slice(ig_rows + down_at, ig_rows + down_at + 32)
-            arena[to, :] = (d_mid[here, :] + grad).astype(bf)
-        ig_spread.send(j)
-    ig_spread.keep().start()
+    @pl.loop(0, team.quarter // 32)
+    def _(r):
+        start = pl.multiple_of(r * 32, 32)
+        here = pl.ds(start, 32)
+        x = arena[here, :].astype(f32)
+        grad = norm_back(x, first_sum.rows(start, 32), gain.at[0], 0)
+        arena[pl.ds(ig_rows + start, 32), :] = (d_mid[here, :] + grad).astype(bf)
+
+    pump(1)
     gain_to_near = remote(gain_sum, gain_near, gain_send.at[0], gain_recv.at[0], team.near)
     gain_to_near.start()
-    load(mid_h, d_mid).wait()
-    for j in range(Spread.pieces):
-        for k in range(act_spread.tall // 32):
-            down_at = j * act_spread.tall + k * 32
-            here = slice(down_at, down_at + 32)
-            to = slice(act_rows + down_at, act_rows + down_at + 32)
-            arena[to, :] = (d_mid[here, :] + feed_sum.from_far[here, :].astype(f32)).astype(bf)
-        act_spread.send(j)
-    act_spread.keep().start()
     gain_to_near.wait()
     gain_sum[...] += gain_near[...]
     gain_to_far = remote(gain_sum, gain_far, gain_send.at[1], gain_recv.at[1], team.far)
     gain_to_far.start()
-    pump(1)
+    for j in range(Spread.pieces):
+        ig_spread.send(j)
+    ig_spread.keep().start()
     gain_to_far.wait()
     gain_near[...] = gain_sum[...] + gain_far[...]
     deep = width // n
@@ -1557,13 +1630,13 @@
     load(gain_parts, parts[5]).wait()
     begin(s_gains)
     for j in range(Spread.pieces):
-        pump(1)
+        pump(2)
+        if j < 2:
+            groups[1 + j].final()
         ig_spread.pass_on(j)
-    for j in range(Spread.pieces):
-        pump(1)
-        act_spread.pass_on(j)
     pump.rest()
-    s_gains.final()
+    for group in groups[3:]:
+        group.final()
     for spread_of in (ig_spread, act_spread):
         spread_of.arrive()
         spread_of.drain()
@@ -1592,7 +1665,8 @@
         ((16, deep), f32),
     ]
     results = [shape((rows, width), bf)] * 2 + [shape(*kind) for kind in kinds]
-    work = [shape((n,) + size, kind) for size, kind in kinds[1:]]
+    work = [shape((width, size[1]), kind) for size, kind in kinds[1:-1]]
+    work += [shape((n,) + kinds[-1][0], f32)]
     work += sum((Scatter.landing(n, *kind) for kind in kinds), [])
     state = (heads_here + 1, tall, 128)
     scratch = [
@@ -1628,6 +1702,101 @@
     return result[: len(results)]
 
 
+def finish_kernel(q_wide, *refs):
+    act_h, ig_h, down_h, gate_h, up_h, out_h, qkv_h, *refs = refs
+    act_o, ig_o, query_o, key_o, value_o, out_o, gate_o, up_o, down_o, *refs = refs
+    act, ig, down, gate, up, out, qkv, *refs = refs
+    ig_f, down_f, gate_f, up_f, out_f, query_f, key_f, value_f, get_sem, put_sem = refs
+    parts = 8
+    rows = ig.shape[0] // parts
+
+    def get_rows(j):
+        here = pl.ds(j * rows, rows)
+        return fetch(ig_h.at[here], ig.at[here], get_sem.at[j])
+
+    def put_rows(j):
+        here = pl.ds(j * rows, rows)
+        return fetch(ig_f.at[here], ig_o.at[here], put_sem.at[j])
+
+    get_act, put_act = fetch(act_h, act, get_sem.at[parts]), fetch(act, act_o, get_sem.at[parts])
+    gets = [
+        fetch(src, dst, get_sem.at[parts + 1 + k])
+        for k, (src, dst) in enumerate(
+            ((down_h, down), (gate_h, gate), (up_h, up), (out_h, out), (qkv_h, qkv))
+        )
+    ]
+    for j in range(parts):
+        get_rows(j).start()
+    for get in gets:
+        get.start()
+    get_act.start()
+    for j in range(parts):
+        get_rows(j).wait()
+
+        @pl.loop(0, rows // 32)
+        def _(r):
+            here = pl.ds(pl.multiple_of(j * rows + r * 32, 32), 32)
+            ig_f[here, :] = ig[here, :].astype(jnp.float32)
+
+        put_rows(j).start()
+    get_act.wait()
+    put_act.start()
+    puts = []
+
+    def put(src, dst):
+        puts.append(fetch(src, dst, put_sem.at[parts + len(puts)]))
+        puts[-1].start()
+
+    for get, src, mid, dst in zip(
+        gets, (down, gate, up, out), (down_f, gate_f, up_f, out_f), (down_o, gate_o, up_o, out_o)
+    ):
+        get.wait()
+        mid[...] = src[...].astype(jnp.float32).T
+        put(mid, dst)
+    gets[4].wait()
+    query_f[...] = qkv[:, 0:q_wide].astype(jnp.float32).T
+    key_f[...] = qkv[:, q_wide : 2 * q_wide].astype(jnp.float32).T
+    value_f[...] = qkv[:, 2 * q_wide :].astype(jnp.float32)
+    put(query_f, query_o)
+    put(key_f, key_o)
+    put(value_f, value_o)
+    for j in range(parts):
+        put_rows(j).wait()
+    for copy in puts:
+        copy.wait()
+    put_act.wait()
+
+
+def finish(q_wide, act, ig, down, gate, up, out, qkv):
+    f32 = jnp.float32
+    deep, hidden = gate.shape
+    values = out.shape[1]
+    shapes = [
+        ig.shape,
+        (q_wide, deep),
+        (q_wide, deep),
+        (deep, values),
+        (values, deep),
+        (hidden, deep),
+        (hidden, deep),
+        (hidden, deep),
+    ]
+    anywhere = pl.BlockSpec(memory_space=pl.ANY)
+    given = (act, ig, down, gate, up, out, qkv)
+    order = (0, 7, 5, 6, 4, 1, 2, 3)
+    return pl.pallas_call(
+        functools.partial(finish_kernel, q_wide),
+        out_shape=[jax.ShapeDtypeStruct(act.shape, act.dtype)]
+        + [jax.ShapeDtypeStruct(a, f32) for a in shapes],
+        in_specs=[anywhere] * len(given),
+        out_specs=[anywhere] * 9,
+        scratch_shapes=[pltpu.VMEM(a.shape, a.dtype) for a in given]
+        + [pltpu.VMEM(shapes[k], f32) for k in order]
+        + [pltpu.SemaphoreType.DMA((16,)), pltpu.SemaphoreType.DMA((16,))],
+        compiler_params=pltpu.CompilerParams(vmem_limit_bytes=56 * MIB),
+    )(*given)
+
+
 def on_device(
     stream_in,
     doc_lengths,
@@ -1644,29 +1813,26 @@
 ):
     n = lax.axis_size("seq")
     f32 = jnp.float32
-    q_wide, k_wide = w_query.shape[1], w_key.shape[1]
-    qkv_own = jnp.concatenate([w_query, w_key, w_value], axis=1)
+    q_wide = w_query.shape[1]
     gains_own = jnp.concatenate([first_gain, second_gain]).astype(f32)
     gains_own = jnp.broadcast_to(gains_own[None], (16, gains_own.shape[0]))
     maps = feature_maps(q_wide)
-    shards = (gains_own, qkv_own, w_out.T, w_gate, w_up, w_down.T)
+    shards = (gains_own, w_query.T, w_key.T, w_value, w_out, w_gate.T, w_up.T, w_down)
     wholes, kept = forward(n, doc_lengths, stream_in, cotangent, maps, shards)
-    activations, input_grad, g_down, g_gate, g_up, g_out, g_qkv, g_gains = backward(
-        n, doc_lengths, maps, stream_in, cotangent, wholes, kept
-    )
-    g_qkv = g_qkv.astype(f32)
+    *results, g_gains = backward(n, doc_lengths, maps, stream_in, cotangent, wholes, kept)
+    activations, input_grad, query, key, value, out, gate, up, down = finish(q_wide, *results)
     return (
         activations,
-        input_grad.astype(f32),
+        input_grad,
         jnp.sum(g_gains[:8], axis=0),
-        g_qkv[:, :q_wide],
-        g_qkv[:, q_wide : q_wide + k_wide],
-        g_qkv[:, q_wide + k_wide :],
-        g_out.astype(f32).T,
+        query.T,
+        key.T,
+        value,
+        out,
         jnp.sum(g_gains[8:], axis=0),
-        g_gate.astype(f32),
-        g_up.astype(f32),
-        g_down.astype(f32).T,
+        gate.T,
+        up.T,
+        down,
     )
 
 

time: 646 us -> 530 us (0.82)
  Pallas kernels: 607 us -> 518 us
  local copies, waits for them, and re-layouts: 20.2 us -> 0.62 us
  other arithmetic: 11.9 us -> 1.97 us
    pallas_call x1, Pallas kernels: 361 us -> 261 us  [backward(): pl.pallas_call(functools.partial(backward_kernel, n), out_shape=results +...]
    unnamed x25 -> x0, local copies, waits for them, and re-layouts: 16.7 us -> none
    pallas_call x0 -> x1, Pallas kernels: none -> 11.1 us  [finish(): pl.pallas_call(functools.partial(finish_kernel, q_wide), out_shape=[jax.S...]
    convert_element_type x1 -> x0, other arithmetic: 6.8 us -> none  [on_device(): input_grad.astype(f32)]
where the time goes in v3:
time: 530 us; the launch traced here: 522 us
  Pallas kernels  518 us (98%)
    pallas_call x1, Pallas kernels, backward(): pl.pallas_call(functools.partial(backward_kernel, n), out_shape=results +...  261 us
    pallas_call x1, Pallas kernels, forward(): pl.pallas_call(functools.partial(forward_kernel, n, None), out_shape=whol...  246 us
    pallas_call x1, Pallas kernels, finish(): pl.pallas_call(functools.partial(finish_kernel, q_wide), out_shape=[jax.S...  11.1 us

profile of v3, /device:TPU:0, one launch (start us, length us, event | category | flops | bytes accessed | tf_op | source)
XLA Modules:
  0.0 522.0 jit_solution(490222830478209048)
XLA Ops:
  0.6 0.7 maximum_convert_fusion
  1.3 0.6 broadcast_in_dim.2.refs_7_
  1.9 245.8 %shard_map.239 = (f32[8,16,512]{2,1,0:T(8,128)}, bf16[2048,640]{1,0:T(8,128)(2,1)}, bf16[2048,512]{1,0:T(8,128)(2,1)}, bf16[2048,1376]{1,0:T(8,128)(2,1)}, bf16[...) custom-call(s32[4]{0:T(128)} %refs_0_.3, ...), custom_call_target="tpu_custom_call" | custom-call | tf_op jit(solution)/shard_map/pallas_call | solution.py:1060
  247.7 261.4 %shard_map.240 = (bf16[1024,2048]{1,0:T(8,128)(2,1)}, bf16[1024,2048]{1,0:T(8,128)(2,1)}, bf16[256,1376]{1,0:T(8,128)(2,1)}, bf16[256,1376]{1,0:T(8,128)(2,1)}, ...) custom-call(s32[4]{0:T(128)} %refs_0_.3, ...), custom_call_target="tpu_custom_call" | custom-call | tf_op jit(solution)/shard_map/pallas_call | solution.py:1692
  509.2 1.3 slice_reduce_fusion
  510.4 11.1 %shard_map.241 = (bf16[1024,2048]{1,0:T(8,128)(2,1)}, f32[1024,2048]{1,0:T(8,128)}, f32[64,256]{1,0:T(8,128)}, f32[64,256]{1,0:T(8,128)}, f32[256,512]{1,0:T(8,1...) custom-call(bf16[1024,2048]{1,0:T(8,128)(2,1)} %get-tuple-element.62.refs_0_, ...), custom_call_target="tpu_custom_call" | custom-call | tf_op jit(solution)/shard_map/pallas_call | solution.py:1787

commit v4 on v3

--- a/solution.py
+++ b/solution.py
@@ -12,6 +12,7 @@
 EPSILON = 1e-06
 MESH = pl.DeviceIdType.MESH
 MIB = 2**20
+GATHER_CUT, SCATTER_CUT = 4, 4
 
 
 def remote(src, dst, send, recv, device):
@@ -57,8 +58,9 @@
 
 
 class Gather:
-    def __init__(self, at, own, held, sems):
+    def __init__(self, at, own, held, sems, balanced):
         self.at, self.own_ref, self.held = at, own, held
+        self.balanced = at.balanced and balanced
         self.send, self.recv, self.half_recv, self.local = sems
 
     @staticmethod
@@ -88,8 +90,9 @@
         )
 
     def half(self, slot, way, which):
-        at, rows = self.at, self.own_ref.shape[0] // 2
-        part = self.slot(slot, which * rows, rows)
+        at, rows = self.at, self.own_ref.shape[0]
+        cut = rows * GATHER_CUT // 8
+        part = self.slot(slot, which * cut, (cut, rows - cut)[which])
         return remote(
             part,
             part,
@@ -110,7 +113,7 @@
 
     def to_pair(self, slot, act):
         at = self.at
-        if not at.balanced:
+        if not self.balanced:
             act(self.copy(slot, 2))
             return
         partner = slot // 2 == at.partner
@@ -140,7 +143,7 @@
 
     def extra(self):
         at = self.at
-        if at.balanced:
+        if self.balanced:
             slot = at.o * 2 + 1 - at.i
             pl.when(at.end | at.next)(lambda: self.copy(slot, 2).wait_recv())
             self.extra_copies(lambda c: c.start())
@@ -150,7 +153,7 @@
         self.local_copy().wait()
         for layer in range(at.m):
             slot = layer * 2 + 1 - at.i
-            if not at.balanced:
+            if not self.balanced:
                 self.copy(slot, 2).wait_recv()
                 continue
             met = (at.o == layer) & (at.end | at.next)
@@ -178,22 +181,8 @@
                     pl.when(on)(lambda: self.copy(slot, way).wait_send())
                     self.to_pair(slot, lambda c: c.wait_send())
 
-        if at.balanced:
+        if self.balanced:
             self.extra_copies(lambda c: c.wait_send())
-
-
-def gather_events(groups):
-    m = groups[0].at.m
-    events = [groups[0].own]
-    for g, group in enumerate(groups):
-        for k in range(1, m):
-            if k == max(1, m - 1) and g + 1 < len(groups):
-                events.append(groups[g + 1].own)
-            events.append(functools.partial(group.step, k))
-            if k == 1 and g:
-                events.append(groups[g - 1].extra)
-    events.append(groups[-1].extra)
-    return events
 
 
 def add_rows(total, part, start, rows):
@@ -207,8 +196,9 @@
 
 
 class Scatter:
-    def __init__(self, at, parts, out, landing, bufs, sems):
+    def __init__(self, at, parts, out, landing, bufs, sems, balanced):
         self.at, self.parts, self.out = at, parts, out
+        self.balanced = at.balanced and balanced
         self.from_pair, self.from_line, self.shifted_in = landing
         self.mine, self.aside, self.stage = bufs
         (
@@ -221,6 +211,7 @@
             self.local,
         ) = sems
         self.rows = self.mine.shape[1]
+        self.cut = self.rows * SCATTER_CUT // 8
 
     @staticmethod
     def landing(n, shape, dtype):
@@ -276,8 +267,8 @@
         )
 
     def half_to_pair(self, layer, which, src):
-        half = self.rows // 2
-        part = pl.ds(which * half, half)
+        cut = self.cut
+        part = pl.ds(which * cut, (cut, self.rows - cut)[which])
         return remote(
             src.at[part],
             self.from_pair.at[layer, part],
@@ -316,10 +307,11 @@
         ).wait_recv()
 
     def shifted(self, way, which=None):
-        at, half = self.at, self.rows // 2
+        at, cut = self.at, self.cut
         src, dst = self.slot(at.partner * 2 + 1 - at.i), self.shifted_in.at[0]
         if which is not None:
-            src, dst = src.at[pl.ds(half, half)], dst.at[pl.ds(half, half)]
+            part = pl.ds(cut, self.rows - cut)
+            src, dst = src.at[part], dst.at[part]
         return remote(
             src, dst, self.extra_send.at[0], self.extra_recv.at[0], (at.right, at.left)[way]
         )
@@ -333,7 +325,7 @@
     def pair_copies(self, act):
         at = self.at
         for layer, there in self.far_first():
-            if not at.balanced:
+            if not self.balanced:
                 pl.when(there)(lambda: act(self.to_pair(layer)))
                 continue
             partner = layer == at.partner
@@ -343,7 +335,7 @@
             pl.when(there & partner & at.end)(
                 lambda: act(self.half_to_pair(layer, 0, self.slot(layer * 2 + 1 - at.i)))
             )
-        if not at.balanced:
+        if not self.balanced:
             act(self.to_pair(at.o))
             return
         pl.when(jnp.logical_not(at.end | at.next))(lambda: act(self.to_pair(at.o)))
@@ -353,7 +345,7 @@
 
     def shift_copies(self, act):
         at = self.at
-        if at.balanced:
+        if self.balanced:
             pl.when(at.o == 0)(lambda: act(self.shifted(0, 1)))
             pl.when(at.o == at.m - 1)(lambda: act(self.shifted(1, 1)))
             pl.when(at.o == 1)(lambda: act(self.shifted(1)))
@@ -365,15 +357,16 @@
         self.pair_copies(lambda c: c.start())
         for layer in range(at.m):
             self.load(layer).start()
-        if at.balanced:
+        if self.balanced:
             self.load_aside().start()
 
     def extra(self):
         at = self.at
-        if not at.balanced:
+        if not self.balanced:
             return
         self.load_aside().wait()
-        half, landed = self.rows // 2, self.shifted_in.at[0]
+        cut, landed = self.cut, self.shifted_in.at[0]
+        left = self.rows - cut
 
         @pl.when(at.end)
         def _():
@@ -386,14 +379,14 @@
         @pl.when(at.next)
         def _():
             self.shifted(0, 1).wait_recv()
-            self.to_stage(landed, 0, half, half).start()
-            self.to_stage(landed, 0, half, half).wait()
-            add_rows(self.aside.at[0], self.stage.at[0], half, half)
+            self.to_stage(landed, 0, cut, left).start()
+            self.to_stage(landed, 0, cut, left).wait()
+            add_rows(self.aside.at[0], self.stage.at[0], cut, left)
             self.half_to_pair(at.o, 1, self.aside.at[0]).start()
 
     def wait_pair(self, layer):
         at = self.at
-        if not at.balanced:
+        if not self.balanced:
             self.to_pair(layer).wait_recv()
             return
         partner, own = layer == at.partner, layer == at.o
@@ -413,10 +406,10 @@
 
             @pl.when(there)
             def _(layer=layer, behind=behind, way=way):
-                mine, paired, half = self.mine.at[layer], self.from_pair.at[layer], self.rows // 2
+                mine, paired, half = self.mine.at[layer], self.from_pair.at[layer], self.cut
                 self.load(layer).wait()
                 self.wait_pair(layer)
-                partner = (layer == at.partner) & at.balanced
+                partner = (layer == at.partner) & self.balanced
                 whole = jnp.logical_not(partner & (at.end | at.next))
                 halved = partner & at.end
                 pl.when(whole)(lambda: self.to_stage(paired, 0).start())
@@ -479,7 +472,7 @@
     def drain(self):
         at = self.at
         self.pair_copies(lambda c: c.wait_send())
-        if at.balanced:
+        if self.balanced:
             pl.when(at.end)(lambda: self.sum_to_pair().wait_send())
             pl.when(at.next)(lambda: self.half_to_pair(at.o, 1, self.aside.at[0]).wait_send())
         self.shift_copies(lambda c: c.wait_send())
@@ -742,7 +735,8 @@
     shards = (gains_own, qkv_own, out_own, gate_own, up_own, down_own)
     wholes = (gains_h, qkv_h, out_h, gate_h, up_h, down_h)
     groups = [
-        Gather(at, shards[g], wholes[g], sems[4 * g : 4 * g + 4]) for g in range(len(shards))
+        Gather(at, shards[g], wholes[g], sems[4 * g : 4 * g + 4], g > 0)
+        for g in range(len(shards))
     ]
     g_gains, g_qkv, g_out, g_gate, g_up, g_down = groups
     cell = iter(range(local.shape[0]))
@@ -767,14 +761,45 @@
     ]
     get_stream = load(stream_h, stream)
     at.greet((team.near, team.far))
-    pump = Pump(gather_events(groups))
-    pump(1)
+    pump = Pump([])
+
+    def queue(group, *steps):
+        for k in steps:
+            pump.events.append(functools.partial(group.step, k) if isinstance(k, int) else k)
+
+    last = at.m - 1
+    def values_here():
+        pass
+
+    queue(g_gains, 1)
+    for k in range(2, last + 1):
+        queue(g_gains, k)
+        queue(g_qkv, k - 1)
+        if k == 2:
+            queue(g_qkv, g_qkv.extra)
+    queue(g_gains, g_gains.extra, g_out.own)
+    queue(g_qkv, last, values_here)
+    queue(g_out, 1, *range(2, last), g_out.extra, last)
+
+    def feed_forward_here():
+        pass
+
+    queue(g_gate, 1, g_gate.extra)
+    for k in range(2, last + 1):
+        queue(g_gate, k)
+        queue(g_up, k - 1)
+        if k == 2:
+            queue(g_up, g_up.extra)
+    queue(g_down, g_down.own)
+    queue(g_up, last, feed_forward_here)
+    queue(g_down, 1, g_down.extra, *range(2, last + 1))
+    g_gains.own()
     for copy in raw[:3]:
         copy.wait()
     qkv_own[:, 0:q_wide] = query_own[...].T
     qkv_own[:, q_wide : 2 * q_wide] = key_own[...].T
     qkv_own[:, 2 * q_wide :] = value_own[...]
-    pump.until(g_qkv.own)
+    g_qkv.own()
     for copy, turned, own in zip(
         raw[3:], (out_raw, gate_raw, up_raw, down_raw), (out_own, gate_own, up_own, down_own)
     ):
@@ -795,7 +820,9 @@
         h_one[here, :] = (x * scale * gain[0, 0:1, :]).astype(jnp.bfloat16)
 
     save(h_one, h_one_h)
-    pump.until(g_qkv.extra)
+    pump.until(values_here)
+    pump(1)
+    g_gate.own()
     g_qkv.arrive()
     load(qkv_h, w_qkv).wait()
 
@@ -847,7 +874,7 @@
             values = with_ones(heads[0:upto, values_of(h)])
             numer[h, j * tile : upto, :] = dot(weights.astype(jnp.bfloat16), values)
 
-    pump(1)
+    pump(2)
 
     def closed(s):
         return jnp.where(row_start(lengths, (s + 1) * rows - 1) >= s * rows, 0.0, 1.0)
@@ -868,8 +895,9 @@
         t_next[h] = (t_two + on_two * middle).astype(jnp.bfloat16)
         state[h] = jnp.where(at.i == 0, come, middle).astype(jnp.bfloat16)
     pl.when(at.has_right)(lambda: to_right.start())
+    g_up.own()
     save(state, state_h)
-    pump(1)
+    pump(2)
 
     rden[...] = jnp.zeros_like(rden)
     @pl.loop(0, heads_here)
@@ -918,7 +946,6 @@
             part_sum.fold(j - 1)
             pump(1)
     part_sum.fold(Sum.pieces - 1)
-    pump(1)
     part_sum.arrive()
     spread = Spread(team, h_two, spread_sems)
     for j in range(Spread.pieces):
@@ -932,17 +959,16 @@
         spread.send(j)
     save(mid, mid_h)
     for j in range(Spread.pieces):
-        pump(1)
+        pump((2, 1, 1, 1)[j])
         spread.pass_on(j)
     get_cot = load(cot_h, stream)
     spread.arrive()
     part_sum.drain()
     spread.drain()
     save(h_two, h_two_h)
-    pump.until(g_gate.extra)
+    pump.until(feed_forward_here)
     g_gate.arrive()
     get_gate = load(gate_h, w_ff.at[0])
-    pump.until(g_up.extra)
     g_up.arrive()
     load(up_h, w_ff.at[1]).wait()
     get_gate.wait()
@@ -1144,6 +1170,7 @@
                 landings[3 * g : 3 * g + 3],
                 (mine, aside, stages[g]),
                 own_sems,
+                g < 3,
             )
         )
     s_down, s_gate, s_up, s_out, s_qkv, s_gains = groups
@@ -1161,7 +1188,8 @@
         group.start()
         for d in range(at.m - 1, 0, -1):
             pump.events.append(functools.partial(group.step, d))
-        pump.events.append(group.extra)
+            if d == max(1, at.m - 2) and group.balanced:
+                pump.events.append(group.extra)
 
     begin(s_down)
     get_gains = load(gains_h, gains)
@@ -1260,7 +1288,7 @@
                     part_sum.fold(p - 1)
         part_sum.fold(Sum.pieces - 1)
         get_two.wait()
-        pump(1)
+        pump(2)
         tile = w_ff.at[0]
 
         def grads(which):
@@ -1291,7 +1319,6 @@
         part_sum.drain()
         pump(1)
         staged(tile_sem, tile, parts[2], grads(1))
-        pump(1)
         get_hid = load(hid_h, ff.at[0])
         get_hid.wait()
         for j in range(Sum.pieces):
@@ -1458,6 +1485,8 @@
             def _(h):
                 intra(h)
 
+            if half == 0:
+                pump(1)
         turn(0)
         pump(1)
 
@@ -1498,6 +1527,7 @@
 
         each_tile(through_in)
         turn(1)
+        pump(1)
 
         def grad_out(columns):
             return dot(dm[:, columns], mixed[...], BOTH)
@@ -1522,7 +1552,6 @@
             act_spread.send(j)
         act_spread.keep().start()
         feed_sum.drain()
-        pump(2)
         for p in range(3, turns):
             turn(p)
 
@@ -1545,7 +1574,7 @@
         each_tile(through_out)
         d_heads[:, 0:q_wide] = d_query[...].astype(jnp.bfloat16)
         d_heads[:, q_wide : 2 * q_wide] = d_key[...].astype(jnp.bfloat16)
-        pump(1)
+        pump(2)
         for j in range(Sum.pieces):
             columns = slice(j * piece, (j + 1) * piece)
             qkv_rows(j).wait()
@@ -1570,9 +1599,9 @@
             return dot(arena[:, columns], d_heads[...], BOTH)
 
         staged(tile_sem, tile_q, parts[4], grad_qkv)
+        pump(1)
         begin(s_qkv)
         s_down.final()
-        pump(2)
         for j in range(Spread.pieces):
             act_spread.pass_on(j)
         to_pair.wait_send()
@@ -1622,6 +1651,7 @@
     for j in range(Spread.pieces):
         ig_spread.send(j)
     ig_spread.keep().start()
+    pump(1)
     gain_to_far.wait()
     gain_near[...] = gain_sum[...] + gain_far[...]
     deep = width // n
@@ -1629,14 +1659,15 @@
         gain_parts[s] = gain_near[:, s * deep : (s + 1) * deep]
     load(gain_parts, parts[5]).wait()
     begin(s_gains)
-    for j in range(Spread.pieces):
-        pump(2)
-        if j < 2:
-            groups[1 + j].final()
-        ig_spread.pass_on(j)
+    pump(1)
+    s_gate.final()
+    pump(1)
+    s_up.final()
     pump.rest()
     for group in groups[3:]:
         group.final()
+    for j in range(Spread.pieces):
+        ig_spread.pass_on(j)
     for spread_of in (ig_spread, act_spread):
         spread_of.arrive()
         spread_of.drain()

time: 530 us -> 500 us (0.943)
  Pallas kernels: 518 us -> 490 us
    pallas_call x1, Pallas kernels: 261 us -> 243 us  [backward(): pl.pallas_call(functools.partial(backward_kernel, n), out_shape=results +...]
    pallas_call x1, Pallas kernels: 246 us -> 236 us  [forward(): pl.pallas_call(functools.partial(forward_kernel, n, None), out_shape=whol...]
where the time goes in v4:
time: 500 us; the launch traced here: 494 us
  Pallas kernels  490 us (98%)
    pallas_call x1, Pallas kernels, backward(): pl.pallas_call(functools.partial(backward_kernel, n), out_shape=results +...  243 us
    pallas_call x1, Pallas kernels, forward(): pl.pallas_call(functools.partial(forward_kernel, n, None), out_shape=whol...  236 us
    pallas_call x1, Pallas kernels, finish(): pl.pallas_call(functools.partial(finish_kernel, q_wide), out_shape=[jax.S...  11.1 us

profile of v4, /device:TPU:0, one launch (start us, length us, event | category | flops | bytes accessed | tf_op | source)
XLA Modules:
  0.0 493.6 jit_solution(2390766512462141843)
XLA Ops:
  0.6 0.7 maximum_convert_fusion
  1.3 0.6 broadcast_in_dim.2.refs_7_
  1.9 235.8 %shard_map.239 = (f32[8,16,512]{2,1,0:T(8,128)}, bf16[2048,640]{1,0:T(8,128)(2,1)}, bf16[2048,512]{1,0:T(8,128)(2,1)}, bf16[2048,1376]{1,0:T(8,128)(2,1)}, bf16[...) custom-call(s32[4]{0:T(128)} %refs_0_.3, ...), custom_call_target="tpu_custom_call" | custom-call | tf_op jit(solution)/shard_map/pallas_call | solution.py:1086
  237.8 243.1 %shard_map.240 = (bf16[1024,2048]{1,0:T(8,128)(2,1)}, bf16[1024,2048]{1,0:T(8,128)(2,1)}, bf16[256,1376]{1,0:T(8,128)(2,1)}, bf16[256,1376]{1,0:T(8,128)(2,1)}, ...) custom-call(s32[4]{0:T(128)} %refs_0_.3, ...), custom_call_target="tpu_custom_call" | custom-call | tf_op jit(solution)/shard_map/pallas_call | solution.py:1723
  480.9 1.3 slice_reduce_fusion
  482.2 11.1 %shard_map.241 = (bf16[1024,2048]{1,0:T(8,128)(2,1)}, f32[1024,2048]{1,0:T(8,128)}, f32[64,256]{1,0:T(8,128)}, f32[64,256]{1,0:T(8,128)}, f32[256,512]{1,0:T(8,1...) custom-call(bf16[1024,2048]{1,0:T(8,128)(2,1)} %get-tuple-element.62.refs_0_, ...), custom_call_target="tpu_custom_call" | custom-call | tf_op jit(solution)/shard_map/pallas_call | solution.py:1818

commit v5 on v4

--- a/solution.py
+++ b/solution.py
@@ -58,8 +58,8 @@
 
 
 class Gather:
-    def __init__(self, at, own, held, sems, balanced):
-        self.at, self.own_ref, self.held = at, own, held
+    def __init__(self, at, own, held, sems, balanced, part=(0, 1)):
+        self.at, self.own_ref, self.held, self.part = at, own, held, part
         self.balanced = at.balanced and balanced
         self.send, self.recv, self.half_recv, self.local = sems
 
@@ -76,7 +76,8 @@
         if self.held.ndim == 3:
             return self.held.at[slot] if rows is None else self.held.at[slot, pl.ds(start, rows)]
         tall = self.own_ref.shape[0]
-        first = pl.multiple_of(slot * tall, 16) + start
+        which, of = self.part
+        first = pl.multiple_of((slot * of + which) * tall, 16) + start
         return self.held.at[pl.ds(first, tall if rows is None else rows)]
 
     def copy(self, slot, way, own=False):
@@ -732,13 +733,21 @@
     team = Team(at, rows)
     near_sum, sems = sems[:6], sems[6:]
     spread_sems, sems = sems[:6], sems[6:]
-    shards = (gains_own, qkv_own, out_own, gate_own, up_own, down_own)
-    wholes = (gains_h, qkv_h, out_h, gate_h, up_h, down_h)
+    tall_half = down_own.shape[0] // 2
+    down_halves = [(down_own.at[pl.ds(k * tall_half, tall_half)], down_h, (k, 2)) for k in range(2)]
+    arrays = [
+        (gains_own, gains_h, (0, 1)),
+        (qkv_own, qkv_h, (0, 1)),
+        (out_own, out_h, (0, 1)),
+        (gate_own, gate_h, (0, 1)),
+        (up_own, up_h, (0, 1)),
+        *down_halves,
+    ]
     groups = [
-        Gather(at, shards[g], wholes[g], sems[4 * g : 4 * g + 4], g > 0)
-        for g in range(len(shards))
+        Gather(at, own, whole, sems[4 * g : 4 * g + 4], g > 0, part)
+        for g, (own, whole, part) in enumerate(arrays)
     ]
-    g_gains, g_qkv, g_out, g_gate, g_up, g_down = groups
+    g_gains, g_qkv, g_out, g_gate, g_up, g_down, g_rest = groups
     cell = iter(range(local.shape[0]))
     copies = []
 
@@ -790,9 +799,13 @@
         queue(g_up, k - 1)
         if k == 2:
             queue(g_up, g_up.extra)
-    queue(g_down, g_down.own)
+    queue(g_down, g_down.own, g_rest.own)
     queue(g_up, last, feed_forward_here)
-    queue(g_down, 1, g_down.extra, *range(2, last + 1))
+    for k in range(1, last + 1):
+        for group in (g_down, g_rest):
+            queue(group, k)
+            if k == 1:
+                queue(group, group.extra)
     g_gains.own()
     for copy in raw[:3]:
         copy.wait()
@@ -959,7 +972,7 @@
         spread.send(j)
     save(mid, mid_h)
     for j in range(Spread.pieces):
-        pump((2, 1, 1, 1)[j])
+        pump((3, 1, 1, 1)[j])
         spread.pass_on(j)
     get_cot = load(cot_h, stream)
     spread.arrive()
@@ -986,7 +999,7 @@
             up_v[here, :] = up.astype(jnp.bfloat16)
             hid[here, :] = hidden.astype(jnp.bfloat16)
 
-        pump(1)
+        pump(1 if stage else 3)
     save(gate_v, gate_v_h)
     save(up_v, up_v_h)
     save(hid, hid_h)
@@ -1011,6 +1024,7 @@
         to_hbm(s, s % 2).wait()
     pump.rest()
     g_down.arrive()
+    g_rest.arrive()
     for group in groups:
         group.drain()
     to_pair.wait_send()
@@ -1081,7 +1095,7 @@
         pltpu.SemaphoreType.DMA((32,)),
         pltpu.SemaphoreType.DMA((2,)),
     ]
-    scratch += Sum.scratch(rows, width) + Spread.scratch() + Gather.scratch(n) * len(wholes)
+    scratch += Sum.scratch(rows, width) + Spread.scratch() + Gather.scratch(n) * (len(wholes) + 1)
     anywhere, inside = pl.BlockSpec(memory_space=pl.ANY), pl.BlockSpec(memory_space=pltpu.VMEM)
     result = pl.pallas_call(
         functools.partial(forward_kernel, n, None),

time: 500 us -> 494 us (0.988)
  Pallas kernels: 490 us -> 485 us
    pallas_call x1, Pallas kernels: 236 us -> 231 us  [forward(): pl.pallas_call(functools.partial(forward_kernel, n, None), out_shape=whol...]
where the time goes in v5:
time: 494 us; the launch traced here: 488 us
  Pallas kernels  485 us (98%)
    pallas_call x1, Pallas kernels, backward(): pl.pallas_call(functools.partial(backward_kernel, n), out_shape=results +...  243 us
    pallas_call x1, Pallas kernels, forward(): pl.pallas_call(functools.partial(forward_kernel, n, None), out_shape=whol...  231 us
    pallas_call x1, Pallas kernels, finish(): pl.pallas_call(functools.partial(finish_kernel, q_wide), out_shape=[jax.S...  11.1 us

profile of v5, /device:TPU:0, one launch (start us, length us, event | category | flops | bytes accessed | tf_op | source)
XLA Modules:
  0.0 488.1 jit_solution(4554164102217387580)
XLA Ops:
  0.6 0.7 maximum_convert_fusion
  1.3 0.6 broadcast_in_dim.2.refs_7_
  1.9 230.5 %shard_map.239 = (f32[8,16,512]{2,1,0:T(8,128)}, bf16[2048,640]{1,0:T(8,128)(2,1)}, bf16[2048,512]{1,0:T(8,128)(2,1)}, bf16[2048,1376]{1,0:T(8,128)(2,1)}, bf16[...) custom-call(s32[4]{0:T(128)} %refs_0_.3, ...), custom_call_target="tpu_custom_call" | custom-call | tf_op jit(solution)/shard_map/pallas_call | solution.py:1100
  232.5 243.0 %shard_map.240 = (bf16[1024,2048]{1,0:T(8,128)(2,1)}, bf16[1024,2048]{1,0:T(8,128)(2,1)}, bf16[256,1376]{1,0:T(8,128)(2,1)}, bf16[256,1376]{1,0:T(8,128)(2,1)}, ...) custom-call(s32[4]{0:T(128)} %refs_0_.3, ...), custom_call_target="tpu_custom_call" | custom-call | tf_op jit(solution)/shard_map/pallas_call | solution.py:1737
  475.5 1.3 slice_reduce_fusion
  476.8 11.1 %shard_map.241 = (bf16[1024,2048]{1,0:T(8,128)(2,1)}, f32[1024,2048]{1,0:T(8,128)}, f32[64,256]{1,0:T(8,128)}, f32[64,256]{1,0:T(8,128)}, f32[256,512]{1,0:T(8,1...) custom-call(bf16[1024,2048]{1,0:T(8,128)(2,1)} %get-tuple-element.62.refs_0_, ...), custom_call_target="tpu_custom_call" | custom-call | tf_op jit(solution)/shard_map/pallas_call | solution.py:1832

commit v6 on v5

--- a/solution.py
+++ b/solution.py
@@ -1246,8 +1246,15 @@
     gain_sum[...] = jnp.zeros_like(gain_sum)
 
     def feed_forward(w_down, w_ff, ff, w_sem, tile_sem):
-        get_cot, get_down = load(cot_h, arena), load(down_h, w_down)
-        get_gate, get_up = load(gate_v_h, ff.at[0]), load(up_v_h, ff.at[1])
+        get_cot = load(cot_h, arena)
+        pieces = [(low, min(hidden, low + 512)) for low in range(0, hidden, 512)]
+        get_pieces = [
+            [
+                load(src.at[:, low:high], dst.at[:, low:high])
+                for src, dst in ((down_h, w_down), (gate_v_h, ff.at[0]), (up_v_h, ff.at[1]))
+            ]
+            for low, high in pieces
+        ]
         tall = w_ff.shape[2]
 
         def weights(j, which):
@@ -1259,12 +1266,10 @@
         for which in (0, 1):
             weights(0, which).start()
         get_cot.wait()
-        get_down.wait()
-        get_gate.wait()
-        get_up.wait()
         block = 256
-        for low in range(0, hidden, 512):
-            high = min(hidden, low + 512)
+        for (low, high), gets in zip(pieces, get_pieces):
+            for get in gets:
+                get.wait()
 
             @pl.loop(0, rows // block)
             def _(r):

time: 494 us -> 494 us (level)
  no operation moved by 1% of the time
where the time goes in v6:
time: 494 us; the launch traced here: 488 us
  Pallas kernels  485 us (98%)
    pallas_call x1, Pallas kernels, backward(): pl.pallas_call(functools.partial(backward_kernel, n), out_shape=results +...  243 us
    pallas_call x1, Pallas kernels, forward(): pl.pallas_call(functools.partial(forward_kernel, n, None), out_shape=whol...  231 us
    pallas_call x1, Pallas kernels, finish(): pl.pallas_call(functools.partial(finish_kernel, q_wide), out_shape=[jax.S...  11.1 us

profile of v6, /device:TPU:0, one launch (start us, length us, event | category | flops | bytes accessed | tf_op | source)
XLA Modules:
  0.0 488.1 jit_solution(1767323634922711721)
XLA Ops:
  0.6 0.7 maximum_convert_fusion
  1.3 0.6 broadcast_in_dim.2.refs_7_
  1.9 230.5 %shard_map.239 = (f32[8,16,512]{2,1,0:T(8,128)}, bf16[2048,640]{1,0:T(8,128)(2,1)}, bf16[2048,512]{1,0:T(8,128)(2,1)}, bf16[2048,1376]{1,0:T(8,128)(2,1)}, bf16[...) custom-call(s32[4]{0:T(128)} %refs_0_.3, ...), custom_call_target="tpu_custom_call" | custom-call | tf_op jit(solution)/shard_map/pallas_call | solution.py:1100
  232.5 243.0 %shard_map.240 = (bf16[1024,2048]{1,0:T(8,128)(2,1)}, bf16[1024,2048]{1,0:T(8,128)(2,1)}, bf16[256,1376]{1,0:T(8,128)(2,1)}, bf16[256,1376]{1,0:T(8,128)(2,1)}, ...) custom-call(s32[4]{0:T(128)} %refs_0_.3, ...), custom_call_target="tpu_custom_call" | custom-call | tf_op jit(solution)/shard_map/pallas_call | solution.py:1742
  475.5 1.3 slice_reduce_fusion
  476.8 11.1 %shard_map.241 = (bf16[1024,2048]{1,0:T(8,128)(2,1)}, f32[1024,2048]{1,0:T(8,128)}, f32[64,256]{1,0:T(8,128)}, f32[64,256]{1,0:T(8,128)}, f32[256,512]{1,0:T(8,1...) custom-call(bf16[1024,2048]{1,0:T(8,128)(2,1)} %get-tuple-element.62.refs_0_, ...), custom_call_target="tpu_custom_call" | custom-call | tf_op jit(solution)/shard_map/pallas_call | solution.py:1837
